TPU v7x, 256 devices: a whole 4x4x8 slice. The times are simulated.
256 devices in a mesh: mem: 8 (over y_lo, x), tile: 32 (over z, y_hi, core).
Axes of the slice: x: 4, y: 4 (y_hi: 2, y_lo: 2; y = y_hi * 2 + y_lo), z: 8, core: 2. Of those that a mesh axis runs over, the one named last changes fastest.
Arguments:
- prior_moisture_sample: float32 [256, 4, 131072], P('mem', None, 'tile'), may hold values from -6 to 6
- measurement_matrix: float32 [4, 64, 32], replicated, may hold values from -0.375 to 0.375
- measured_window_readings: float32 [2048, 32], P(('tile', 'mem')), may hold values from -6 to 6
- measurement_noise_spread: float32 [2048, 32], P(('tile', 'mem')), may hold values from 1 to 4
- nearby_window_indices: int32 [4096, 8], P(('tile', 'mem')), may hold values from 0 to 2047, as said below
- window_damping_weight: int32 [4096, 8], P(('tile', 'mem')), may hold values from 0 to 3
Outputs:
- analysis: float32 [256, 4, 131072], P(None, None, ('tile', 'mem'))
Inputs may be any that keep to these rules, and one draw needn't show every extreme that they name: `nearby_window_indices`: entry 0 of group g's list is the block of its own cells, g * 32 // 64; every entry is a block of the same tile of 64 consecutive blocks as entry 0 or of a tile next to it.
All inputs are finite; a program needn't handle non-finite values. Where the computation divides by a largest or mean magnitude, that divisor is 1e-20 or more.
Results may differ from a plain program's by a relative error of at most 0.00011.
Values sent between devices are 32-bit elements; how exact they have to be, the bound alone decides.
No kernel may reach another device: no remote copies, remote signals or barrier semaphores. Data moves between devices by JAX's collectives and lax.ppermute only.
A program may use at most 128 MiB of HBM per device.

v0:
```python
import jax
import jax.numpy as jnp
from jax import lax
from jax.experimental import pallas as pl
from jax.experimental.pallas import tpu as pltpu
from jax.sharding import PartitionSpec as P

F32 = jnp.float32
BF16 = jnp.bfloat16
MEM = 8
LANES = 128


def split(x):
    hi = x.astype(BF16)
    lo = (x - hi.astype(F32)).astype(BF16)
    return hi, lo


def dot(a, b):
    return jnp.dot(a, b, preferred_element_type=F32)


def dot_nt(a, b):
    return lax.dot_general(a, b, (((1,), (1,)), ((), ())), preferred_element_type=F32)


def mul3(a, b):
    (ah, al), (bh, bl) = a, b
    return dot(ah, bh) + (dot(ah, bl) + dot(al, bh))


def exchange_lanes(parts, first, second):
    out = list(parts)
    for bit, shift, odd in ((1, 32, first), (2, 64, second)):
        for low in range(4):
            if low & bit:
                continue
            a, b = out[low], out[low | bit]
            out[low] = jnp.where(odd, pltpu.roll(b, shift, 1), a)
            out[low | bit] = jnp.where(odd, b, pltpu.roll(a, LANES - shift, 1))
    return out


def lane_bits(rows):
    lane = lax.broadcasted_iota(jnp.int32, (rows, LANES), 1)
    return (lane // 32) % 2 == 1, lane // 64 == 1


def obs_kernel(where_ref, prior_ref, map_ref, extra_ref, *refs):
    pieces, obs_ref, stack = refs[:MEM], refs[MEM], refs[MEM + 1]
    members = prior_ref.shape[0]
    me = where_ref[0]
    first, second = lane_bits(members)
    for s in range(MEM):
        peer = me ^ s
        for c in range(4):
            base = pl.multiple_of(peer * 512 + c * LANES, LANES)
            layers = [prior_ref[:, l, pl.ds(base, LANES)] for l in range(4)]
            groups = exchange_lanes(layers, first, second)
            for g in range(4):
                at = c * 4 + g
                pieces[s][:, at * LANES : (at + 1) * LANES] = groups[g]
                row = pl.multiple_of((peer * 2 + at // 8) * members, members)
                stack[pl.ds(row, members), (at % 8) * LANES : (at % 8 + 1) * LANES] = groups[g]
    halves = [map_ref[l, 32 * h : 32 * h + 32, :] for h in range(2) for l in range(4)]
    tall = jnp.concatenate(halves, axis=0)
    wide = jnp.concatenate([tall] * 4, axis=1)
    big = jnp.concatenate([wide] * 4, axis=0)
    row = lax.broadcasted_iota(jnp.int32, big.shape, 0)
    lane = lax.broadcasted_iota(jnp.int32, big.shape, 1)
    weights = jnp.where(row // 256 == lane // 32, big, 0.0)
    values = mul3(split(stack[...]), split(weights))
    for q in range(16):
        obs_ref[:, q * LANES : (q + 1) * LANES] = values[q * members : (q + 1) * members]
    obs_ref[0:8, 2048:2176] = extra_ref[...]
    obs_ref[8:, 2048:2176] = jnp.zeros((members - 8, LANES), F32)


def local_obs(where, prior, measurement_matrix, extra):
    members = prior.shape[0]
    vmem = pl.BlockSpec(memory_space=pltpu.VMEM)
    return pl.pallas_call(
        obs_kernel,
        out_shape=[jax.ShapeDtypeStruct((members, 2048), F32)] * MEM
        + [jax.ShapeDtypeStruct((members, 2176), F32)],
        in_specs=[pl.BlockSpec(memory_space=pltpu.SMEM), vmem, vmem, vmem],
        out_specs=[vmem] * (MEM + 1),
        scratch_shapes=[pltpu.VMEM((512, 1024), F32)],
        compiler_params=pltpu.CompilerParams(vmem_limit_bytes=48 << 20),
        name="local_obs",
    )(where, prior, measurement_matrix, extra)


def square(p):
    h, l = p
    m = dot(h, l)
    return dot(h, h) + (m + dot(l, h))


def analysis_kernel(*refs):
    where_ref, column_ref, weight_ref = refs[:3]
    pieces = refs[3 : 3 + MEM]
    obs = refs[3 + MEM : 3 + MEM + 9]
    out_ref = refs[3 + MEM + 9]
    raw, table, field, sems = refs[3 + MEM + 10 :]
    me = where_ref[0]
    own, g1, g3, g2o, g2h, sib, sib1, sib3, sib2 = obs
    copies = []

    def place(source, row, slot, peer):
        copies.append(
            pltpu.make_async_copy(
                source.at[pl.ds(row, 32), :],
                raw.at[slot, pl.ds(pl.multiple_of(peer * 32, 32), 32), :],
                sems.at[len(copies)],
            )
        )

    for source, x in ((own, 0), (g1, 1), (g3, 3)):
        for half in range(2):
            for y in range(2):
                place(source, half * 64 + y * 32, 2 * half, me ^ x ^ (4 * y))
    for source, slot in ((g2o, 0), (g2h, 2)):
        for y in range(2):
            place(source, y * 32, slot, me ^ 2 ^ (4 * y))
    for source, x in ((sib, 0), (sib1, 1), (sib3, 3), (sib2, 2)):
        for y in range(2):
            place(source, y * 32, 1, me ^ x ^ (4 * y))
    for copy in copies:
        copy.start()
    total = jnp.zeros((1, 2048), F32)
    for s in range(MEM):
        row = pl.multiple_of((me ^ s) * 32, 32)
        value = pieces[s][...]
        field[pl.ds(row, 32), :] = value
        total = total + jnp.sum(value, axis=0, keepdims=True)
    field[256:257, :] = total * (1.0 / 256.0)
    for copy in copies:
        copy.wait()
    for slot in range(3):
        extras = [raw[slot, 32 * m : 32 * m + 8, 2048:2176] for m in range(MEM)]
        reading = jnp.concatenate([e[i : i + 1] for e in extras for i in (0, 1)], axis=1)
        spread = jnp.concatenate([e[i : i + 1] for e in extras for i in (2, 3)], axis=1)
        scale = 1.0 / jnp.sqrt(spread)
        value = raw[slot, :, 0:2048]
        mean = jnp.sum(value, axis=0, keepdims=True) * (1.0 / 256.0)
        table[0:256, slot * 2048 : (slot + 1) * 2048] = (value - mean) * scale
        table[256:264, slot * 2048 : (slot + 1) * 2048] = jnp.broadcast_to(
            (reading - mean) * scale, (8, 2048)
        )

    rows = lax.broadcasted_iota(jnp.int32, (256, 256), 0)
    cols = lax.broadcasted_iota(jnp.int32, (256, 256), 1)
    diagonal = rows == cols
    block = lax.broadcasted_iota(jnp.int32, (1, LANES), 1) // 32

    def pick(g):
        halves = []
        for h in range(2):
            piece = jnp.zeros((264, LANES), F32)
            factor = jnp.zeros((1, LANES), F32)
            for i in range(4):
                place_at = column_ref[g * 8 + 4 * h + i]
                base = pl.multiple_of((place_at // 4) * LANES, LANES)
                shift = lax.rem(i - lax.rem(place_at, 4) + 4, 4) * 32
                moved = pltpu.roll(table[:, pl.ds(base, LANES)], shift, 1)
                piece = jnp.where(block == i, moved, piece)
                factor = jnp.where(block == i, weight_ref[g * 8 + 4 * h + i], factor)
            halves.append(piece * factor)
        return jnp.concatenate(halves, axis=1)

    def one(g):
        both = pick(g)
        chosen = both[0:256]
        drive = jnp.sum(chosen * both[256:257], axis=1, keepdims=True)
        h, l = split(chosen)
        gram = dot_nt(h, h) + (dot_nt(h, l) + dot_nt(l, h))
        precision = gram + jnp.where(diagonal, 255.0, 0.0)
        bound = jnp.max(jnp.sum(jnp.abs(precision), axis=0, keepdims=True), axis=1, keepdims=True)
        inverse = 1.0 / bound
        first = precision * inverse
        roots = []
        current = first
        for step in range(3):
            parts = split(current)
            second = square(parts)
            if step != 1:
                mixed = split(second - 4.5 * current)
                roots.append(
                    0.0625 * square(mixed)
                    + (0.421875 * second - 2.4375 * current + jnp.where(diagonal, 2.25, 0.0))
                )
            if step < 2:
                current = 2.25 * current - 1.5 * second + 0.25 * mul3(parts, split(second))
        root = mul3(split(roots[0]), split(roots[1]))
        inner = jnp.sum(root * drive, axis=0, keepdims=True)
        offset = jnp.sum(root * inner, axis=1, keepdims=True) * inverse
        at = pl.multiple_of(g * LANES, LANES)
        average = field[256:257, pl.ds(at, LANES)]
        anomaly = field[0:256, pl.ds(at, LANES)] - average
        base = average + jnp.sum(anomaly * offset, axis=0, keepdims=True)
        spread = mul3(split(root), split(anomaly))
        field[0:256, pl.ds(at, LANES)] = base + jnp.sqrt(255.0 * inverse) * spread

    def pair(i, carry):
        one(2 * i)
        one(2 * i + 1)
        return carry

    lax.fori_loop(0, 8, pair, 0)
    odd, high = lane_bits(256)
    for c in range(4):
        groups = [field[0:256, (4 * c + g) * LANES : (4 * c + g + 1) * LANES] for g in range(4)]
        layers = exchange_lanes(groups, odd, high)
        for l in range(4):
            out_ref[:, l, c * LANES : (c + 1) * LANES] = layers[l]


def analyse(where, columns, weights, pieces, obs):
    vmem = pl.BlockSpec(memory_space=pltpu.VMEM)
    smem = pl.BlockSpec(memory_space=pltpu.SMEM)
    anywhere = pl.BlockSpec(memory_space=pl.ANY)
    return pl.pallas_call(
        analysis_kernel,
        out_shape=jax.ShapeDtypeStruct((256, 4, 512), F32),
        in_specs=[smem] * 3 + [vmem] * MEM + [anywhere] * 9,
        out_specs=vmem,
        scratch_shapes=[
            pltpu.VMEM((3, 256, 2176), F32),
            pltpu.VMEM((264, 6144), F32),
            pltpu.VMEM((264, 2048), F32),
            pltpu.SemaphoreType.DMA((24,)),
        ],
        compiler_params=pltpu.CompilerParams(vmem_limit_bytes=52 << 20),
        name="analysis",
    )(where, columns, weights, *pieces, *obs)


def send(x, flip):
    return lax.ppermute(x, "mem", [(i, i ^ flip) for i in range(MEM)])


def swap_cores(x):
    return lax.ppermute(x, "tile", [(i, i ^ 1) for i in range(32)])


def local(prior, measurement_matrix, readings, noise, nearby, damping):
    me = lax.axis_index("mem").astype(jnp.int32)
    tile = lax.axis_index("tile").astype(jnp.int32)
    where = jnp.stack([me, tile])
    extra = jnp.concatenate(
        [readings.reshape(2, 128), noise.reshape(2, 128), jnp.zeros((4, 128), F32)], axis=0
    )
    *pieces, obs = local_obs(where, prior, measurement_matrix, extra)
    outer = lax.ppermute(
        obs,
        "tile",
        [(i, i + 1) for i in range(1, 31, 2)] + [(i + 1, i) for i in range(1, 31, 2)],
    )
    across = [send(obs, 4), None]
    across[1] = send(outer, 4)
    own = jnp.concatenate([obs, across[0], outer, across[1]], axis=0)
    g1 = send(own, 1)
    g3 = send(own, 3)
    g2o = send(g3[:64], 1)
    g2h = send(g1[64:], 3)
    sib = swap_cores(own[:64])
    sib1 = swap_cores(g1[:64])
    sib3 = swap_cores(g3[:64])
    sib2 = swap_cores(g2o)
    got = [pieces[0]] + [send(pieces[s], s) for s in range(1, MEM)]
    block_tile = nearby // 64
    slot = jnp.where(block_tile == tile, 0, jnp.where(block_tile // 2 == tile // 2, 1, 2))
    columns = (slot * 64 + nearby % 64).reshape(-1)
    weights = jnp.sqrt(1.0 / (1.0 + damping.astype(F32))).reshape(-1)
    return analyse(where, columns, weights, got, (own, g1, g3, g2o, g2h, sib, sib1, sib3, sib2))


def solution(mesh):
    in_specs = (
        P("mem", None, "tile"),
        P(),
        P(("tile", "mem"), None),
        P(("tile", "mem"), None),
        P(("tile", "mem"), None),
        P(("tile", "mem"), None),
    )
    out_specs = P(None, None, ("tile", "mem"))
    return jax.shard_map(local, mesh=mesh, in_specs=in_specs, out_specs=out_specs, check_vma=False)
```

profile of v0, /device:TPU:192, one launch (start us, length us, event | category | flops | bytes accessed | tf_op | source)
XLA Modules:
  0.0 163.6 jit_solution(5788549471055089327)
XLA Ops:
  2.7 1.6 copy-done
  4.3 4.0 %local_obs.1 = (f32[32,2048]{1,0:T(8,128)S(1)}, f32[32,2048]{1,0:T(8,128)S(1)}, f32[32,2048]{1,0:T(8,128)S(1)}, f32[32,2048]{1,0:T(8,128)S(1)}, f32[32,2048]{1,0...) custom-call(s32[2]{0:T(128)S(1)} %pad_add_fusion.where_ref.refs_0_, ...), custom_call_target="tpu_custom_call" | custom-call | tf_op jit(solution)/shard_map/local_obs/pallas_call | solution.py:83
  8.3 5.0 %collective-permute-start.8 = (f32[32,2176]{1,0:T(8,128)S(1)}, f32[32,2176]{1,0:T(8,128)S(1)}, u32[]{:S(2)}, u32[]{:S(2)}) collective-permute-start(f32[32,2176]{1,0:T(8,128)S(1)} %get-tuple-element.22), channel_id=1, source_target_pairs={{1,2},{3,4},{5,6},{7,8},{9,10},{11,12},{13,14},{15,16},{17,18},{19... | collective-permute-start | bytes 835592 | tf_op jit(solution)/shard_map/ppermute | solution.py:256
  14.1 4.6 %collective-permute-done.8 = f32[32,2176]{1,0:T(8,128)S(1)} collective-permute-done((f32[32,2176]{1,0:T(8,128)S(1)}, f32[32,2176]{1,0:T(8,128)S(1)}, u32[]{:S(2)}, u32[]{:S(2)}) %collective-permute-start.8) | collective-permute-done | bytes 278560 | tf_op jit(solution)/shard_map/ppermute | solution.py:256
  18.7 1.6 collective-permute-start.9
  20.3 4.8 %collective-permute-done.7 = f32[32,2176]{1,0:T(8,128)S(1)} collective-permute-done((f32[32,2176]{1,0:T(8,128)S(1)}, f32[32,2176]{1,0:T(8,128)S(1)}, u32[]{:S(2)}, u32[]{:S(2)}) %collective-permute-start.7) | collective-permute-done | bytes 278560 | tf_op jit(solution)/shard_map/ppermute | solution.py:241
  25.1 5.9 %collective-permute-done.9 = f32[32,2176]{1,0:T(8,128)S(1)} collective-permute-done((f32[32,2176]{1,0:T(8,128)S(1)}, f32[32,2176]{1,0:T(8,128)S(1)}, u32[]{:S(2)}, u32[]{:S(2)}) %collective-permute-start.9) | collective-permute-done | bytes 278560 | tf_op jit(solution)/shard_map/ppermute | solution.py:241
  31.1 2.8 %collective-permute-start.11 = (f32[128,2176]{1,0:T(8,128)S(1)}, f32[128,2176]{1,0:T(8,128)S(1)}, u32[]{:S(2)}, u32[]{:S(2)}) collective-permute-start(f32[128,2176]{1,0:T(8,128)S(1)} %constant_dynamic-update-slice_fusion.refs_11_), channel_id=1, source_target_pairs={{0,96},{32,64},{64,32},{96,0},{128,224},{160,192},{192,160},{224,1... | collective-permute-start | bytes 3342344 | tf_op jit(solution)/shard_map/ppermute | solution.py:241
  34.2 1.8 %collective-permute-start = (f32[32,2048]{1,0:T(8,128)S(1)}, f32[32,2048]{1,0:T(8,128)S(1)}, u32[]{:S(2)}, u32[]{:S(2)}) collective-permute-start(f32[32,2048]{1,0:T(8,128)S(1)} %get-tuple-element.15), channel_id=1, source_target_pairs={{0,32},{32,0},{64,96},{96,64},{128,160},{160,128},{192,224},{224,1... | collective-permute-start | bytes 786440 | tf_op jit(solution)/shard_map/ppermute | solution.py:241
  36.8 2.1 %collective-permute-start.2 = (f32[32,2048]{1,0:T(8,128)S(1)}, f32[32,2048]{1,0:T(8,128)S(1)}, u32[]{:S(2)}, u32[]{:S(2)}) collective-permute-start(f32[32,2048]{1,0:T(8,128)S(1)} %get-tuple-element.17), channel_id=1, source_target_pairs={{0,96},{32,64},{64,32},{96,0},{128,224},{160,192},{192,160},{224,1... | collective-permute-start | bytes 786440 | tf_op jit(solution)/shard_map/ppermute | solution.py:241
  39.7 19.4 %collective-permute-done.11.refs_13_ = f32[128,2176]{1,0:T(8,128)S(1)} collective-permute-done((f32[128,2176]{1,0:T(8,128)S(1)}, f32[128,2176]{1,0:T(8,128)S(1)}, u32[]{:S(2)}, u32[]{:S(2)}) %collective-permute-start.11) | collective-permute-done | bytes 1114144 | tf_op jit(solution)/shard_map/ppermute | solution.py:241
  59.1 1.3 collective-permute-start.3
  61.2 5.4 %collective-permute-done.refs_4_ = f32[32,2048]{1,0:T(8,128)S(1)} collective-permute-done((f32[32,2048]{1,0:T(8,128)S(1)}, f32[32,2048]{1,0:T(8,128)S(1)}, u32[]{:S(2)}, u32[]{:S(2)}) %collective-permute-start) | collective-permute-done | bytes 262176 | tf_op jit(solution)/shard_map/ppermute | solution.py:241
  67.4 4.7 %collective-permute-done.1.refs_5_ = f32[32,2048]{1,0:T(8,128)S(1)} collective-permute-done((f32[32,2048]{1,0:T(8,128)S(1)}, f32[32,2048]{1,0:T(8,128)S(1)}, u32[]{:S(2)}, u32[]{:S(2)}) %collective-permute-start.1) | collective-permute-done | bytes 262176 | tf_op jit(solution)/shard_map/ppermute | solution.py:241
  72.1 2.5 %collective-permute-start.5 = (f32[32,2048]{1,0:T(8,128)S(1)}, f32[32,2048]{1,0:T(8,128)S(1)}, u32[]{:S(2)}, u32[]{:S(2)}) collective-permute-start(f32[32,2048]{1,0:T(8,128)S(1)} %get-tuple-element.20), channel_id=1, source_target_pairs={{0,192},{32,224},{64,128},{96,160},{128,64},{160,96},{192,0},{224,... | collective-permute-start | bytes 786440 | tf_op jit(solution)/shard_map/ppermute | solution.py:241
  74.6 1.4 collective-permute-start.6
  76.6 1.1 fusion.5
  78.6 1.0 collective-permute-start.16
  79.5 4.7 %collective-permute-done.5.refs_9_ = f32[32,2048]{1,0:T(8,128)S(1)} collective-permute-done((f32[32,2048]{1,0:T(8,128)S(1)}, f32[32,2048]{1,0:T(8,128)S(1)}, u32[]{:S(2)}, u32[]{:S(2)}) %collective-permute-start.5) | collective-permute-done | bytes 262176 | tf_op jit(solution)/shard_map/ppermute | solution.py:241
  84.9 5.3 %collective-permute-done.6.refs_10_ = f32[32,2048]{1,0:T(8,128)S(1)} collective-permute-done((f32[32,2048]{1,0:T(8,128)S(1)}, f32[32,2048]{1,0:T(8,128)S(1)}, u32[]{:S(2)}, u32[]{:S(2)}) %collective-permute-start.6) | collective-permute-done | bytes 262176 | tf_op jit(solution)/shard_map/ppermute | solution.py:241
  90.2 2.2 %collective-permute-start.13 = (f32[64,2176]{1,0:T(8,128)}, f32[64,2176]{1,0:T(8,128)S(1)}, u32[]{:S(2)}, u32[]{:S(2)}) collective-permute-start(f32[64,2176]{1,0:T(8,128)} %get-tuple-element.24), channel_id=1, source_target_pairs={{0,96},{32,64},{64,32},{96,0},{128,224},{160,192},{192,160},{224,1... | collective-permute-start | bytes 1671176 | tf_op jit(solution)/shard_map/ppermute | solution.py:241
  92.4 3.3 %collective-permute-done.12.refs_14_ = f32[64,2176]{1,0:T(8,128)} collective-permute-done((f32[64,2176]{1,0:T(8,128)}, f32[64,2176]{1,0:T(8,128)}, u32[]{:S(2)}, u32[]{:S(2)}) %collective-permute-start.12) | collective-permute-done | bytes 557088 | tf_op jit(solution)/shard_map/ppermute | solution.py:241
  96.3 9.9 %collective-permute-done.13.refs_15_ = f32[64,2176]{1,0:T(8,128)S(1)} collective-permute-done((f32[64,2176]{1,0:T(8,128)}, f32[64,2176]{1,0:T(8,128)S(1)}, u32[]{:S(2)}, u32[]{:S(2)}) %collective-permute-start.13) | collective-permute-done | bytes 557088 | tf_op jit(solution)/shard_map/ppermute | solution.py:241
  107.2 56.2 %analysis.1 = f32[256,4,512]{2,1,0:T(4,128)} custom-call(s32[2]{0:T(128)S(1)} %pad_add_fusion.where_ref.refs_0_, s32[128]{0:T(128)S(1)} %reshape.12.refs_1_, f32[128]{0:T(128)S(1)} %reshape.13.refs_2_, f32[32,2048]{1,0:T(8,128)S(1)} %get-tuple-element.14.refs_3_, f32[32,2048]{1,0:T(8,128)S(1)} %collective-permute-done.refs_4_, ...), custom_call_target="tpu_custom_call" | custom-call | tf_op jit(solution)/shard_map/analysis/pallas_call | solution.py:224
  (52 shorter events, 10.9 us)
Async XLA Ops:
  8.3 10.4 %collective-permute-start.8 = (f32[32,2176]{1,0:T(8,128)S(1)}, f32[32,2176]{1,0:T(8,128)S(1)}, u32[]{:S(2)}, u32[]{:S(2)}) collective-permute-start(f32[32,2176]{1,0:T(8,128)S(1)} %get-tuple-element.22), channel_id=1, source_target_pairs={{1,2},{3,4},{5,6},{7,8},{9,10},{11,12},{13,14},{15,16},{17,18},{19... | collective-permute-start | bytes 835592 | tf_op jit(solution)/shard_map/ppermute | solution.py:256
  13.3 11.8 %collective-permute-start.7 = (f32[32,2176]{1,0:T(8,128)S(1)}, f32[32,2176]{1,0:T(8,128)S(1)}, u32[]{:S(2)}, u32[]{:S(2)}) collective-permute-start(f32[32,2176]{1,0:T(8,128)S(1)} %get-tuple-element.22), channel_id=1, source_target_pairs={{0,128},{32,160},{64,192},{96,224},{128,0},{160,32},{192,64},{224,... | collective-permute-start | bytes 835592 | tf_op jit(solution)/shard_map/ppermute | solution.py:241
  18.7 12.4 %collective-permute-start.9 = (f32[32,2176]{1,0:T(8,128)S(1)}, f32[32,2176]{1,0:T(8,128)S(1)}, u32[]{:S(2)}, u32[]{:S(2)}) collective-permute-start(f32[32,2176]{1,0:T(8,128)S(1)} %collective-permute-done.8), channel_id=1, source_target_pairs={{0,128},{32,160},{64,192},{96,224},{128,0},{160,32},{192,64},{224,... | collective-permute-start | bytes 835592 | tf_op jit(solution)/shard_map/ppermute | solution.py:241
  31.1 30.1 %copy-start.3 = (f32[128,2176]{1,0:T(8,128)}, f32[128,2176]{1,0:T(8,128)S(1)}, u32[]{:S(2)}) copy-start(f32[128,2176]{1,0:T(8,128)S(1)} %constant_dynamic-update-slice_fusion.refs_11_) | copy-start | bytes 3342340
  31.1 28.0 %collective-permute-start.11 = (f32[128,2176]{1,0:T(8,128)S(1)}, f32[128,2176]{1,0:T(8,128)S(1)}, u32[]{:S(2)}, u32[]{:S(2)}) collective-permute-start(f32[128,2176]{1,0:T(8,128)S(1)} %constant_dynamic-update-slice_fusion.refs_11_), channel_id=1, source_target_pairs={{0,96},{32,64},{64,32},{96,0},{128,224},{160,192},{192,160},{224,1... | collective-permute-start | bytes 3342344 | tf_op jit(solution)/shard_map/ppermute | solution.py:241
  33.9 42.0 %collective-permute-start.10 = (f32[128,2176]{1,0:T(8,128)S(1)}, f32[128,2176]{1,0:T(8,128)S(1)}, u32[]{:S(2)}, u32[]{:S(2)}) collective-permute-start(f32[128,2176]{1,0:T(8,128)S(1)} %constant_dynamic-update-slice_fusion.refs_11_), channel_id=1, source_target_pairs={{0,32},{32,0},{64,96},{96,64},{128,160},{160,128},{192,224},{224,1... | collective-permute-start | bytes 3342344 | tf_op jit(solution)/shard_map/ppermute | solution.py:241
  34.2 32.4 %collective-permute-start = (f32[32,2048]{1,0:T(8,128)S(1)}, f32[32,2048]{1,0:T(8,128)S(1)}, u32[]{:S(2)}, u32[]{:S(2)}) collective-permute-start(f32[32,2048]{1,0:T(8,128)S(1)} %get-tuple-element.15), channel_id=1, source_target_pairs={{0,32},{32,0},{64,96},{96,64},{128,160},{160,128},{192,224},{224,1... | collective-permute-start | bytes 786440 | tf_op jit(solution)/shard_map/ppermute | solution.py:241
  36.0 36.2 %collective-permute-start.1 = (f32[32,2048]{1,0:T(8,128)S(1)}, f32[32,2048]{1,0:T(8,128)S(1)}, u32[]{:S(2)}, u32[]{:S(2)}) collective-permute-start(f32[32,2048]{1,0:T(8,128)S(1)} %get-tuple-element.16), channel_id=1, source_target_pairs={{0,64},{32,96},{64,0},{96,32},{128,192},{160,224},{192,128},{224,1... | collective-permute-start | bytes 786440 | tf_op jit(solution)/shard_map/ppermute | solution.py:241
  36.8 37.8 %collective-permute-start.2 = (f32[32,2048]{1,0:T(8,128)S(1)}, f32[32,2048]{1,0:T(8,128)S(1)}, u32[]{:S(2)}, u32[]{:S(2)}) collective-permute-start(f32[32,2048]{1,0:T(8,128)S(1)} %get-tuple-element.17), channel_id=1, source_target_pairs={{0,96},{32,64},{64,32},{96,0},{128,224},{160,192},{192,160},{224,1... | collective-permute-start | bytes 786440 | tf_op jit(solution)/shard_map/ppermute | solution.py:241
  59.1 18.5 %copy-start.2 = (f32[128,2176]{1,0:T(8,128)}, f32[128,2176]{1,0:T(8,128)S(1)}, u32[]{:S(2)}) copy-start(f32[128,2176]{1,0:T(8,128)S(1)} %collective-permute-done.11.refs_13_) | copy-start | bytes 3342340
  59.1 18.5 %collective-permute-start.3 = (f32[32,2048]{1,0:T(8,128)S(1)}, f32[32,2048]{1,0:T(8,128)S(1)}, u32[]{:S(2)}, u32[]{:S(2)}) collective-permute-start(f32[32,2048]{1,0:T(8,128)S(1)} %get-tuple-element.18), channel_id=1, source_target_pairs={{0,128},{32,160},{64,192},{96,224},{128,0},{160,32},{192,64},{224,... | collective-permute-start | bytes 786440 | tf_op jit(solution)/shard_map/ppermute | solution.py:241
  66.6 12.0 %collective-permute-start.4 = (f32[32,2048]{1,0:T(8,128)S(1)}, f32[32,2048]{1,0:T(8,128)S(1)}, u32[]{:S(2)}, u32[]{:S(2)}) collective-permute-start(f32[32,2048]{1,0:T(8,128)S(1)} %get-tuple-element.19), channel_id=1, source_target_pairs={{0,160},{32,128},{64,224},{96,192},{128,32},{160,0},{192,96},{224,... | collective-permute-start | bytes 786440 | tf_op jit(solution)/shard_map/ppermute | solution.py:241
  72.1 12.1 %collective-permute-start.5 = (f32[32,2048]{1,0:T(8,128)S(1)}, f32[32,2048]{1,0:T(8,128)S(1)}, u32[]{:S(2)}, u32[]{:S(2)}) collective-permute-start(f32[32,2048]{1,0:T(8,128)S(1)} %get-tuple-element.20), channel_id=1, source_target_pairs={{0,192},{32,224},{64,128},{96,160},{128,64},{160,96},{192,0},{224,... | collective-permute-start | bytes 786440 | tf_op jit(solution)/shard_map/ppermute | solution.py:241
  74.6 21.4 %copy-start.7 = (s32[16,8]{0,1:T(8,128)S(1)}, s32[16,8]{0,1:T(8,128)}, u32[]{:S(2)}) copy-start(s32[16,8]{0,1:T(8,128)} %param.10) | copy-start | bytes 1540
  74.6 21.6 %copy-start.8 = (s32[16,8]{0,1:T(8,128)S(1)}, s32[16,8]{0,1:T(8,128)}, u32[]{:S(2)}) copy-start(s32[16,8]{0,1:T(8,128)} %param.11) | copy-start | bytes 1540
  74.6 15.6 %collective-permute-start.6 = (f32[32,2048]{1,0:T(8,128)S(1)}, f32[32,2048]{1,0:T(8,128)S(1)}, u32[]{:S(2)}, u32[]{:S(2)}) collective-permute-start(f32[32,2048]{1,0:T(8,128)S(1)} %get-tuple-element.21), channel_id=1, source_target_pairs={{0,224},{32,192},{64,160},{96,128},{128,96},{160,64},{192,32},{224... | collective-permute-start | bytes 786440 | tf_op jit(solution)/shard_map/ppermute | solution.py:241
  76.0 8.3 %copy-start.1 = (f32[128,2176]{1,0:T(8,128)}, f32[128,2176]{1,0:T(8,128)S(1)}, u32[]{:S(2)}) copy-start(f32[128,2176]{1,0:T(8,128)S(1)} %collective-permute-done.10.refs_12_) | copy-start | bytes 3342340
  76.0 19.8 %collective-permute-start.12 = (f32[64,2176]{1,0:T(8,128)}, f32[64,2176]{1,0:T(8,128)}, u32[]{:S(2)}, u32[]{:S(2)}) collective-permute-start(f32[64,2176]{1,0:T(8,128)} %slice.15), channel_id=1, source_target_pairs={{0,32},{32,0},{64,96},{96,64},{128,160},{160,128},{192,224},{224,1... | collective-permute-start | bytes 1671176 | tf_op jit(solution)/shard_map/ppermute | solution.py:241
  77.6 18.7 %collective-permute-start.14 = (f32[64,2176]{1,0:T(8,128)}, f32[64,2176]{1,0:T(8,128)}, u32[]{:S(2)}, u32[]{:S(2)}) collective-permute-start(f32[64,2176]{1,0:T(8,128)} %pad_maximum_fusion), channel_id=1, source_target_pairs={{0,1},{1,0},{2,3},{3,2},{4,5},{5,4},{6,7},{7,6},{8,9},{9,8},{10,11... | collective-permute-start | bytes 1671176 | tf_op jit(solution)/shard_map/ppermute | solution.py:245
  78.6 17.8 %collective-permute-start.16 = (f32[64,2176]{1,0:T(8,128)}, f32[64,2176]{1,0:T(8,128)}, u32[]{:S(2)}, u32[]{:S(2)}) collective-permute-start(f32[64,2176]{1,0:T(8,128)} %slice.15), channel_id=1, source_target_pairs={{0,1},{1,0},{2,3},{3,2},{4,5},{5,4},{6,7},{7,6},{8,9},{9,8},{10,11... | collective-permute-start | bytes 1671176 | tf_op jit(solution)/shard_map/ppermute | solution.py:245
  84.2 12.1 %collective-permute-start.15 = (f32[64,2176]{1,0:T(8,128)}, f32[64,2176]{1,0:T(8,128)}, u32[]{:S(2)}, u32[]{:S(2)}) collective-permute-start(f32[64,2176]{1,0:T(8,128)} %get-tuple-element.23), channel_id=1, source_target_pairs={{0,1},{1,0},{2,3},{3,2},{4,5},{5,4},{6,7},{7,6},{8,9},{9,8},{10,11... | collective-permute-start | bytes 1671176 | tf_op jit(solution)/shard_map/ppermute | solution.py:245
  90.2 16.0 %copy-start.6 = (f32[32,2048]{1,0:T(8,128)}, f32[32,2048]{1,0:T(8,128)S(1)}, u32[]{:S(2)}) copy-start(f32[32,2048]{1,0:T(8,128)S(1)} %collective-permute-done.6.refs_10_) | copy-start | bytes 786436
  90.2 16.0 %collective-permute-start.13 = (f32[64,2176]{1,0:T(8,128)}, f32[64,2176]{1,0:T(8,128)S(1)}, u32[]{:S(2)}, u32[]{:S(2)}) collective-permute-start(f32[64,2176]{1,0:T(8,128)} %get-tuple-element.24), channel_id=1, source_target_pairs={{0,96},{32,64},{64,32},{96,0},{128,224},{160,192},{192,160},{224,1... | collective-permute-start | bytes 1671176 | tf_op jit(solution)/shard_map/ppermute | solution.py:241
  95.7 10.5 %collective-permute-start.17 = (f32[64,2176]{1,0:T(8,128)}, f32[64,2176]{1,0:T(8,128)S(1)}, u32[]{:S(2)}, u32[]{:S(2)}) collective-permute-start(f32[64,2176]{1,0:T(8,128)} %collective-permute-done.12.refs_14_), channel_id=1, source_target_pairs={{0,1},{1,0},{2,3},{3,2},{4,5},{5,4},{6,7},{7,6},{8,9},{9,8},{10,11... | collective-permute-start | bytes 1671176 | tf_op jit(solution)/shard_map/ppermute | solution.py:245
  (3 other events, 3.4 us)
where the time goes:
time: 164 us
  waiting for transfers between devices  68.7 us (42%)
  Pallas kernels  60.2 us (37%)
  starting transfers between devices  25.9 us (16%)
  local copies, waits for them, and re-layouts  7.46 us (5%)
    ppermute x13, waiting for transfers between devices, send(): return lax.ppermute(x, 'mem', [(i, i ^ flip) for i in range(MEM)])  64.1 us
    pallas_call x1, Pallas kernels, analyse(): pl.pallas_call(analysis_kernel, out_shape=jax.ShapeDtypeStruct((256, 4, 5...  56.2 us
    ppermute x13, starting transfers between devices, send(): return lax.ppermute(x, 'mem', [(i, i ^ flip) for i in range(MEM)])  18.9 us
    ppermute x1, starting transfers between devices, local(): lax.ppermute(obs, 'tile', [(i, i + 1) for i in range(1, 31, 2)] + [(i + 1...  4.99 us
    ppermute x1, waiting for transfers between devices, local(): lax.ppermute(obs, 'tile', [(i, i + 1) for i in range(1, 31, 2)] + [(i + 1...  4.59 us
    pallas_call x1, Pallas kernels, local_obs(): pl.pallas_call(obs_kernel, out_shape=[jax.ShapeDtypeStruct((members, 2048...  4.02 us
    unnamed x22, local copies, waits for them, and re-layouts  3.6 us
  transfers between devices with their start and end apart: 18, of which 11 were waited for; matrix products, arithmetic and copies ran while one was open for 2% of the time, Pallas kernels for 0%

commit v1 on v0

v1 whole, which is shorter than its diff:
```python
import jax
import jax.numpy as jnp
from jax import lax
from jax.experimental import pallas as pl
from jax.experimental.pallas import tpu as pltpu
from jax.sharding import PartitionSpec as P

F32 = jnp.float32
BF16 = jnp.bfloat16
MEM = 8
LANES = 128
WIDE = 4


def split(x):
    hi = x.astype(BF16)
    lo = (x - hi.astype(F32)).astype(BF16)
    return hi, lo


def dot(a, b):
    return jnp.dot(a, b, preferred_element_type=F32)


def dot_nt(a, b):
    return lax.dot_general(a, b, (((1,), (1,)), ((), ())), preferred_element_type=F32)


def mul3(a, b):
    (ah, al), (bh, bl) = a, b
    return dot(ah, bh) + (dot(ah, bl) + dot(al, bh))


def exchange_lanes(parts, first, second):
    out = list(parts)
    for bit, shift, odd in ((1, 32, first), (2, 64, second)):
        for low in range(4):
            if low & bit:
                continue
            a, b = out[low], out[low | bit]
            out[low] = jnp.where(odd, pltpu.roll(b, shift, 1), a)
            out[low | bit] = jnp.where(odd, b, pltpu.roll(a, LANES - shift, 1))
    return out


def lane_bits(rows):
    lane = lax.broadcasted_iota(jnp.int32, (rows, LANES), 1)
    return (lane // 32) % 2 == 1, lane // 64 == 1


def obs_kernel(where_ref, prior_ref, map_ref, extra_ref, *refs):
    pieces, obs_ref, stack = refs[:MEM], refs[MEM], refs[MEM + 1]
    members = prior_ref.shape[0]
    me = where_ref[0]
    first, second = lane_bits(members)
    for s in range(MEM):
        peer = me ^ s
        for c in range(4):
            base = pl.multiple_of(peer * 512 + c * LANES, LANES)
            layers = [prior_ref[:, l, pl.ds(base, LANES)] for l in range(4)]
            groups = exchange_lanes(layers, first, second)
            for g in range(4):
                at = c * 4 + g
                pieces[s][:, at * LANES : (at + 1) * LANES] = groups[g]
                row = pl.multiple_of((peer * 2 + at // 8) * members, members)
                stack[pl.ds(row, members), (at % 8) * LANES : (at % 8 + 1) * LANES] = groups[g]
    halves = [map_ref[l, 32 * h : 32 * h + 32, :] for h in range(2) for l in range(4)]
    tall = jnp.concatenate(halves, axis=0)
    wide = jnp.concatenate([tall] * 4, axis=1)
    big = jnp.concatenate([wide] * 4, axis=0)
    row = lax.broadcasted_iota(jnp.int32, big.shape, 0)
    lane = lax.broadcasted_iota(jnp.int32, big.shape, 1)
    weights = jnp.where(row // 256 == lane // 32, big, 0.0)
    values = mul3(split(stack[...]), split(weights))
    for q in range(16):
        obs_ref[:, q * LANES : (q + 1) * LANES] = values[q * members : (q + 1) * members]
    obs_ref[0:8, 2048:2176] = extra_ref[...]
    obs_ref[8:, 2048:2176] = jnp.zeros((members - 8, LANES), F32)


def local_obs(where, prior, measurement_matrix, extra):
    members = prior.shape[0]
    vmem = pl.BlockSpec(memory_space=pltpu.VMEM)
    return pl.pallas_call(
        obs_kernel,
        out_shape=[jax.ShapeDtypeStruct((members, 2048), F32)] * MEM
        + [jax.ShapeDtypeStruct((members, 2176), F32)],
        in_specs=[pl.BlockSpec(memory_space=pltpu.SMEM), vmem, vmem, vmem],
        out_specs=[vmem] * (MEM + 1),
        scratch_shapes=[pltpu.VMEM((512, 1024), F32)],
        compiler_params=pltpu.CompilerParams(vmem_limit_bytes=48 << 20),
        name="local_obs",
    )(where, prior, measurement_matrix, extra)


def square(p):
    h, l = p
    m = dot(h, l)
    return dot(h, h) + (m + dot(l, h))


def each(function, *lists):
    return [function(*items) for items in zip(*lists)]


def mixing_kernel(*refs):
    where_ref, column_ref, weight_ref = refs[:3]
    obs = refs[3:18]
    root_ref, offset_ref, raw, table, sems = refs[18:]
    me = where_ref[0]

    @pl.when(pl.program_id(0) == 0)
    def gather():
        copies = [[], [], []]

        def place(source, row, slot, peer):
            copies[slot].append(
                pltpu.make_async_copy(
                    source.at[pl.ds(row, 32), :],
                    raw.at[slot, pl.ds(pl.multiple_of(peer * 32, 32), 32), :],
                    sems.at[slot, len(copies[slot])],
                )
            )

        for slot, (own, one, three, two_own, two_far) in zip((0, 2, 1), (obs[:5], obs[5:10], obs[10:])):
            for source, x in ((own, 0), (one, 1), (three, 3)):
                for y in range(2):
                    place(source, y * 32, slot, me ^ x ^ (4 * y))
            place(two_own, 0, slot, me ^ 2)
            place(two_far, 0, slot, me ^ 6)
        for slot in range(3):
            for copy in copies[slot]:
                copy.start()
        for slot in range(3):
            for copy in copies[slot]:
                copy.wait()
            extras = [raw[slot, 32 * m : 32 * m + 8, 2048:2176] for m in range(MEM)]
            reading = jnp.concatenate([e[i : i + 1] for e in extras for i in (0, 1)], axis=1)
            spread = jnp.concatenate([e[i : i + 1] for e in extras for i in (2, 3)], axis=1)
            scale = 1.0 / jnp.sqrt(spread)
            for c in range(16):
                lanes = slice(c * LANES, (c + 1) * LANES)
                value = raw[slot, :, lanes]
                mean = jnp.sum(value, axis=0, keepdims=True) * (1.0 / 256.0)
                table[slot * 16 + c, 0:256, :] = (value - mean) * scale[:, lanes]
                table[slot * 16 + c, 256:264, :] = jnp.broadcast_to(
                    (reading[:, lanes] - mean) * scale[:, lanes], (8, LANES)
                )
        offset_ref[...] = jnp.zeros((256, LANES), F32)

    rows = lax.broadcasted_iota(jnp.int32, (256, 256), 0)
    cols = lax.broadcasted_iota(jnp.int32, (256, 256), 1)
    diagonal = rows == cols
    block = lax.broadcasted_iota(jnp.int32, (1, LANES), 1) // 32
    lane = lax.broadcasted_iota(jnp.int32, (256, LANES), 1)

    def pick(g):
        halves = []
        for h in range(2):
            piece = jnp.zeros((264, LANES), F32)
            factor = jnp.zeros((1, LANES), F32)
            for i in range(4):
                place_at = column_ref[g * 8 + 4 * h + i]
                shift = lax.rem(i - lax.rem(place_at, 4) + 4, 4) * 32
                moved = pltpu.roll(table[place_at // 4], shift, 1)
                piece = jnp.where(block == i, moved, piece)
                factor = jnp.where(block == i, weight_ref[g * 8 + 4 * h + i], factor)
            halves.append(piece * factor)
        return jnp.concatenate(halves, axis=1)

    groups = [pl.program_id(0) * WIDE + u for u in range(WIDE)]
    picked = each(pick, groups)
    drives = each(
        lambda p: jnp.sum(p[0:256] * p[256:257], axis=1, keepdims=True), picked
    )
    parts = each(lambda p: split(p[0:256]), picked)
    grams = each(
        lambda p: dot_nt(p[0], p[0]) + (dot_nt(p[0], p[1]) + dot_nt(p[1], p[0])), parts
    )
    grams = each(lambda g: g + jnp.where(diagonal, 255.0, 0.0), grams)
    inverses = each(
        lambda g: 1.0
        / jnp.max(jnp.sum(jnp.abs(g), axis=0, keepdims=True), axis=1, keepdims=True),
        grams,
    )
    current = each(lambda g, v: g * v, grams, inverses)
    roots = []
    for step in range(3):
        parts = each(split, current)
        second = each(square, parts)
        if step < 2:
            products = each(mul3, parts, each(split, second))
        if step != 1:
            mixed = each(lambda s, c: split(s - 4.5 * c), second, current)
            roots.append(
                each(
                    lambda m, s, c: 0.0625 * square(m)
                    + (0.421875 * s - 2.4375 * c + jnp.where(diagonal, 2.25, 0.0)),
                    mixed,
                    second,
                    current,
                )
            )
        if step < 2:
            current = each(
                lambda c, s, p: 2.25 * c - 1.5 * s + 0.25 * p, current, second, products
            )
    root = each(mul3, each(split, roots[0]), each(split, roots[1]))
    inner = each(lambda r, d: jnp.sum(r * d, axis=0, keepdims=True), root, drives)
    offsets = each(
        lambda r, n, v: jnp.sum(r * n, axis=1, keepdims=True) * v, root, inner, inverses
    )
    held = offset_ref[...]
    for u, (g, r, v, o) in enumerate(zip(groups, root, inverses, offsets)):
        root_ref[u] = jnp.sqrt(255.0 * v) * r
        held = jnp.where(lane == g, o, held)
    offset_ref[...] = held


def apply_kernel(where_ref, root_ref, offset_ref, *refs):
    pieces = refs[:MEM]
    out_ref, field = refs[MEM:]
    me = where_ref[0]

    @pl.when(pl.program_id(0) == 0)
    def gather():
        for s in range(MEM):
            row = pl.multiple_of((me ^ s) * 32, 32)
            for g in range(16):
                field[g, pl.ds(row, 32), :] = pieces[s][:, g * LANES : (g + 1) * LANES]

    odd, high = lane_bits(256)
    lane = lax.broadcasted_iota(jnp.int32, (256, LANES), 1)
    groups = [pl.program_id(0) * 4 + g for g in range(4)]
    value = [field[g] for g in groups]
    centre = each(lambda x: jnp.sum(x, axis=0, keepdims=True) * (1.0 / 256.0), value)
    anomaly = each(lambda x, a: x - a, value, centre)
    offset = [
        jnp.sum(jnp.where(lane == g, offset_ref[...], 0.0), axis=1, keepdims=True) for g in groups
    ]
    base = each(
        lambda a, x, o: a + jnp.sum(x * o, axis=0, keepdims=True), centre, anomaly, offset
    )
    spread = each(mul3, [split(root_ref[u]) for u in range(4)], each(split, anomaly))
    layers = exchange_lanes(each(lambda b, x: b + x, base, spread), odd, high)
    for l in range(4):
        out_ref[:, l, :] = layers[l]


VMEM = pl.BlockSpec(memory_space=pltpu.VMEM)
SMEM = pl.BlockSpec(memory_space=pltpu.SMEM)
ANYWHERE = pl.BlockSpec(memory_space=pl.ANY)


def find_mixing(where, columns, weights, obs):
    return pl.pallas_call(
        mixing_kernel,
        out_shape=[
            jax.ShapeDtypeStruct((16, 256, 256), F32),
            jax.ShapeDtypeStruct((256, LANES), F32),
        ],
        grid=(16 // WIDE,),
        in_specs=[SMEM] * 3 + [ANYWHERE] * 15,
        out_specs=[
            pl.BlockSpec((WIDE, 256, 256), lambda i: (i, 0, 0)),
            pl.BlockSpec((256, LANES), lambda i: (0, 0)),
        ],
        scratch_shapes=[
            pltpu.VMEM((3, 256, 2176), F32),
            pltpu.VMEM((48, 264, LANES), F32),
            pltpu.SemaphoreType.DMA((3, 8)),
        ],
        compiler_params=pltpu.CompilerParams(vmem_limit_bytes=48 << 20),
        cost_estimate=pl.CostEstimate(
            flops=16 * 30 * 2 * 256**3, bytes_accessed=12 << 20, transcendentals=0
        ),
        name="mixing",
    )(where, columns, weights, *obs)


def apply_mixing(where, root, offset, pieces):
    return pl.pallas_call(
        apply_kernel,
        out_shape=jax.ShapeDtypeStruct((256, 4, 512), F32),
        grid=(4,),
        in_specs=[SMEM, pl.BlockSpec((4, 256, 256), lambda i: (i, 0, 0)), VMEM] + [VMEM] * MEM,
        out_specs=pl.BlockSpec((256, 4, LANES), lambda i: (0, 0, i)),
        scratch_shapes=[pltpu.VMEM((16, 256, LANES), F32)],
        compiler_params=pltpu.CompilerParams(vmem_limit_bytes=60 << 20),
        name="apply",
    )(where, root, offset, *pieces)


def send(x, flip):
    return lax.ppermute(x, "mem", [(i, i ^ flip) for i in range(MEM)])


def swap_cores(x):
    return lax.ppermute(x, "tile", [(i, i ^ 1) for i in range(32)])


def local(prior, measurement_matrix, readings, noise, nearby, damping):
    me = lax.axis_index("mem").astype(jnp.int32)
    tile = lax.axis_index("tile").astype(jnp.int32)
    where = jnp.stack([me, tile])
    extra = jnp.concatenate(
        [readings.reshape(2, 128), noise.reshape(2, 128), jnp.zeros((4, 128), F32)], axis=0
    )
    *pieces, obs = local_obs(where, prior, measurement_matrix, extra)
    outer = lax.ppermute(
        obs,
        "tile",
        [(i, i + 1) for i in range(1, 31, 2)] + [(i + 1, i) for i in range(1, 31, 2)],
    )
    own = jnp.concatenate([obs, send(obs, 4)], axis=0)
    got = [pieces[0]] + [send(pieces[s], s) for s in range(1, 4)]
    own1, own3 = send(own, 1), send(own, 3)
    far = jnp.concatenate([outer, send(outer, 4)], axis=0)
    far1, far3 = send(far, 1), send(far, 3)
    own2 = [send(own3[:32], 1), send(own1[32:], 3)]
    sib = [swap_cores(x) for x in (own, own1, own3, *own2)]
    far2 = [send(far3[:32], 1), send(far1[32:], 3)]
    *late, _ = lax.optimization_barrier((*pieces[4:], far1))
    got += [send(x, s) for s, x in zip(range(4, MEM), late)]
    obs = (own, own1, own3, *own2, far, far1, far3, *far2, *sib)
    block_tile = nearby // 64
    slot = jnp.where(block_tile == tile, 0, jnp.where(block_tile // 2 == tile // 2, 1, 2))
    columns = (slot * 64 + nearby % 64).reshape(-1)
    weights = jnp.sqrt(1.0 / (1.0 + damping.astype(F32))).reshape(-1)
    root, offset = find_mixing(
        where, columns, weights, obs
    )
    return apply_mixing(where, root, offset, got)


def solution(mesh):
    in_specs = (
        P("mem", None, "tile"),
        P(),
        P(("tile", "mem"), None),
        P(("tile", "mem"), None),
        P(("tile", "mem"), None),
        P(("tile", "mem"), None),
    )
    out_specs = P(None, None, ("tile", "mem"))
    return jax.shard_map(local, mesh=mesh, in_specs=in_specs, out_specs=out_specs, check_vma=False)
```

time: 164 us -> 129 us (0.79)
  waiting for transfers between devices: 68.7 us -> 45.5 us
  Pallas kernels: 60.2 us -> 37.5 us
  starting transfers between devices: 25.9 us -> 34.8 us
  local copies, waits for them, and re-layouts: 7.46 us -> 10.3 us
    pallas_call x1 -> x2, Pallas kernels: 56.2 us -> 33.5 us  [the longest x1 26.3 us: find_mixing(): pl.pallas_call(mixing_kernel, out_shape=[jax.ShapeDtypeStruct((16, 256, 2...]
    ppermute x13 -> x17, waiting for transfers between devices: 64.1 us -> 44.4 us  [send(): return lax.ppermute(x, 'mem', [(i, i ^ flip) for i in range(MEM)])]
    ppermute x13 -> x17, starting transfers between devices: 18.9 us -> 28.6 us  [send(): return lax.ppermute(x, 'mem', [(i, i ^ flip) for i in range(MEM)])]
    ppermute x1, waiting for transfers between devices: 4.59 us -> 0.01 us  [local(): lax.ppermute(obs, 'tile', [(i, i + 1) for i in range(1, 31, 2)] + [(i + 1...]
    unnamed x22 -> x33, local copies, waits for them, and re-layouts: 3.6 us -> 6.09 us
  transfers between devices with their start and end apart: 18 -> 23, of which waited for: 11 -> 8; matrix products, arithmetic and copies ran while one was open for 2% -> 2% of each run, Pallas kernels for 0% -> 21%
where the time goes in v1:
time: 129 us; the launch traced here: 128 us
  waiting for transfers between devices  45.5 us (35%)
  Pallas kernels  37.5 us (29%)
  starting transfers between devices  34.8 us (27%)
  local copies, waits for them, and re-layouts  10.3 us (8%)
    ppermute x17, waiting for transfers between devices, send(): return lax.ppermute(x, 'mem', [(i, i ^ flip) for i in range(MEM)])  44.4 us
    ppermute x17, starting transfers between devices, send(): return lax.ppermute(x, 'mem', [(i, i ^ flip) for i in range(MEM)])  28.6 us
    pallas_call x1, Pallas kernels, find_mixing(): pl.pallas_call(mixing_kernel, out_shape=[jax.ShapeDtypeStruct((16, 256, 2...  26.3 us
    pallas_call x1, Pallas kernels, apply_mixing(): pl.pallas_call(apply_kernel, out_shape=jax.ShapeDtypeStruct((256, 4, 512)...  7.1 us
    unnamed x33, local copies, waits for them, and re-layouts  6.09 us
    ppermute x1, starting transfers between devices, local(): lax.ppermute(obs, 'tile', [(i, i + 1) for i in range(1, 31, 2)] + [(i + 1...  4.97 us
    pallas_call x1, Pallas kernels, local_obs(): pl.pallas_call(obs_kernel, out_shape=[jax.ShapeDtypeStruct((members, 2048...  4.03 us
  transfers between devices with their start and end apart: 23, of which 8 were waited for; matrix products, arithmetic and copies ran while one was open for 2% of the time, Pallas kernels for 21%

profile of v1, /device:TPU:192, one launch (start us, length us, event | category | flops | bytes accessed | tf_op | source)
XLA Modules:
  0.0 128.5 jit_solution(5312669781349166202)
XLA Ops:
  0.8 0.8 reshape.15
  1.5 0.9 copy.12.map_ref
  2.7 1.6 %copy-done = f32[32,4,4096]{2,1,0:T(4,128)S(1)} copy-done((f32[32,4,4096]{2,1,0:T(4,128)S(1)}, f32[32,4,4096]{2,1,0:T(4,128)}, u32[]{:S(2)}) %copy-start) | copy-done | bytes 2097176
  4.3 4.0 %local_obs.1 = (f32[32,2048]{1,0:T(8,128)S(1)}, f32[32,2048]{1,0:T(8,128)S(1)}, f32[32,2048]{1,0:T(8,128)S(1)}, f32[32,2048]{1,0:T(8,128)S(1)}, f32[32,2048]{1,0...) custom-call(s32[2]{0:T(128)S(1)} %pad_add_fusion.where_ref.refs_0_, ...), custom_call_target="tpu_custom_call" | custom-call | tf_op jit(solution)/shard_map/local_obs/pallas_call | solution.py:84
  10.5 5.0 %collective-permute-start.5 = (f32[32,2176]{1,0:T(8,128)S(1)}, f32[32,2176]{1,0:T(8,128)S(1)}, u32[]{:S(2)}, u32[]{:S(2)}) collective-permute-start(f32[32,2176]{1,0:T(8,128)S(1)} %get-tuple-element.20), channel_id=1, source_target_pairs={{1,2},{3,4},{5,6},{7,8},{9,10},{11,12},{13,14},{15,16},{17,18},{19... | collective-permute-start | bytes 835592 | tf_op jit(solution)/shard_map/ppermute | solution.py:310
  15.4 0.8 collective-permute-start
  16.2 1.5 %collective-permute-start.16 = (f32[32,2048]{1,0:T(8,128)S(1)}, f32[32,2048]{1,0:T(8,128)S(1)}, u32[]{:S(2)}, u32[]{:S(2)}) collective-permute-start(f32[32,2048]{1,0:T(8,128)S(1)} %get-tuple-element.24), channel_id=1, source_target_pairs={{0,32},{32,0},{64,96},{96,64},{128,160},{160,128},{192,224},{224,1... | collective-permute-start | bytes 786440 | tf_op jit(solution)/shard_map/ppermute | solution.py:295
  17.7 9.5 %collective-permute-done = f32[32,2176]{1,0:T(8,128)S(1)} collective-permute-done((f32[32,2176]{1,0:T(8,128)S(1)}, f32[32,2176]{1,0:T(8,128)S(1)}, u32[]{:S(2)}, u32[]{:S(2)}) %collective-permute-start) | collective-permute-done | bytes 278560 | tf_op jit(solution)/shard_map/ppermute | solution.py:295
  27.2 2.8 %collective-permute-start.2 = (f32[64,2176]{1,0:T(8,128)S(1)}, f32[64,2176]{1,0:T(8,128)S(1)}, u32[]{:S(2)}, u32[]{:S(2)}) collective-permute-start(f32[64,2176]{1,0:T(8,128)S(1)} %constant_dynamic-update-slice_fusion.refs_3_), channel_id=1, source_target_pairs={{0,96},{32,64},{64,32},{96,0},{128,224},{160,192},{192,160},{224,1... | collective-permute-start | bytes 1671176 | tf_op jit(solution)/shard_map/ppermute | solution.py:295
  30.3 1.3 %collective-permute-start.6 = (f32[32,2176]{1,0:T(8,128)S(1)}, f32[32,2176]{1,0:T(8,128)S(1)}, u32[]{:S(2)}, u32[]{:S(2)}) collective-permute-start(f32[32,2176]{1,0:T(8,128)S(1)} %collective-permute-done.5), channel_id=1, source_target_pairs={{0,128},{32,160},{64,192},{96,224},{128,0},{160,32},{192,64},{224,... | collective-permute-start | bytes 835592 | tf_op jit(solution)/shard_map/ppermute | solution.py:295
  31.6 7.8 %collective-permute-done.6 = f32[32,2176]{1,0:T(8,128)S(1)} collective-permute-done((f32[32,2176]{1,0:T(8,128)S(1)}, f32[32,2176]{1,0:T(8,128)S(1)}, u32[]{:S(2)}, u32[]{:S(2)}) %collective-permute-start.6) | collective-permute-done | bytes 278560 | tf_op jit(solution)/shard_map/ppermute | solution.py:295
  39.5 1.4 %collective-permute-start.8 = (f32[64,2176]{1,0:T(8,128)S(1)}, f32[64,2176]{1,0:T(8,128)S(1)}, u32[]{:S(2)}, u32[]{:S(2)}) collective-permute-start(f32[64,2176]{1,0:T(8,128)S(1)} %constant_dynamic-update-slice_fusion.2.refs_8_), channel_id=1, source_target_pairs={{0,96},{32,64},{64,32},{96,0},{128,224},{160,192},{192,160},{224,1... | collective-permute-start | bytes 1671176 | tf_op jit(solution)/shard_map/ppermute | solution.py:295
  41.6 1.6 %collective-permute-done.2.refs_5_ = f32[64,2176]{1,0:T(8,128)S(1)} collective-permute-done((f32[64,2176]{1,0:T(8,128)S(1)}, f32[64,2176]{1,0:T(8,128)S(1)}, u32[]{:S(2)}, u32[]{:S(2)}) %collective-permute-start.2) | collective-permute-done | bytes 557088 | tf_op jit(solution)/shard_map/ppermute | solution.py:295
  45.2 4.0 %collective-permute-start.17 = (f32[32,2048]{1,0:T(8,128)S(1)}, f32[32,2048]{1,0:T(8,128)S(1)}, u32[]{:S(2)}, u32[]{:S(2)}) collective-permute-start(f32[32,2048]{1,0:T(8,128)S(1)} %get-tuple-element.25), channel_id=1, source_target_pairs={{0,64},{32,96},{64,0},{96,32},{128,192},{160,224},{192,128},{224,1... | collective-permute-start | bytes 786440 | tf_op jit(solution)/shard_map/ppermute | solution.py:295
  49.9 19.1 %collective-permute-done.17.refs_2_ = f32[32,2048]{1,0:T(8,128)S(1)} collective-permute-done((f32[32,2048]{1,0:T(8,128)S(1)}, f32[32,2048]{1,0:T(8,128)S(1)}, u32[]{:S(2)}, u32[]{:S(2)}) %collective-permute-start.17) | collective-permute-done | bytes 262176 | tf_op jit(solution)/shard_map/ppermute | solution.py:295
  69.0 2.4 %collective-permute-start.4 = (f32[32,2176]{1,0:T(8,128)}, f32[32,2176]{1,0:T(8,128)}, u32[]{:S(2)}, u32[]{:S(2)}) collective-permute-start(f32[32,2176]{1,0:T(8,128)} %slice.17), channel_id=1, source_target_pairs={{0,96},{32,64},{64,32},{96,0},{128,224},{160,192},{192,160},{224,1... | collective-permute-start | bytes 835592 | tf_op jit(solution)/shard_map/ppermute | solution.py:295
  73.5 5.3 %collective-permute-done.4.refs_7_ = f32[32,2176]{1,0:T(8,128)} collective-permute-done((f32[32,2176]{1,0:T(8,128)}, f32[32,2176]{1,0:T(8,128)}, u32[]{:S(2)}, u32[]{:S(2)}) %collective-permute-start.4) | collective-permute-done | bytes 278560 | tf_op jit(solution)/shard_map/ppermute | solution.py:295
  78.8 2.9 %collective-permute-start.10 = (f32[32,2176]{1,0:T(8,128)}, f32[32,2176]{1,0:T(8,128)}, u32[]{:S(2)}, u32[]{:S(2)}) collective-permute-start(f32[32,2176]{1,0:T(8,128)} %slice.19), channel_id=1, source_target_pairs={{0,96},{32,64},{64,32},{96,0},{128,224},{160,192},{192,160},{224,1... | collective-permute-start | bytes 835592 | tf_op jit(solution)/shard_map/ppermute | solution.py:295
  82.5 1.1 collective-permute-done.15.refs_17_
  83.6 1.3 %collective-permute-start.19 = (f32[32,2048]{1,0:T(8,128)}, f32[32,2048]{1,0:T(8,128)S(1)}, u32[]{:S(2)}, u32[]{:S(2)}) collective-permute-start(f32[32,2048]{1,0:T(8,128)} %copy-done.7), channel_id=1, source_target_pairs={{0,128},{32,160},{64,192},{96,224},{128,0},{160,32},{192,64},{224,... | collective-permute-start | bytes 786440 | tf_op jit(solution)/shard_map/ppermute | solution.py:295
  84.9 4.2 %collective-permute-start.21 = (f32[32,2048]{1,0:T(8,128)}, f32[32,2048]{1,0:T(8,128)}, u32[]{:S(2)}, u32[]{:S(2)}) collective-permute-start(f32[32,2048]{1,0:T(8,128)} %copy-done.5), channel_id=1, source_target_pairs={{0,192},{32,224},{64,128},{96,160},{128,64},{160,96},{192,0},{224,... | collective-permute-start | bytes 786440 | tf_op jit(solution)/shard_map/ppermute | solution.py:295
  89.6 4.0 %collective-permute-start.22 = (f32[32,2048]{1,0:T(8,128)}, f32[32,2048]{1,0:T(8,128)}, u32[]{:S(2)}, u32[]{:S(2)}) collective-permute-start(f32[32,2048]{1,0:T(8,128)} %copy-done.4), channel_id=1, source_target_pairs={{0,224},{32,192},{64,160},{96,128},{128,96},{160,64},{192,32},{224... | collective-permute-start | bytes 786440 | tf_op jit(solution)/shard_map/ppermute | solution.py:295
  93.6 26.3 %mixing.1 = (f32[16,256,256]{2,1,0:T(8,128)}, f32[256,128]{1,0:T(8,128)S(1)}) custom-call(s32[2]{0:T(128)S(1)} %pad_add_fusion.where_ref.refs_0_, s32[128]{0:T(128)S(1)} %reshape.12.refs_1_, f32[128]{0:T(128)S(1)} %reshape.13.refs_2_, f32[64,2176]{1,0:T(8,128)S(1)} %constant_dynamic-update-slice_fusion.refs_3_, ...), custom_call_target="tpu_custom_call" | custom-call | flops 16106127360 | bytes 12582912 | tf_op jit(solution)/shard_map/mixing/pallas_call | solution.py:256
  121.4 7.1 %apply.1 = f32[256,4,512]{2,1,0:T(4,128)} custom-call(s32[2]{0:T(128)} %copy-done.3, f32[16,256,256]{2,1,0:T(8,128)} %get-tuple-element.21.root_ref, f32[256,128]{1,0:T(8,128)} %copy-done.2, f32[32,2048]{1,0:T(8,128)} %copy-done.1, f32[32,2048]{1,0:T(8,128)} %copy-done.9, f32[32,2048]{1,0:T(8,128)} %copy-done.10, f32[32,2048]{1,0:T(8,128)} %copy-done.11, ...), custom_call_target="tpu_custom_call" | custom-call | tf_op jit(solution)/shard_map/apply/pallas_call | solution.py:282
  (76 shorter events, 11.6 us)
Async XLA Ops:
  2.5 91.0 %copy-start.3 = (s32[2]{0:T(128)}, s32[2]{0:T(128)S(1)}, u32[]{:S(2)}) copy-start(s32[2]{0:T(128)S(1)} %pad_add_fusion.where_ref.refs_0_) | copy-start | bytes 28
  10.5 19.8 %collective-permute-start.5 = (f32[32,2176]{1,0:T(8,128)S(1)}, f32[32,2176]{1,0:T(8,128)S(1)}, u32[]{:S(2)}, u32[]{:S(2)}) collective-permute-start(f32[32,2176]{1,0:T(8,128)S(1)} %get-tuple-element.20), channel_id=1, source_target_pairs={{1,2},{3,4},{5,6},{7,8},{9,10},{11,12},{13,14},{15,16},{17,18},{19... | collective-permute-start | bytes 835592 | tf_op jit(solution)/shard_map/ppermute | solution.py:310
  15.4 11.8 %collective-permute-start = (f32[32,2176]{1,0:T(8,128)S(1)}, f32[32,2176]{1,0:T(8,128)S(1)}, u32[]{:S(2)}, u32[]{:S(2)}) collective-permute-start(f32[32,2176]{1,0:T(8,128)S(1)} %get-tuple-element.20), channel_id=1, source_target_pairs={{0,128},{32,160},{64,192},{96,224},{128,0},{160,32},{192,64},{224,... | collective-permute-start | bytes 835592 | tf_op jit(solution)/shard_map/ppermute | solution.py:295
  16.2 27.8 %collective-permute-start.16 = (f32[32,2048]{1,0:T(8,128)S(1)}, f32[32,2048]{1,0:T(8,128)S(1)}, u32[]{:S(2)}, u32[]{:S(2)}) collective-permute-start(f32[32,2048]{1,0:T(8,128)S(1)} %get-tuple-element.24), channel_id=1, source_target_pairs={{0,32},{32,0},{64,96},{96,64},{128,160},{160,128},{192,224},{224,1... | collective-permute-start | bytes 786440 | tf_op jit(solution)/shard_map/ppermute | solution.py:295
  27.2 16.1 %collective-permute-start.2 = (f32[64,2176]{1,0:T(8,128)S(1)}, f32[64,2176]{1,0:T(8,128)S(1)}, u32[]{:S(2)}, u32[]{:S(2)}) collective-permute-start(f32[64,2176]{1,0:T(8,128)S(1)} %constant_dynamic-update-slice_fusion.refs_3_), channel_id=1, source_target_pairs={{0,96},{32,64},{64,32},{96,0},{128,224},{160,192},{192,160},{224,1... | collective-permute-start | bytes 1671176 | tf_op jit(solution)/shard_map/ppermute | solution.py:295
  30.1 15.1 %collective-permute-start.1 = (f32[64,2176]{1,0:T(8,128)S(1)}, f32[64,2176]{1,0:T(8,128)S(1)}, u32[]{:S(2)}, u32[]{:S(2)}) collective-permute-start(f32[64,2176]{1,0:T(8,128)S(1)} %constant_dynamic-update-slice_fusion.refs_3_), channel_id=1, source_target_pairs={{0,32},{32,0},{64,96},{96,64},{128,160},{160,128},{192,224},{224,1... | collective-permute-start | bytes 1671176 | tf_op jit(solution)/shard_map/ppermute | solution.py:295
  30.3 9.2 %collective-permute-start.6 = (f32[32,2176]{1,0:T(8,128)S(1)}, f32[32,2176]{1,0:T(8,128)S(1)}, u32[]{:S(2)}, u32[]{:S(2)}) collective-permute-start(f32[32,2176]{1,0:T(8,128)S(1)} %collective-permute-done.5), channel_id=1, source_target_pairs={{0,128},{32,160},{64,192},{96,224},{128,0},{160,32},{192,64},{224,... | collective-permute-start | bytes 835592 | tf_op jit(solution)/shard_map/ppermute | solution.py:295
  39.5 31.9 %collective-permute-start.8 = (f32[64,2176]{1,0:T(8,128)S(1)}, f32[64,2176]{1,0:T(8,128)S(1)}, u32[]{:S(2)}, u32[]{:S(2)}) collective-permute-start(f32[64,2176]{1,0:T(8,128)S(1)} %constant_dynamic-update-slice_fusion.2.refs_8_), channel_id=1, source_target_pairs={{0,96},{32,64},{64,32},{96,0},{128,224},{160,192},{192,160},{224,1... | collective-permute-start | bytes 1671176 | tf_op jit(solution)/shard_map/ppermute | solution.py:295
  40.9 31.0 %collective-permute-start.7 = (f32[64,2176]{1,0:T(8,128)S(1)}, f32[64,2176]{1,0:T(8,128)S(1)}, u32[]{:S(2)}, u32[]{:S(2)}) collective-permute-start(f32[64,2176]{1,0:T(8,128)S(1)} %constant_dynamic-update-slice_fusion.2.refs_8_), channel_id=1, source_target_pairs={{0,32},{32,0},{64,96},{96,64},{128,160},{160,128},{192,224},{224,1... | collective-permute-start | bytes 1671176 | tf_op jit(solution)/shard_map/ppermute | solution.py:295
  43.3 30.2 %collective-permute-start.11 = (f32[64,2176]{1,0:T(8,128)S(1)}, f32[64,2176]{1,0:T(8,128)}, u32[]{:S(2)}, u32[]{:S(2)}) collective-permute-start(f32[64,2176]{1,0:T(8,128)S(1)} %constant_dynamic-update-slice_fusion.refs_3_), channel_id=1, source_target_pairs={{0,1},{1,0},{2,3},{3,2},{4,5},{5,4},{6,7},{7,6},{8,9},{9,8},{10,11... | collective-permute-start | bytes 1671176 | tf_op jit(solution)/shard_map/ppermute | solution.py:299
  44.0 27.4 %collective-permute-start.3 = (f32[32,2176]{1,0:T(8,128)S(1)}, f32[32,2176]{1,0:T(8,128)}, u32[]{:S(2)}, u32[]{:S(2)}) collective-permute-start(f32[32,2176]{1,0:T(8,128)S(1)} %slice.16), channel_id=1, source_target_pairs={{0,32},{32,0},{64,96},{96,64},{128,160},{160,128},{192,224},{224,1... | collective-permute-start | bytes 835592 | tf_op jit(solution)/shard_map/ppermute | solution.py:295
  45.2 23.8 %collective-permute-start.17 = (f32[32,2048]{1,0:T(8,128)S(1)}, f32[32,2048]{1,0:T(8,128)S(1)}, u32[]{:S(2)}, u32[]{:S(2)}) collective-permute-start(f32[32,2048]{1,0:T(8,128)S(1)} %get-tuple-element.25), channel_id=1, source_target_pairs={{0,64},{32,96},{64,0},{96,32},{128,192},{160,224},{192,128},{224,1... | collective-permute-start | bytes 786440 | tf_op jit(solution)/shard_map/ppermute | solution.py:295
  69.0 9.8 %collective-permute-start.4 = (f32[32,2176]{1,0:T(8,128)}, f32[32,2176]{1,0:T(8,128)}, u32[]{:S(2)}, u32[]{:S(2)}) collective-permute-start(f32[32,2176]{1,0:T(8,128)} %slice.17), channel_id=1, source_target_pairs={{0,96},{32,64},{64,32},{96,0},{128,224},{160,192},{192,160},{224,1... | collective-permute-start | bytes 835592 | tf_op jit(solution)/shard_map/ppermute | solution.py:295
  71.4 10.3 %collective-permute-start.14 = (f32[32,2176]{1,0:T(8,128)}, f32[32,2176]{1,0:T(8,128)}, u32[]{:S(2)}, u32[]{:S(2)}) collective-permute-start(f32[32,2176]{1,0:T(8,128)} %collective-permute-done.3.refs_6_), channel_id=1, source_target_pairs={{0,1},{1,0},{2,3},{3,2},{4,5},{5,4},{6,7},{7,6},{8,9},{9,8},{10,11... | collective-permute-start | bytes 835592 | tf_op jit(solution)/shard_map/ppermute | solution.py:299
  71.4 10.7 %collective-permute-start.13 = (f32[64,2176]{1,0:T(8,128)S(1)}, f32[64,2176]{1,0:T(8,128)}, u32[]{:S(2)}, u32[]{:S(2)}) collective-permute-start(f32[64,2176]{1,0:T(8,128)S(1)} %collective-permute-done.2.refs_5_), channel_id=1, source_target_pairs={{0,1},{1,0},{2,3},{3,2},{4,5},{5,4},{6,7},{7,6},{8,9},{9,8},{10,11... | collective-permute-start | bytes 1671176 | tf_op jit(solution)/shard_map/ppermute | solution.py:299
  71.9 13.0 %collective-permute-start.12 = (f32[64,2176]{1,0:T(8,128)S(1)}, f32[64,2176]{1,0:T(8,128)}, u32[]{:S(2)}, u32[]{:S(2)}) collective-permute-start(f32[64,2176]{1,0:T(8,128)S(1)} %collective-permute-done.1.refs_4_), channel_id=1, source_target_pairs={{0,1},{1,0},{2,3},{3,2},{4,5},{5,4},{6,7},{7,6},{8,9},{9,8},{10,11... | collective-permute-start | bytes 1671176 | tf_op jit(solution)/shard_map/ppermute | solution.py:299
  73.5 11.4 %collective-permute-start.9 = (f32[32,2176]{1,0:T(8,128)}, f32[32,2176]{1,0:T(8,128)}, u32[]{:S(2)}, u32[]{:S(2)}) collective-permute-start(f32[32,2176]{1,0:T(8,128)} %slice.18), channel_id=1, source_target_pairs={{0,32},{32,0},{64,96},{96,64},{128,160},{160,128},{192,224},{224,1... | collective-permute-start | bytes 835592 | tf_op jit(solution)/shard_map/ppermute | solution.py:295
  78.8 10.8 %collective-permute-start.10 = (f32[32,2176]{1,0:T(8,128)}, f32[32,2176]{1,0:T(8,128)}, u32[]{:S(2)}, u32[]{:S(2)}) collective-permute-start(f32[32,2176]{1,0:T(8,128)} %slice.19), channel_id=1, source_target_pairs={{0,96},{32,64},{64,32},{96,0},{128,224},{160,192},{192,160},{224,1... | collective-permute-start | bytes 835592 | tf_op jit(solution)/shard_map/ppermute | solution.py:295
  81.7 1.9 %collective-permute-start.15 = (f32[32,2176]{1,0:T(8,128)}, f32[32,2176]{1,0:T(8,128)}, u32[]{:S(2)}, u32[]{:S(2)}) collective-permute-start(f32[32,2176]{1,0:T(8,128)} %collective-permute-done.4.refs_7_), channel_id=1, source_target_pairs={{0,1},{1,0},{2,3},{3,2},{4,5},{5,4},{6,7},{7,6},{8,9},{9,8},{10,11... | collective-permute-start | bytes 835592 | tf_op jit(solution)/shard_map/ppermute | solution.py:299
  82.1 38.5 %collective-permute-start.18 = (f32[32,2048]{1,0:T(8,128)}, f32[32,2048]{1,0:T(8,128)S(1)}, u32[]{:S(2)}, u32[]{:S(2)}) collective-permute-start(f32[32,2048]{1,0:T(8,128)} %copy-done.8), channel_id=1, source_target_pairs={{0,96},{32,64},{64,32},{96,0},{128,224},{160,192},{192,160},{224,1... | collective-permute-start | bytes 786440 | tf_op jit(solution)/shard_map/ppermute | solution.py:295
  83.6 37.0 %collective-permute-start.19 = (f32[32,2048]{1,0:T(8,128)}, f32[32,2048]{1,0:T(8,128)S(1)}, u32[]{:S(2)}, u32[]{:S(2)}) collective-permute-start(f32[32,2048]{1,0:T(8,128)} %copy-done.7), channel_id=1, source_target_pairs={{0,128},{32,160},{64,192},{96,224},{128,0},{160,32},{192,64},{224,... | collective-permute-start | bytes 786440 | tf_op jit(solution)/shard_map/ppermute | solution.py:295
  84.9 35.7 %collective-permute-start.20 = (f32[32,2048]{1,0:T(8,128)}, f32[32,2048]{1,0:T(8,128)}, u32[]{:S(2)}, u32[]{:S(2)}) collective-permute-start(f32[32,2048]{1,0:T(8,128)} %copy-done.6), channel_id=1, source_target_pairs={{0,160},{32,128},{64,224},{96,192},{128,32},{160,0},{192,96},{224,... | collective-permute-start | bytes 786440 | tf_op jit(solution)/shard_map/ppermute | solution.py:295
  84.9 35.7 %collective-permute-start.21 = (f32[32,2048]{1,0:T(8,128)}, f32[32,2048]{1,0:T(8,128)}, u32[]{:S(2)}, u32[]{:S(2)}) collective-permute-start(f32[32,2048]{1,0:T(8,128)} %copy-done.5), channel_id=1, source_target_pairs={{0,192},{32,224},{64,128},{96,160},{128,64},{160,96},{192,0},{224,... | collective-permute-start | bytes 786440 | tf_op jit(solution)/shard_map/ppermute | solution.py:295
  89.6 31.0 %collective-permute-start.22 = (f32[32,2048]{1,0:T(8,128)}, f32[32,2048]{1,0:T(8,128)}, u32[]{:S(2)}, u32[]{:S(2)}) collective-permute-start(f32[32,2048]{1,0:T(8,128)} %copy-done.4), channel_id=1, source_target_pairs={{0,224},{32,192},{64,160},{96,128},{128,96},{160,64},{192,32},{224... | collective-permute-start | bytes 786440 | tf_op jit(solution)/shard_map/ppermute | solution.py:295
  (14 other events, 230.4 us)

commit v2 on v1

--- a/solution.py
+++ b/solution.py
@@ -48,7 +48,7 @@
     return (lane // 32) % 2 == 1, lane // 64 == 1
 
 
-def obs_kernel(where_ref, prior_ref, map_ref, extra_ref, *refs):
+def obs_kernel(where_ref, prior_ref, map_ref, reading_ref, noise_ref, *refs):
     pieces, obs_ref, stack = refs[:MEM], refs[MEM], refs[MEM + 1]
     members = prior_ref.shape[0]
     me = where_ref[0]
@@ -64,33 +64,38 @@
                 pieces[s][:, at * LANES : (at + 1) * LANES] = groups[g]
                 row = pl.multiple_of((peer * 2 + at // 8) * members, members)
                 stack[pl.ds(row, members), (at % 8) * LANES : (at % 8 + 1) * LANES] = groups[g]
-    halves = [map_ref[l, 32 * h : 32 * h + 32, :] for h in range(2) for l in range(4)]
-    tall = jnp.concatenate(halves, axis=0)
-    wide = jnp.concatenate([tall] * 4, axis=1)
-    big = jnp.concatenate([wide] * 4, axis=0)
+    halves = [map_ref[l, :, 32 * h : 32 * h + 32] for h in range(2) for l in range(4)]
+    thin = jnp.concatenate(halves, axis=1)
+    tall = jnp.concatenate([thin] * 4, axis=0)
+    big = jnp.concatenate([tall] * 4, axis=1)
     row = lax.broadcasted_iota(jnp.int32, big.shape, 0)
     lane = lax.broadcasted_iota(jnp.int32, big.shape, 1)
-    weights = jnp.where(row // 256 == lane // 32, big, 0.0)
-    values = mul3(split(stack[...]), split(weights))
+    weights = jnp.where(lane // 256 == row // 32, big, 0.0)
+    (xh, xl), (wh, wl) = split(stack[...]), split(weights)
+    values = dot_nt(xh, wh) + (dot_nt(xh, wl) + dot_nt(xl, wh))
     for q in range(16):
         obs_ref[:, q * LANES : (q + 1) * LANES] = values[q * members : (q + 1) * members]
-    obs_ref[0:8, 2048:2176] = extra_ref[...]
-    obs_ref[8:, 2048:2176] = jnp.zeros((members - 8, LANES), F32)
-
-
-def local_obs(where, prior, measurement_matrix, extra):
+    obs_ref[:, 2048:2176] = jnp.zeros((members, LANES), F32)
+    for at, ref in enumerate((reading_ref, noise_ref)):
+        for half in range(2):
+            line = [ref[half * 4 + j : half * 4 + j + 1, :] for j in range(4)]
+            at_row = at * 2 + half
+            obs_ref[at_row : at_row + 1, 2048:2176] = jnp.concatenate(line, axis=1)
+
+
+def local_obs(where, prior, measurement_map, readings, noise):
     members = prior.shape[0]
     vmem = pl.BlockSpec(memory_space=pltpu.VMEM)
     return pl.pallas_call(
         obs_kernel,
         out_shape=[jax.ShapeDtypeStruct((members, 2048), F32)] * MEM
         + [jax.ShapeDtypeStruct((members, 2176), F32)],
-        in_specs=[pl.BlockSpec(memory_space=pltpu.SMEM), vmem, vmem, vmem],
+        in_specs=[pl.BlockSpec(memory_space=pltpu.SMEM)] + [vmem] * 4,
         out_specs=[vmem] * (MEM + 1),
         scratch_shapes=[pltpu.VMEM((512, 1024), F32)],
-        compiler_params=pltpu.CompilerParams(vmem_limit_bytes=48 << 20),
+        compiler_params=pltpu.CompilerParams(vmem_limit_bytes=24 << 20),
         name="local_obs",
-    )(where, prior, measurement_matrix, extra)
+    )(where, prior, measurement_map, readings, noise)
 
 
 def square(p):
@@ -270,7 +275,7 @@
             pltpu.VMEM((48, 264, LANES), F32),
             pltpu.SemaphoreType.DMA((3, 8)),
         ],
-        compiler_params=pltpu.CompilerParams(vmem_limit_bytes=48 << 20),
+        compiler_params=pltpu.CompilerParams(vmem_limit_bytes=30 << 20),
         cost_estimate=pl.CostEstimate(
             flops=16 * 30 * 2 * 256**3, bytes_accessed=12 << 20, transcendentals=0
         ),
@@ -286,7 +291,7 @@
         in_specs=[SMEM, pl.BlockSpec((4, 256, 256), lambda i: (i, 0, 0)), VMEM] + [VMEM] * MEM,
         out_specs=pl.BlockSpec((256, 4, LANES), lambda i: (0, 0, i)),
         scratch_shapes=[pltpu.VMEM((16, 256, LANES), F32)],
-        compiler_params=pltpu.CompilerParams(vmem_limit_bytes=60 << 20),
+        compiler_params=pltpu.CompilerParams(vmem_limit_bytes=24 << 20),
         name="apply",
     )(where, root, offset, *pieces)
 
@@ -303,25 +308,30 @@
     me = lax.axis_index("mem").astype(jnp.int32)
     tile = lax.axis_index("tile").astype(jnp.int32)
     where = jnp.stack([me, tile])
-    extra = jnp.concatenate(
-        [readings.reshape(2, 128), noise.reshape(2, 128), jnp.zeros((4, 128), F32)], axis=0
-    )
-    *pieces, obs = local_obs(where, prior, measurement_matrix, extra)
+    measurement_map = jnp.swapaxes(measurement_matrix, 1, 2)
+    *pieces, obs = local_obs(where, prior, measurement_map, readings, noise)
+    hold = lax.optimization_barrier
+    across, got1, got3 = send(obs, 4), send(pieces[1], 1), send(pieces[3], 3)
+    across, got1, got3, obs = hold((across, got1, got3, obs))
+    own = jnp.concatenate([obs, across], axis=0)
+    own1, own3 = send(own, 1), send(own, 3)
     outer = lax.ppermute(
         obs,
         "tile",
         [(i, i + 1) for i in range(1, 31, 2)] + [(i + 1, i) for i in range(1, 31, 2)],
     )
-    own = jnp.concatenate([obs, send(obs, 4)], axis=0)
-    got = [pieces[0]] + [send(pieces[s], s) for s in range(1, 4)]
-    own1, own3 = send(own, 1), send(own, 3)
+    own1, own3, outer = hold((own1, own3, outer))
+    own2 = [send(own3[:32], 1), send(own1[32:], 3)]
     far = jnp.concatenate([outer, send(outer, 4)], axis=0)
+    sib = [swap_cores(x) for x in (own, own1, own3)]
+    far, *rest = hold((far, *own2, *sib))
+    own2, sib = rest[:2], rest[2:]
     far1, far3 = send(far, 1), send(far, 3)
-    own2 = [send(own3[:32], 1), send(own1[32:], 3)]
-    sib = [swap_cores(x) for x in (own, own1, own3, *own2)]
+    sib += [swap_cores(x) for x in own2]
+    far1, far3, *rest = hold((far1, far3, *pieces[4:], pieces[2]))
     far2 = [send(far3[:32], 1), send(far1[32:], 3)]
-    *late, _ = lax.optimization_barrier((*pieces[4:], far1))
-    got += [send(x, s) for s, x in zip(range(4, MEM), late)]
+    late = [send(x, s) for s, x in zip((4, 5, 6, 7, 2), rest)]
+    got = [pieces[0], got1, late[4], got3, *late[:4]]
     obs = (own, own1, own3, *own2, far, far1, far3, *far2, *sib)
     block_tile = nearby // 64
     slot = jnp.where(block_tile == tile, 0, jnp.where(block_tile // 2 == tile // 2, 1, 2))

time: 129 us -> 127 us (0.984); the launches traced: 128 us -> 124 us
  starting transfers between devices: 34.8 us -> 28.2 us
  local copies, waits for them, and re-layouts: 10.3 us -> 16.4 us
  Pallas kernels: 37.5 us -> 34.3 us
    unnamed x33 -> x43, local copies, waits for them, and re-layouts: 6.09 us -> 13.6 us
    ppermute x1, waiting for transfers between devices: 0.01 us -> 7.43 us  [local(): lax.ppermute(obs, 'tile', [(i, i + 1) for i in range(1, 31, 2)] + [(i + 1...]
    ppermute x17, waiting for transfers between devices: 44.4 us -> 37.7 us  [send(): return lax.ppermute(x, 'mem', [(i, i ^ flip) for i in range(MEM)])]
    ppermute x17, starting transfers between devices: 28.6 us -> 24.3 us  [send(): return lax.ppermute(x, 'mem', [(i, i ^ flip) for i in range(MEM)])]
    ppermute x1, starting transfers between devices: 4.97 us -> 2.92 us  [local(): lax.ppermute(obs, 'tile', [(i, i + 1) for i in range(1, 31, 2)] + [(i + 1...]
    pallas_call x1, Pallas kernels: 7.1 us -> 5.27 us  [apply_mixing(): pl.pallas_call(apply_kernel, out_shape=jax.ShapeDtypeStruct((256, 4, 512)...]
    reshape x2 -> x0, local copies, waits for them, and re-layouts: 1.53 us -> none  [the longest x1 0.76 us: local(): noise.reshape(2, 128)]
  transfers between devices with their start and end apart: 23 -> 23, of which waited for: 8 -> 12; matrix products, arithmetic and copies ran while one was open for 2% -> 2% of each run, Pallas kernels for 21% -> 20%
where the time goes in v2:
time: 127 us; the launch traced here: 124 us
  waiting for transfers between devices  45.2 us (36%)
  Pallas kernels  34.3 us (27%)
  starting transfers between devices  28.2 us (22%)
  local copies, waits for them, and re-layouts  16.4 us (13%)
    ppermute x17, waiting for transfers between devices, send(): return lax.ppermute(x, 'mem', [(i, i ^ flip) for i in range(MEM)])  37.7 us
    pallas_call x1, Pallas kernels, find_mixing(): pl.pallas_call(mixing_kernel, out_shape=[jax.ShapeDtypeStruct((16, 256, 2...  25.2 us
    ppermute x17, starting transfers between devices, send(): return lax.ppermute(x, 'mem', [(i, i ^ flip) for i in range(MEM)])  24.3 us
    unnamed x43, local copies, waits for them, and re-layouts  13.6 us
    ppermute x1, waiting for transfers between devices, local(): lax.ppermute(obs, 'tile', [(i, i + 1) for i in range(1, 31, 2)] + [(i + 1...  7.43 us
    pallas_call x1, Pallas kernels, apply_mixing(): pl.pallas_call(apply_kernel, out_shape=jax.ShapeDtypeStruct((256, 4, 512)...  5.27 us
    pallas_call x1, Pallas kernels, local_obs(): pl.pallas_call(obs_kernel, out_shape=[jax.ShapeDtypeStruct((members, 2048...  3.75 us
    ppermute x1, starting transfers between devices, local(): lax.ppermute(obs, 'tile', [(i, i + 1) for i in range(1, 31, 2)] + [(i + 1...  2.92 us
  transfers between devices with their start and end apart: 23, of which 12 were waited for; matrix products, arithmetic and copies ran while one was open for 2% of the time, Pallas kernels for 20%

profile of v2, /device:TPU:192, one launch (start us, length us, event | category | flops | bytes accessed | tf_op | source)
XLA Modules:
  0.0 124.4 jit_solution(12429875767519148035)
XLA Ops:
  0.1 1.6 %copy-done = f32[32,4,4096]{2,1,0:T(4,128)S(1)} copy-done((f32[32,4,4096]{2,1,0:T(4,128)S(1)}, f32[32,4,4096]{2,1,0:T(4,128)}, u32[]{:S(2)}) %copy-start) | copy-done | bytes 2097176
  3.9 3.8 %local_obs.1 = (f32[32,2048]{1,0:T(8,128)S(1)}, f32[32,2048]{1,0:T(8,128)S(1)}, f32[32,2048]{1,0:T(8,128)S(1)}, f32[32,2048]{1,0:T(8,128)S(1)}, f32[32,2048]{1,0...) custom-call(s32[2]{0:T(128)S(1)} %pad_add_fusion.where_ref.refs_0_, ...), custom_call_target="tpu_custom_call" | custom-call | tf_op jit(solution)/shard_map/local_obs/pallas_call | solution.py:89
  9.8 1.6 %collective-permute-start = (f32[32,2176]{1,0:T(8,128)S(1)}, f32[32,2176]{1,0:T(8,128)S(1)}, u32[]{:S(2)}, u32[]{:S(2)}) collective-permute-start(f32[32,2176]{1,0:T(8,128)S(1)} %get-tuple-element.39), channel_id=1, source_target_pairs={{0,128},{32,160},{64,192},{96,224},{128,0},{160,32},{192,64},{224,... | collective-permute-start | bytes 835592 | tf_op jit(solution)/shard_map/ppermute | solution.py:300
  11.4 1.5 %collective-permute-start.1 = (f32[32,2048]{1,0:T(8,128)S(1)}, f32[32,2048]{1,0:T(8,128)S(1)}, u32[]{:S(2)}, u32[]{:S(2)}) collective-permute-start(f32[32,2048]{1,0:T(8,128)S(1)} %get-tuple-element.37), channel_id=1, source_target_pairs={{0,32},{32,0},{64,96},{96,64},{128,160},{160,128},{192,224},{224,1... | collective-permute-start | bytes 786440 | tf_op jit(solution)/shard_map/ppermute | solution.py:300
  12.8 2.1 %collective-permute-start.2 = (f32[32,2048]{1,0:T(8,128)S(1)}, f32[32,2048]{1,0:T(8,128)S(1)}, u32[]{:S(2)}, u32[]{:S(2)}) collective-permute-start(f32[32,2048]{1,0:T(8,128)S(1)} %get-tuple-element.38), channel_id=1, source_target_pairs={{0,96},{32,64},{64,32},{96,0},{128,224},{160,192},{192,160},{224,1... | collective-permute-start | bytes 786440 | tf_op jit(solution)/shard_map/ppermute | solution.py:300
  14.9 4.2 %collective-permute-done.1.refs_1_ = f32[32,2048]{1,0:T(8,128)S(1)} collective-permute-done((f32[32,2048]{1,0:T(8,128)S(1)}, f32[32,2048]{1,0:T(8,128)S(1)}, u32[]{:S(2)}, u32[]{:S(2)}) %collective-permute-start.1) | collective-permute-done | bytes 262176 | tf_op jit(solution)/shard_map/ppermute | solution.py:300
  19.1 2.4 %collective-permute-done.2.refs_3_ = f32[32,2048]{1,0:T(8,128)S(1)} collective-permute-done((f32[32,2048]{1,0:T(8,128)S(1)}, f32[32,2048]{1,0:T(8,128)S(1)}, u32[]{:S(2)}, u32[]{:S(2)}) %collective-permute-start.2) | collective-permute-done | bytes 262176 | tf_op jit(solution)/shard_map/ppermute | solution.py:300
  21.6 2.2 %collective-permute-start.4 = (f32[64,2176]{1,0:T(8,128)S(1)}, f32[64,2176]{1,0:T(8,128)S(1)}, u32[]{:S(2)}, u32[]{:S(2)}) collective-permute-start(f32[64,2176]{1,0:T(8,128)S(1)} %constant_dynamic-update-slice_fusion.refs_3_), channel_id=1, source_target_pairs={{0,96},{32,64},{64,32},{96,0},{128,224},{160,192},{192,160},{224,1... | collective-permute-start | bytes 1671176 | tf_op jit(solution)/shard_map/ppermute | solution.py:300
  23.8 2.9 %collective-permute-start.5 = (f32[32,2176]{1,0:T(8,128)S(1)}, f32[32,2176]{1,0:T(8,128)S(1)}, u32[]{:S(2)}, u32[]{:S(2)}) collective-permute-start(f32[32,2176]{1,0:T(8,128)S(1)} %get-tuple-element.39), channel_id=1, source_target_pairs={{1,2},{3,4},{5,6},{7,8},{9,10},{11,12},{13,14},{15,16},{17,18},{19... | collective-permute-start | bytes 835592 | tf_op jit(solution)/shard_map/ppermute | solution.py:318
  26.7 7.4 %collective-permute-done.5 = f32[32,2176]{1,0:T(8,128)S(1)} collective-permute-done((f32[32,2176]{1,0:T(8,128)S(1)}, f32[32,2176]{1,0:T(8,128)S(1)}, u32[]{:S(2)}, u32[]{:S(2)}) %collective-permute-start.5) | collective-permute-done | bytes 278560 | tf_op jit(solution)/shard_map/ppermute | solution.py:318
  34.2 1.6 %collective-permute-done.4.refs_5_ = f32[64,2176]{1,0:T(8,128)S(1)} collective-permute-done((f32[64,2176]{1,0:T(8,128)S(1)}, f32[64,2176]{1,0:T(8,128)S(1)}, u32[]{:S(2)}, u32[]{:S(2)}) %collective-permute-start.4) | collective-permute-done | bytes 557088 | tf_op jit(solution)/shard_map/ppermute | solution.py:300
  38.7 5.8 %collective-permute-done.6 = f32[32,2176]{1,0:T(8,128)S(1)} collective-permute-done((f32[32,2176]{1,0:T(8,128)S(1)}, f32[32,2176]{1,0:T(8,128)S(1)}, u32[]{:S(2)}, u32[]{:S(2)}) %collective-permute-start.6) | collective-permute-done | bytes 278560 | tf_op jit(solution)/shard_map/ppermute | solution.py:300
  46.6 6.3 %collective-permute-done.8.refs_7_ = f32[32,2176]{1,0:T(8,128)S(1)} collective-permute-done((f32[32,2176]{1,0:T(8,128)S(1)}, f32[32,2176]{1,0:T(8,128)S(1)}, u32[]{:S(2)}, u32[]{:S(2)}) %collective-permute-start.8) | collective-permute-done | bytes 278560 | tf_op jit(solution)/shard_map/ppermute | solution.py:300
  55.4 1.8 %collective-permute-start.12 = (f32[64,2176]{1,0:T(8,128)S(1)}, f32[64,2176]{1,0:T(8,128)}, u32[]{:S(2)}, u32[]{:S(2)}) collective-permute-start(f32[64,2176]{1,0:T(8,128)S(1)} %pad_maximum_fusion.refs_8_), channel_id=1, source_target_pairs={{0,32},{32,0},{64,96},{96,64},{128,160},{160,128},{192,224},{224,1... | collective-permute-start | bytes 1671176 | tf_op jit(solution)/shard_map/ppermute | solution.py:300
  57.7 10.4 %collective-permute-done.13.refs_10_ = f32[64,2176]{1,0:T(8,128)S(1)} collective-permute-done((f32[64,2176]{1,0:T(8,128)S(1)}, f32[64,2176]{1,0:T(8,128)S(1)}, u32[]{:S(2)}, u32[]{:S(2)}) %collective-permute-start.13) | collective-permute-done | bytes 557088 | tf_op jit(solution)/shard_map/ppermute | solution.py:300
  69.4 1.7 %slice.15 = f32[32,2176]{1,0:T(8,128)} slice(f32[64,2176]{1,0:T(8,128)} %collective-permute-done.12.refs_9_), slice={[32:64], [0:2176]} | slice | bytes 557056 | tf_op jit(solution)/shard_map/slice | solution.py:332
  71.8 1.7 %collective-permute-start.14 = (f32[32,2176]{1,0:T(8,128)}, f32[32,2176]{1,0:T(8,128)}, u32[]{:S(2)}, u32[]{:S(2)}) collective-permute-start(f32[32,2176]{1,0:T(8,128)} %slice.14), channel_id=1, source_target_pairs={{0,32},{32,0},{64,96},{96,64},{128,160},{160,128},{192,224},{224,1... | collective-permute-start | bytes 835592 | tf_op jit(solution)/shard_map/ppermute | solution.py:300
  73.6 2.1 %collective-permute-start.15 = (f32[32,2176]{1,0:T(8,128)}, f32[32,2176]{1,0:T(8,128)}, u32[]{:S(2)}, u32[]{:S(2)}) collective-permute-start(f32[32,2176]{1,0:T(8,128)} %slice.15), channel_id=1, source_target_pairs={{0,96},{32,64},{64,32},{96,0},{128,224},{160,192},{192,160},{224,1... | collective-permute-start | bytes 835592 | tf_op jit(solution)/shard_map/ppermute | solution.py:300
  76.6 3.0 %collective-permute-start.20 = (f32[32,2048]{1,0:T(8,128)}, f32[32,2048]{1,0:T(8,128)S(1)}, u32[]{:S(2)}, u32[]{:S(2)}) collective-permute-start(f32[32,2048]{1,0:T(8,128)} %copy-done.16), channel_id=1, source_target_pairs={{0,160},{32,128},{64,224},{96,192},{128,32},{160,0},{192,96},{224,... | collective-permute-start | bytes 786440 | tf_op jit(solution)/shard_map/ppermute | solution.py:300
  79.6 1.8 %collective-permute-done.14.refs_11_ = f32[32,2176]{1,0:T(8,128)} collective-permute-done((f32[32,2176]{1,0:T(8,128)}, f32[32,2176]{1,0:T(8,128)}, u32[]{:S(2)}, u32[]{:S(2)}) %collective-permute-start.14) | collective-permute-done | bytes 278560 | tf_op jit(solution)/shard_map/ppermute | solution.py:300
  81.4 3.3 %collective-permute-start.21 = (f32[32,2048]{1,0:T(8,128)}, f32[32,2048]{1,0:T(8,128)S(1)}, u32[]{:S(2)}, u32[]{:S(2)}) collective-permute-start(f32[32,2048]{1,0:T(8,128)} %copy-done.15), channel_id=1, source_target_pairs={{0,192},{32,224},{64,128},{96,160},{128,64},{160,96},{192,0},{224,... | collective-permute-start | bytes 786440 | tf_op jit(solution)/shard_map/ppermute | solution.py:300
  84.7 3.2 %collective-permute-done.15.refs_12_ = f32[32,2176]{1,0:T(8,128)} collective-permute-done((f32[32,2176]{1,0:T(8,128)}, f32[32,2176]{1,0:T(8,128)}, u32[]{:S(2)}, u32[]{:S(2)}) %collective-permute-start.15) | collective-permute-done | bytes 278560 | tf_op jit(solution)/shard_map/ppermute | solution.py:300
  93.8 25.2 %mixing.1 = (f32[16,256,256]{2,1,0:T(8,128)S(1)}, f32[256,128]{1,0:T(8,128)S(1)}) custom-call(s32[2]{0:T(128)S(1)} %pad_add_fusion.where_ref.refs_0_, s32[128]{0:T(128)S(1)} %reshape.6.refs_1_, f32[128]{0:T(128)S(1)} %reshape.7.refs_2_, f32[64,2176]{1,0:T(8,128)S(1)} %copy-done.2, f32[64,2176]{1,0:T(8,128)S(1)} %collective-permute-done.3.refs_4_, ...), custom_call_target="tpu_custom_call" | custom-call | flops 16106127360 | bytes 12582912 | tf_op jit(solution)/shard_map/mixing/pallas_call | solution.py:261
  119.1 5.3 %apply.1 = f32[256,4,512]{2,1,0:T(4,128)} custom-call(s32[2]{0:T(128)S(1)} %pad_add_fusion.where_ref.refs_0_, f32[16,256,256]{2,1,0:T(8,128)S(1)} %get-tuple-element.57.root_ref, f32[256,128]{1,0:T(8,128)S(1)} %get-tuple-element.58.offset_ref, f32[32,2048]{1,0:T(8,128)S(1)} %get-tuple-element.59.refs_0_, f32[32,2048]{1,0:T(8,128)S(1)} %collective-permute-done.1.refs_1_, ...), custom_call_target="tpu_custom_call" | custom-call | tf_op jit(solution)/shard_map/apply/pallas_call | solution.py:287
  (81 shorter events, 21.5 us)
Async XLA Ops:
  9.8 11.8 %collective-permute-start = (f32[32,2176]{1,0:T(8,128)S(1)}, f32[32,2176]{1,0:T(8,128)S(1)}, u32[]{:S(2)}, u32[]{:S(2)}) collective-permute-start(f32[32,2176]{1,0:T(8,128)S(1)} %get-tuple-element.39), channel_id=1, source_target_pairs={{0,128},{32,160},{64,192},{96,224},{128,0},{160,32},{192,64},{224,... | collective-permute-start | bytes 835592 | tf_op jit(solution)/shard_map/ppermute | solution.py:300
  11.4 7.8 %collective-permute-start.1 = (f32[32,2048]{1,0:T(8,128)S(1)}, f32[32,2048]{1,0:T(8,128)S(1)}, u32[]{:S(2)}, u32[]{:S(2)}) collective-permute-start(f32[32,2048]{1,0:T(8,128)S(1)} %get-tuple-element.37), channel_id=1, source_target_pairs={{0,32},{32,0},{64,96},{96,64},{128,160},{160,128},{192,224},{224,1... | collective-permute-start | bytes 786440 | tf_op jit(solution)/shard_map/ppermute | solution.py:300
  12.8 8.7 %collective-permute-start.2 = (f32[32,2048]{1,0:T(8,128)S(1)}, f32[32,2048]{1,0:T(8,128)S(1)}, u32[]{:S(2)}, u32[]{:S(2)}) collective-permute-start(f32[32,2048]{1,0:T(8,128)S(1)} %get-tuple-element.38), channel_id=1, source_target_pairs={{0,96},{32,64},{64,32},{96,0},{128,224},{160,192},{192,160},{224,1... | collective-permute-start | bytes 786440 | tf_op jit(solution)/shard_map/ppermute | solution.py:300
  21.6 54.3 %copy-start.20 = (s32[16,8]{0,1:T(8,128)S(1)}, s32[16,8]{0,1:T(8,128)}, u32[]{:S(2)}) copy-start(s32[16,8]{0,1:T(8,128)} %param.11) | copy-start | bytes 1540
  21.6 14.2 %collective-permute-start.4 = (f32[64,2176]{1,0:T(8,128)S(1)}, f32[64,2176]{1,0:T(8,128)S(1)}, u32[]{:S(2)}, u32[]{:S(2)}) collective-permute-start(f32[64,2176]{1,0:T(8,128)S(1)} %constant_dynamic-update-slice_fusion.refs_3_), channel_id=1, source_target_pairs={{0,96},{32,64},{64,32},{96,0},{128,224},{160,192},{192,160},{224,1... | collective-permute-start | bytes 1671176 | tf_op jit(solution)/shard_map/ppermute | solution.py:300
  23.8 12.6 %collective-permute-start.3 = (f32[64,2176]{1,0:T(8,128)S(1)}, f32[64,2176]{1,0:T(8,128)S(1)}, u32[]{:S(2)}, u32[]{:S(2)}) collective-permute-start(f32[64,2176]{1,0:T(8,128)S(1)} %constant_dynamic-update-slice_fusion.refs_3_), channel_id=1, source_target_pairs={{0,32},{32,0},{64,96},{96,64},{128,160},{160,128},{192,224},{224,1... | collective-permute-start | bytes 1671176 | tf_op jit(solution)/shard_map/ppermute | solution.py:300
  23.8 10.4 %collective-permute-start.5 = (f32[32,2176]{1,0:T(8,128)S(1)}, f32[32,2176]{1,0:T(8,128)S(1)}, u32[]{:S(2)}, u32[]{:S(2)}) collective-permute-start(f32[32,2176]{1,0:T(8,128)S(1)} %get-tuple-element.39), channel_id=1, source_target_pairs={{1,2},{3,4},{5,6},{7,8},{9,10},{11,12},{13,14},{15,16},{17,18},{19... | collective-permute-start | bytes 835592 | tf_op jit(solution)/shard_map/ppermute | solution.py:318
  36.4 8.1 %collective-permute-start.6 = (f32[32,2176]{1,0:T(8,128)S(1)}, f32[32,2176]{1,0:T(8,128)S(1)}, u32[]{:S(2)}, u32[]{:S(2)}) collective-permute-start(f32[32,2176]{1,0:T(8,128)S(1)} %collective-permute-done.5), channel_id=1, source_target_pairs={{0,128},{32,160},{64,192},{96,224},{128,0},{160,32},{192,64},{224,... | collective-permute-start | bytes 835592 | tf_op jit(solution)/shard_map/ppermute | solution.py:300
  36.9 8.8 %collective-permute-start.9 = (f32[64,2176]{1,0:T(8,128)S(1)}, f32[64,2176]{1,0:T(8,128)S(1)}, u32[]{:S(2)}, u32[]{:S(2)}) collective-permute-start(f32[64,2176]{1,0:T(8,128)S(1)} %constant_dynamic-update-slice_fusion.refs_3_), channel_id=1, source_target_pairs={{0,1},{1,0},{2,3},{3,2},{4,5},{5,4},{6,7},{7,6},{8,9},{9,8},{10,11... | collective-permute-start | bytes 1671176 | tf_op jit(solution)/shard_map/ppermute | solution.py:304
  36.9 16.0 %collective-permute-start.10 = (f32[64,2176]{1,0:T(8,128)S(1)}, f32[64,2176]{1,0:T(8,128)S(1)}, u32[]{:S(2)}, u32[]{:S(2)}) collective-permute-start(f32[64,2176]{1,0:T(8,128)S(1)} %collective-permute-done.3.refs_4_), channel_id=1, source_target_pairs={{0,1},{1,0},{2,3},{3,2},{4,5},{5,4},{6,7},{7,6},{8,9},{9,8},{10,11... | collective-permute-start | bytes 1671176 | tf_op jit(solution)/shard_map/ppermute | solution.py:304
  37.4 16.4 %collective-permute-start.11 = (f32[64,2176]{1,0:T(8,128)S(1)}, f32[64,2176]{1,0:T(8,128)S(1)}, u32[]{:S(2)}, u32[]{:S(2)}) collective-permute-start(f32[64,2176]{1,0:T(8,128)S(1)} %collective-permute-done.4.refs_5_), channel_id=1, source_target_pairs={{0,1},{1,0},{2,3},{3,2},{4,5},{5,4},{6,7},{7,6},{8,9},{9,8},{10,11... | collective-permute-start | bytes 1671176 | tf_op jit(solution)/shard_map/ppermute | solution.py:304
  37.4 9.2 %collective-permute-start.7 = (f32[32,2176]{1,0:T(8,128)S(1)}, f32[32,2176]{1,0:T(8,128)S(1)}, u32[]{:S(2)}, u32[]{:S(2)}) collective-permute-start(f32[32,2176]{1,0:T(8,128)S(1)} %slice.12), channel_id=1, source_target_pairs={{0,32},{32,0},{64,96},{96,64},{128,160},{160,128},{192,224},{224,1... | collective-permute-start | bytes 835592 | tf_op jit(solution)/shard_map/ppermute | solution.py:300
  44.5 8.4 %collective-permute-start.8 = (f32[32,2176]{1,0:T(8,128)S(1)}, f32[32,2176]{1,0:T(8,128)S(1)}, u32[]{:S(2)}, u32[]{:S(2)}) collective-permute-start(f32[32,2176]{1,0:T(8,128)S(1)} %slice.13), channel_id=1, source_target_pairs={{0,96},{32,64},{64,32},{96,0},{128,224},{160,192},{192,160},{224,1... | collective-permute-start | bytes 835592 | tf_op jit(solution)/shard_map/ppermute | solution.py:300
  54.6 13.4 %collective-permute-start.13 = (f32[64,2176]{1,0:T(8,128)S(1)}, f32[64,2176]{1,0:T(8,128)S(1)}, u32[]{:S(2)}, u32[]{:S(2)}) collective-permute-start(f32[64,2176]{1,0:T(8,128)S(1)} %pad_maximum_fusion.refs_8_), channel_id=1, source_target_pairs={{0,96},{32,64},{64,32},{96,0},{128,224},{160,192},{192,160},{224,1... | collective-permute-start | bytes 1671176 | tf_op jit(solution)/shard_map/ppermute | solution.py:300
  55.4 14.0 %collective-permute-start.12 = (f32[64,2176]{1,0:T(8,128)S(1)}, f32[64,2176]{1,0:T(8,128)}, u32[]{:S(2)}, u32[]{:S(2)}) collective-permute-start(f32[64,2176]{1,0:T(8,128)S(1)} %pad_maximum_fusion.refs_8_), channel_id=1, source_target_pairs={{0,32},{32,0},{64,96},{96,64},{128,160},{160,128},{192,224},{224,1... | collective-permute-start | bytes 1671176 | tf_op jit(solution)/shard_map/ppermute | solution.py:300
  57.1 19.2 %collective-permute-start.16 = (f32[32,2176]{1,0:T(8,128)S(1)}, f32[32,2176]{1,0:T(8,128)}, u32[]{:S(2)}, u32[]{:S(2)}) collective-permute-start(f32[32,2176]{1,0:T(8,128)S(1)} %collective-permute-done.7.refs_6_), channel_id=1, source_target_pairs={{0,1},{1,0},{2,3},{3,2},{4,5},{5,4},{6,7},{7,6},{8,9},{9,8},{10,11... | collective-permute-start | bytes 835592 | tf_op jit(solution)/shard_map/ppermute | solution.py:304
  57.2 19.5 %collective-permute-start.17 = (f32[32,2176]{1,0:T(8,128)}, f32[32,2176]{1,0:T(8,128)}, u32[]{:S(2)}, u32[]{:S(2)}) collective-permute-start(f32[32,2176]{1,0:T(8,128)} %copy-done.12), channel_id=1, source_target_pairs={{0,1},{1,0},{2,3},{3,2},{4,5},{5,4},{6,7},{7,6},{8,9},{9,8},{10,11... | collective-permute-start | bytes 835592 | tf_op jit(solution)/shard_map/ppermute | solution.py:304
  71.8 9.6 %collective-permute-start.14 = (f32[32,2176]{1,0:T(8,128)}, f32[32,2176]{1,0:T(8,128)}, u32[]{:S(2)}, u32[]{:S(2)}) collective-permute-start(f32[32,2176]{1,0:T(8,128)} %slice.14), channel_id=1, source_target_pairs={{0,32},{32,0},{64,96},{96,64},{128,160},{160,128},{192,224},{224,1... | collective-permute-start | bytes 835592 | tf_op jit(solution)/shard_map/ppermute | solution.py:300
  73.6 14.3 %collective-permute-start.15 = (f32[32,2176]{1,0:T(8,128)}, f32[32,2176]{1,0:T(8,128)}, u32[]{:S(2)}, u32[]{:S(2)}) collective-permute-start(f32[32,2176]{1,0:T(8,128)} %slice.15), channel_id=1, source_target_pairs={{0,96},{32,64},{64,32},{96,0},{128,224},{160,192},{192,160},{224,1... | collective-permute-start | bytes 835592 | tf_op jit(solution)/shard_map/ppermute | solution.py:300
  76.0 43.1 %collective-permute-start.18 = (f32[32,2048]{1,0:T(8,128)}, f32[32,2048]{1,0:T(8,128)S(1)}, u32[]{:S(2)}, u32[]{:S(2)}) collective-permute-start(f32[32,2048]{1,0:T(8,128)} %copy-done.18), channel_id=1, source_target_pairs={{0,64},{32,96},{64,0},{96,32},{128,192},{160,224},{192,128},{224,1... | collective-permute-start | bytes 786440 | tf_op jit(solution)/shard_map/ppermute | solution.py:300
  76.4 42.7 %collective-permute-start.19 = (f32[32,2048]{1,0:T(8,128)}, f32[32,2048]{1,0:T(8,128)S(1)}, u32[]{:S(2)}, u32[]{:S(2)}) collective-permute-start(f32[32,2048]{1,0:T(8,128)} %copy-done.17), channel_id=1, source_target_pairs={{0,128},{32,160},{64,192},{96,224},{128,0},{160,32},{192,64},{224,... | collective-permute-start | bytes 786440 | tf_op jit(solution)/shard_map/ppermute | solution.py:300
  76.6 42.5 %collective-permute-start.20 = (f32[32,2048]{1,0:T(8,128)}, f32[32,2048]{1,0:T(8,128)S(1)}, u32[]{:S(2)}, u32[]{:S(2)}) collective-permute-start(f32[32,2048]{1,0:T(8,128)} %copy-done.16), channel_id=1, source_target_pairs={{0,160},{32,128},{64,224},{96,192},{128,32},{160,0},{192,96},{224,... | collective-permute-start | bytes 786440 | tf_op jit(solution)/shard_map/ppermute | solution.py:300
  81.4 37.7 %collective-permute-start.21 = (f32[32,2048]{1,0:T(8,128)}, f32[32,2048]{1,0:T(8,128)S(1)}, u32[]{:S(2)}, u32[]{:S(2)}) collective-permute-start(f32[32,2048]{1,0:T(8,128)} %copy-done.15), channel_id=1, source_target_pairs={{0,192},{32,224},{64,128},{96,160},{128,64},{160,96},{192,0},{224,... | collective-permute-start | bytes 786440 | tf_op jit(solution)/shard_map/ppermute | solution.py:300
  87.8 31.3 %collective-permute-start.22 = (f32[32,2048]{1,0:T(8,128)}, f32[32,2048]{1,0:T(8,128)S(1)}, u32[]{:S(2)}, u32[]{:S(2)}) collective-permute-start(f32[32,2048]{1,0:T(8,128)} %copy-done.14), channel_id=1, source_target_pairs={{0,224},{32,192},{64,160},{96,128},{128,96},{160,64},{192,32},{224... | collective-permute-start | bytes 786440 | tf_op jit(solution)/shard_map/ppermute | solution.py:300
  (20 other events, 159.8 us)

commit v3 on v2

v3 whole, which is shorter than its diff:
```python
import jax
import jax.numpy as jnp
from jax import lax
from jax.experimental import pallas as pl
from jax.experimental.pallas import tpu as pltpu
from jax.sharding import PartitionSpec as P

F32 = jnp.float32
BF16 = jnp.bfloat16
MEM = 8
LANES = 128
WIDE = 4
LIMIT = 62 << 20
VMEM = pl.BlockSpec(memory_space=pltpu.VMEM)
SMEM = pl.BlockSpec(memory_space=pltpu.SMEM)
ANYWHERE = pl.BlockSpec(memory_space=pl.ANY)
HBM = pl.BlockSpec(memory_space=pltpu.HBM)


def split(x):
    hi = x.astype(BF16)
    lo = (x - hi.astype(F32)).astype(BF16)
    return hi, lo


def dot(a, b):
    return jnp.dot(a, b, preferred_element_type=F32)


def dot_nt(a, b):
    return lax.dot_general(a, b, (((1,), (1,)), ((), ())), preferred_element_type=F32)


def mul3(a, b):
    (ah, al), (bh, bl) = a, b
    return dot(ah, bh) + (dot(ah, bl) + dot(al, bh))


def exchange_lanes(parts, first, second):
    out = list(parts)
    for bit, shift, odd in ((1, 32, first), (2, 64, second)):
        for low in range(4):
            if low & bit:
                continue
            a, b = out[low], out[low | bit]
            out[low] = jnp.where(odd, pltpu.roll(b, shift, 1), a)
            out[low | bit] = jnp.where(odd, b, pltpu.roll(a, LANES - shift, 1))
    return out


def lane_bits(rows):
    lane = lax.broadcasted_iota(jnp.int32, (rows, LANES), 1)
    return (lane // 32) % 2 == 1, lane // 64 == 1


def obs_kernel(where_ref, prior_ref, map_ref, reading_ref, noise_ref, *refs):
    pieces, obs_ref = refs[:MEM], refs[MEM]
    part, staged, stack, map_in, reading_in, noise_in, in_sems, out_sems = refs[MEM + 1 :]
    members = prior_ref.shape[0]
    me = where_ref[0]
    reads = []
    for s in range(MEM):
        cells = pl.ds(pl.multiple_of((me ^ s) * 512, 512), 512)
        reads.append(pltpu.make_async_copy(prior_ref.at[:, :, cells], part.at[s], in_sems.at[s]))
    for at, (source, target) in enumerate(
        ((map_ref, map_in), (reading_ref, reading_in), (noise_ref, noise_in))
    ):
        reads.append(pltpu.make_async_copy(source, target, in_sems.at[MEM + at]))
    writes = [
        pltpu.make_async_copy(staged.at[s], pieces[s], out_sems.at[s]) for s in range(MEM)
    ]
    for read in reads:
        read.start()
    first, second = lane_bits(members)
    for s in range(MEM):
        peer = me ^ s
        reads[s].wait()
        for c in range(4):
            lanes = slice(c * LANES, (c + 1) * LANES)
            layers = [part[s, :, l, lanes] for l in range(4)]
            groups = exchange_lanes(layers, first, second)
            for g in range(4):
                at = c * 4 + g
                staged[s, :, at * LANES : (at + 1) * LANES] = groups[g]
                row = pl.multiple_of((peer * 2 + at // 8) * members, members)
                stack[pl.ds(row, members), (at % 8) * LANES : (at % 8 + 1) * LANES] = groups[g]
        writes[s].start()
    for read in reads[MEM:]:
        read.wait()
    halves = [map_in[l, :, 32 * h : 32 * h + 32] for h in range(2) for l in range(4)]
    thin = jnp.concatenate(halves, axis=1)
    tall = jnp.concatenate([thin] * 4, axis=0)
    big = jnp.concatenate([tall] * 4, axis=1)
    row = lax.broadcasted_iota(jnp.int32, big.shape, 0)
    lane = lax.broadcasted_iota(jnp.int32, big.shape, 1)
    weights = jnp.where(lane // 256 == row // 32, big, 0.0)
    (xh, xl), (wh, wl) = split(stack[...]), split(weights)
    values = dot_nt(xh, wh) + (dot_nt(xh, wl) + dot_nt(xl, wh))
    for q in range(16):
        obs_ref[:, q * LANES : (q + 1) * LANES] = values[q * members : (q + 1) * members]
    obs_ref[:, 2048:2176] = jnp.zeros((members, LANES), F32)
    for at, ref in enumerate((reading_in, noise_in)):
        for half in range(2):
            line = [ref[half * 4 + j : half * 4 + j + 1, :] for j in range(4)]
            at_row = at * 2 + half
            obs_ref[at_row : at_row + 1, 2048:2176] = jnp.concatenate(line, axis=1)
    for write in writes:
        write.wait()


def local_obs(where, prior, measurement_map, readings, noise):
    members = prior.shape[0]
    return pl.pallas_call(
        obs_kernel,
        out_shape=[jax.ShapeDtypeStruct((members, 2048), F32)] * MEM
        + [jax.ShapeDtypeStruct((members, 2176), F32)],
        in_specs=[SMEM] + [HBM] * 4,
        out_specs=[HBM] * MEM + [VMEM],
        scratch_shapes=[
            pltpu.VMEM((MEM, members, 4, 512), F32),
            pltpu.VMEM((MEM, members, 2048), F32),
            pltpu.VMEM((512, 1024), F32),
            pltpu.VMEM(measurement_map.shape, F32),
            pltpu.VMEM(readings.shape, F32),
            pltpu.VMEM(noise.shape, F32),
            pltpu.SemaphoreType.DMA((MEM + 3,)),
            pltpu.SemaphoreType.DMA((MEM,)),
        ],
        compiler_params=pltpu.CompilerParams(vmem_limit_bytes=LIMIT),
        name="local_obs",
    )(where, prior, measurement_map, readings, noise)


def square(p):
    h, l = p
    m = dot(h, l)
    return dot(h, h) + (m + dot(l, h))


def each(function, *lists):
    return [function(*items) for items in zip(*lists)]


PLACES = (0, 4, 1, 3, 5, 7, 2, 6)


def placing(me, sources, raw, sems):
    return [
        pltpu.make_async_copy(
            source, raw.at[pl.ds(pl.multiple_of((me ^ x) * 32, 32), 32), :], sems.at[at]
        )
        for at, (x, source) in enumerate(zip(PLACES, sources))
    ]


def scale_tile(raw, table, first):
    extras = [raw[32 * m : 32 * m + 8, 2048:2176] for m in range(MEM)]
    reading = jnp.concatenate([e[i : i + 1] for e in extras for i in (0, 1)], axis=1)
    noise = jnp.concatenate([e[i : i + 1] for e in extras for i in (2, 3)], axis=1)
    scale = 1.0 / jnp.sqrt(noise)
    for c in range(16):
        lanes = slice(c * LANES, (c + 1) * LANES)
        value = raw[:, lanes]
        mean = jnp.sum(value, axis=0, keepdims=True) * (1.0 / 256.0)
        table[first + c, 0:256, :] = (value - mean) * scale[:, lanes]
        table[first + c, 256:264, :] = jnp.broadcast_to(
            (reading[:, lanes] - mean) * scale[:, lanes], (8, LANES)
        )


def table_kernel(where_ref, *refs):
    table_ref, raw, sems = refs[MEM:]
    copies = placing(where_ref[0], refs[:MEM], raw, sems)
    for copy in copies:
        copy.start()
    for copy in copies:
        copy.wait()
    scale_tile(raw, table_ref, 0)


def own_table(where, parts):
    return pl.pallas_call(
        table_kernel,
        out_shape=jax.ShapeDtypeStruct((16, 264, LANES), F32),
        in_specs=[SMEM] + [ANYWHERE] * MEM,
        out_specs=VMEM,
        scratch_shapes=[pltpu.VMEM((256, 2176), F32), pltpu.SemaphoreType.DMA((MEM,))],
        compiler_params=pltpu.CompilerParams(vmem_limit_bytes=12 << 20),
        cost_estimate=pl.CostEstimate(
            flops=4 * 256 * 2048, bytes_accessed=6 << 20, transcendentals=2048
        ),
        name="own_table",
    )(where, *parts)


def mixing_kernel(*refs):
    where_ref, near_ref, damp_ref, own_ref, sib_ref = refs[:5]
    far = refs[5 : 5 + MEM]
    root_ref, offset_ref, raw, table, sems = refs[5 + MEM :]

    @pl.when(pl.program_id(0) == 0)
    def gather():
        copies = placing(where_ref[0], far, raw, sems)
        for at, source in enumerate((own_ref, sib_ref)):
            copies.append(
                pltpu.make_async_copy(
                    source, table.at[pl.ds(at * 16, 16)], sems.at[MEM + at]
                )
            )
        for copy in copies:
            copy.start()
        for copy in copies[:MEM]:
            copy.wait()
        scale_tile(raw, table, 32)
        offset_ref[...] = jnp.zeros((256, LANES), F32)
        for copy in copies[MEM:]:
            copy.wait()

    rows = lax.broadcasted_iota(jnp.int32, (256, 256), 0)
    cols = lax.broadcasted_iota(jnp.int32, (256, 256), 1)
    diagonal = rows == cols
    block = lax.broadcasted_iota(jnp.int32, (1, LANES), 1) // 32
    lane = lax.broadcasted_iota(jnp.int32, (256, LANES), 1)

    def pick(g):
        halves = []
        for h in range(2):
            piece = jnp.zeros((264, LANES), F32)
            level = jnp.zeros((1, LANES), jnp.int32)
            for i in range(4):
                entry = near_ref[4 * h + i, g]
                tile = lax.shift_right_logical(entry, 6)
                other = jnp.where((tile ^ where_ref[1]) == 1, 16, 32)
                chunk = jnp.where(tile == where_ref[1], 0, other) + (
                    lax.shift_right_logical(entry, 2) & 15
                )
                shift = ((i - entry) & 3) * 32
                moved = pltpu.roll(table[chunk], shift, 1)
                piece = jnp.where(block == i, moved, piece)
                level = jnp.where(block == i, damp_ref[4 * h + i, g], level)
            halves.append(piece * jnp.sqrt(1.0 / (1.0 + level.astype(F32))))
        return jnp.concatenate(halves, axis=1)

    groups = [pl.program_id(0) * WIDE + u for u in range(WIDE)]
    picked = each(pick, groups)
    drives = each(
        lambda p: jnp.sum(p[0:256] * p[256:257], axis=1, keepdims=True), picked
    )
    parts = each(lambda p: split(p[0:256]), picked)
    grams = each(
        lambda p: dot_nt(p[0], p[0]) + (dot_nt(p[0], p[1]) + dot_nt(p[1], p[0])), parts
    )
    grams = each(lambda g: g + jnp.where(diagonal, 255.0, 0.0), grams)
    inverses = each(
        lambda g: 1.0
        / jnp.max(jnp.sum(jnp.abs(g), axis=0, keepdims=True), axis=1, keepdims=True),
        grams,
    )
    current = each(lambda g, v: g * v, grams, inverses)
    roots = []
    for step in range(3):
        parts = each(split, current)
        second = each(square, parts)
        if step < 2:
            products = each(mul3, parts, each(split, second))
        if step != 1:
            mixed = each(lambda s, c: split(s - 4.5 * c), second, current)
            roots.append(
                each(
                    lambda m, s, c: 0.0625 * square(m)
                    + (0.421875 * s - 2.4375 * c + jnp.where(diagonal, 2.25, 0.0)),
                    mixed,
                    second,
                    current,
                )
            )
        if step < 2:
            current = each(
                lambda c, s, p: 2.25 * c - 1.5 * s + 0.25 * p, current, second, products
            )
    root = each(mul3, each(split, roots[0]), each(split, roots[1]))
    inner = each(lambda r, d: jnp.sum(r * d, axis=0, keepdims=True), root, drives)
    offsets = each(
        lambda r, n, v: jnp.sum(r * n, axis=1, keepdims=True) * v, root, inner, inverses
    )
    held = offset_ref[...]
    for u, (g, r, v, o) in enumerate(zip(groups, root, inverses, offsets)):
        root_ref[u] = jnp.sqrt(255.0 * v) * r
        held = jnp.where(lane == g, o, held)
    offset_ref[...] = held


def apply_kernel(where_ref, root_ref, offset_ref, *refs):
    pieces = refs[:MEM]
    out_ref, field, sems = refs[MEM:]
    me = where_ref[0]

    @pl.when(pl.program_id(0) == 0)
    def gather():
        copies = [
            pltpu.make_async_copy(
                pieces[s], field.at[pl.ds(pl.multiple_of((me ^ s) * 32, 32), 32), :], sems.at[s]
            )
            for s in range(MEM)
        ]
        for copy in copies:
            copy.start()
        for copy in copies:
            copy.wait()

    odd, high = lane_bits(256)
    lane = lax.broadcasted_iota(jnp.int32, (256, LANES), 1)
    groups = [pl.program_id(0) * 4 + g for g in range(4)]
    value = [field[:, pl.ds(pl.multiple_of(g * LANES, LANES), LANES)] for g in groups]
    centre = each(lambda x: jnp.sum(x, axis=0, keepdims=True) * (1.0 / 256.0), value)
    anomaly = each(lambda x, a: x - a, value, centre)
    offset = [
        jnp.sum(jnp.where(lane == g, offset_ref[...], 0.0), axis=1, keepdims=True) for g in groups
    ]
    base = each(
        lambda a, x, o: a + jnp.sum(x * o, axis=0, keepdims=True), centre, anomaly, offset
    )
    spread = each(mul3, [split(root_ref[u]) for u in range(4)], each(split, anomaly))
    layers = exchange_lanes(each(lambda b, x: b + x, base, spread), odd, high)
    for l in range(4):
        out_ref[:, l, :] = layers[l]


def find_mixing(where, nearby, damping, own, sib, far):
    return pl.pallas_call(
        mixing_kernel,
        out_shape=[
            jax.ShapeDtypeStruct((16, 256, 256), F32),
            jax.ShapeDtypeStruct((256, LANES), F32),
        ],
        grid=(16 // WIDE,),
        in_specs=[SMEM] * 3 + [ANYWHERE] * (2 + MEM),
        out_specs=[
            pl.BlockSpec((WIDE, 256, 256), lambda i: (i, 0, 0)),
            pl.BlockSpec((256, LANES), lambda i: (0, 0)),
        ],
        scratch_shapes=[
            pltpu.VMEM((256, 2176), F32),
            pltpu.VMEM((48, 264, LANES), F32),
            pltpu.SemaphoreType.DMA((MEM + 2,)),
        ],
        compiler_params=pltpu.CompilerParams(vmem_limit_bytes=30 << 20),
        cost_estimate=pl.CostEstimate(
            flops=16 * 30 * 2 * 256**3, bytes_accessed=12 << 20, transcendentals=0
        ),
        name="mixing",
    )(where, nearby, damping, own, sib, *far)


def apply_mixing(where, root, offset, pieces):
    return pl.pallas_call(
        apply_kernel,
        out_shape=jax.ShapeDtypeStruct((256, 4, 512), F32),
        grid=(4,),
        in_specs=[SMEM, pl.BlockSpec((4, 256, 256), lambda i: (i, 0, 0)), VMEM] + [ANYWHERE] * MEM,
        out_specs=pl.BlockSpec((256, 4, LANES), lambda i: (0, 0, i)),
        scratch_shapes=[pltpu.VMEM((256, 2048), F32), pltpu.SemaphoreType.DMA((MEM,))],
        compiler_params=pltpu.CompilerParams(vmem_limit_bytes=30 << 20),
        name="apply",
    )(where, root, offset, *pieces)


def send(x, flip):
    return lax.ppermute(x, "mem", [(i, i ^ flip) for i in range(MEM)])


def swap_cores(x):
    return lax.ppermute(x, "tile", [(i, i ^ 1) for i in range(32)])


def local(prior, measurement_matrix, readings, noise, nearby, damping):
    me = lax.axis_index("mem").astype(jnp.int32)
    tile = lax.axis_index("tile").astype(jnp.int32)
    where = jnp.stack([me, tile])
    measurement_map = jnp.swapaxes(measurement_matrix, 1, 2)
    *pieces, obs = local_obs(where, prior, measurement_map, readings, noise)
    hold = lax.optimization_barrier
    got = [pieces[0]] + [None] * 7
    own4, own1, own3 = send(obs, 4), send(obs, 1), send(obs, 3)
    far0 = lax.ppermute(
        obs,
        "tile",
        [(i, i + 1) for i in range(1, 31, 2)] + [(i + 1, i) for i in range(1, 31, 2)],
    )
    own5, own7, own2 = send(own4, 1), send(own4, 3), send(own3, 1)
    far4, far1, far3 = send(far0, 4), send(far0, 1), send(far0, 3)
    own6 = send(own5, 3)
    far5, far7 = send(far4, 1), send(far4, 3)
    far1, far3, own4 = hold((far1, far3, own4))
    table = own_table(where, (obs, own4, own1, own3, own5, own7, own2, own6))
    table, four, one = hold((table, pieces[4], pieces[1]))
    sibling = swap_cores(table)
    got[4] = send(four, 4)
    far2, far6 = send(far3, 1), send(far5, 3)
    far5, far7, *rest = hold((far5, far7, one, pieces[3]))
    got[1], got[3] = send(rest[0], 1), send(rest[1], 3)
    far2, sibling, got[4], *rest = hold((far2, sibling, got[4], pieces[2], *pieces[5:]))
    for s, x in zip((2, 5, 6, 7), rest):
        got[s] = send(x, s)
    far = (far0, far4, far1, far3, far5, far7, far2, far6)
    root, offset = find_mixing(where, nearby.T, damping.T, table, sibling, far)
    return apply_mixing(where, root, offset, got)


def solution(mesh):
    in_specs = (
        P("mem", None, "tile"),
        P(),
        P(("tile", "mem"), None),
        P(("tile", "mem"), None),
        P(("tile", "mem"), None),
        P(("tile", "mem"), None),
    )
    out_specs = P(None, None, ("tile", "mem"))
    return jax.shard_map(local, mesh=mesh, in_specs=in_specs, out_specs=out_specs, check_vma=False)
```

time: 127 us -> 112 us (0.88); the launches traced: 124 us -> 112 us
  local copies, waits for them, and re-layouts: 16.4 us -> 0.99 us
  waiting for transfers between devices: 45.2 us -> 33.9 us
  starting transfers between devices: 28.2 us -> 38.8 us
  Pallas kernels: 34.3 us -> 36.8 us
    unnamed x43 -> x24, local copies, waits for them, and re-layouts: 13.6 us -> 0.99 us
    ppermute x17 -> x21, starting transfers between devices: 24.3 us -> 32.1 us  [send(): return lax.ppermute(x, 'mem', [(i, i ^ flip) for i in range(MEM)])]
    ppermute x1, waiting for transfers between devices: 7.43 us -> 0.01 us  [local(): lax.ppermute(obs, 'tile', [(i, i + 1) for i in range(1, 31, 2)] + [(i + 1...]
    ppermute x17 -> x21, waiting for transfers between devices: 37.7 us -> 33.9 us  [send(): return lax.ppermute(x, 'mem', [(i, i ^ flip) for i in range(MEM)])]
    pallas_call x1, Pallas kernels: 3.75 us -> 6.26 us  [local_obs(): pl.pallas_call(obs_kernel, out_shape=[jax.ShapeDtypeStruct((members, 2048...]
    slice x4 -> x0, local copies, waits for them, and re-layouts: 2.45 us -> none  [the longest x2 2.41 us: local(): far2 = [send(far3[:32], 1), send(far1[32:], 3)]]
    ppermute x1, starting transfers between devices: 2.92 us -> 4.4 us  [local(): lax.ppermute(obs, 'tile', [(i, i + 1) for i in range(1, 31, 2)] + [(i + 1...]
    pallas_call x1, Pallas kernels: 25.2 us -> 23.9 us  [find_mixing(): pl.pallas_call(mixing_kernel, out_shape=[jax.ShapeDtypeStruct((16, 256, 2...]
  transfers between devices with their start and end apart: 23 -> 23, of which waited for: 12 -> 9; matrix products, arithmetic and copies ran while one was open for 2% -> 0% of each run, Pallas kernels for 20% -> 21%
where the time goes in v3:
time: 112 us
  starting transfers between devices  38.8 us (35%)
  Pallas kernels  36.8 us (33%)
  waiting for transfers between devices  33.9 us (30%)
    ppermute x21, waiting for transfers between devices, send(): return lax.ppermute(x, 'mem', [(i, i ^ flip) for i in range(MEM)])  33.9 us
    ppermute x21, starting transfers between devices, send(): return lax.ppermute(x, 'mem', [(i, i ^ flip) for i in range(MEM)])  32.1 us
    pallas_call x1, Pallas kernels, find_mixing(): pl.pallas_call(mixing_kernel, out_shape=[jax.ShapeDtypeStruct((16, 256, 2...  23.9 us
    pallas_call x1, Pallas kernels, local_obs(): pl.pallas_call(obs_kernel, out_shape=[jax.ShapeDtypeStruct((members, 2048...  6.26 us
    pallas_call x1, Pallas kernels, apply_mixing(): pl.pallas_call(apply_kernel, out_shape=jax.ShapeDtypeStruct((256, 4, 512)...  5.42 us
    ppermute x1, starting transfers between devices, local(): lax.ppermute(obs, 'tile', [(i, i + 1) for i in range(1, 31, 2)] + [(i + 1...  4.4 us
    ppermute x1, starting transfers between devices, swap_cores(): return lax.ppermute(x, 'tile', [(i, i ^ 1) for i in range(32)])  2.28 us
  transfers between devices with their start and end apart: 23, of which 9 were waited for; matrix products, arithmetic and copies ran while one was open for 0% of the time, Pallas kernels for 21%

profile of v3, /device:TPU:192, one launch (start us, length us, event | category | flops | bytes accessed | tf_op | source)
XLA Modules:
  0.0 111.5 jit_solution(5041118993805163241)
XLA Ops:
  0.7 6.3 %local_obs.1 = (f32[32,2048]{1,0:T(8,128)}, f32[32,2048]{1,0:T(8,128)}, f32[32,2048]{1,0:T(8,128)}, f32[32,2048]{1,0:T(8,128)}, f32[32,2048]{1,0:T(8,128)}, /*in...) custom-call(s32[2]{0:T(128)} %pad_add_fusion.where_ref.refs_0_, ...), custom_call_target="tpu_custom_call" | custom-call | tf_op jit(solution)/shard_map/local_obs/pallas_call | solution.py:113
  6.9 1.7 %collective-permute-start.3 = (f32[32,2176]{1,0:T(8,128)}, f32[32,2176]{1,0:T(8,128)S(1)}, u32[]{:S(2)}, u32[]{:S(2)}) collective-permute-start(f32[32,2176]{1,0:T(8,128)} %get-tuple-element.33.refs_0_), channel_id=1, source_target_pairs={{0,128},{32,160},{64,192},{96,224},{128,0},{160,32},{192,64},{224,... | collective-permute-start | bytes 835592 | tf_op jit(solution)/shard_map/ppermute | solution.py:369
  8.6 4.4 %collective-permute-start = (f32[32,2176]{1,0:T(8,128)}, f32[32,2176]{1,0:T(8,128)S(1)}, u32[]{:S(2)}, u32[]{:S(2)}) collective-permute-start(f32[32,2176]{1,0:T(8,128)} %get-tuple-element.33.refs_0_), channel_id=1, source_target_pairs={{1,2},{3,4},{5,6},{7,8},{9,10},{11,12},{13,14},{15,16},{17,18},{19... | collective-permute-start | bytes 835592 | tf_op jit(solution)/shard_map/ppermute | solution.py:385
  13.0 2.8 %collective-permute-start.5 = (f32[32,2176]{1,0:T(8,128)}, f32[32,2176]{1,0:T(8,128)S(1)}, u32[]{:S(2)}, u32[]{:S(2)}) collective-permute-start(f32[32,2176]{1,0:T(8,128)} %get-tuple-element.33.refs_0_), channel_id=1, source_target_pairs={{0,96},{32,64},{64,32},{96,0},{128,224},{160,192},{192,160},{224,1... | collective-permute-start | bytes 835592 | tf_op jit(solution)/shard_map/ppermute | solution.py:369
  15.9 3.6 %collective-permute-done.3.refs_1_ = f32[32,2176]{1,0:T(8,128)S(1)} collective-permute-done((f32[32,2176]{1,0:T(8,128)}, f32[32,2176]{1,0:T(8,128)S(1)}, u32[]{:S(2)}, u32[]{:S(2)}) %collective-permute-start.3) | collective-permute-done | bytes 278560 | tf_op jit(solution)/shard_map/ppermute | solution.py:369
  19.5 1.5 %collective-permute-start.6 = (f32[32,2176]{1,0:T(8,128)S(1)}, f32[32,2176]{1,0:T(8,128)S(1)}, u32[]{:S(2)}, u32[]{:S(2)}) collective-permute-start(f32[32,2176]{1,0:T(8,128)S(1)} %collective-permute-done.3.refs_1_), channel_id=1, source_target_pairs={{0,32},{32,0},{64,96},{96,64},{128,160},{160,128},{192,224},{224,1... | collective-permute-start | bytes 835592 | tf_op jit(solution)/shard_map/ppermute | solution.py:369
  21.0 2.1 %collective-permute-start.2 = (f32[32,2176]{1,0:T(8,128)S(1)}, f32[32,2176]{1,0:T(8,128)S(1)}, u32[]{:S(2)}, u32[]{:S(2)}) collective-permute-start(f32[32,2176]{1,0:T(8,128)S(1)} %collective-permute-done.refs_5_), channel_id=1, source_target_pairs={{0,96},{32,64},{64,32},{96,0},{128,224},{160,192},{192,160},{224,1... | collective-permute-start | bytes 835592 | tf_op jit(solution)/shard_map/ppermute | solution.py:369
  27.5 2.2 %collective-permute-done.2.refs_8_ = f32[32,2176]{1,0:T(8,128)S(1)} collective-permute-done((f32[32,2176]{1,0:T(8,128)S(1)}, f32[32,2176]{1,0:T(8,128)S(1)}, u32[]{:S(2)}, u32[]{:S(2)}) %collective-permute-start.2) | collective-permute-done | bytes 278560 | tf_op jit(solution)/shard_map/ppermute | solution.py:369
  29.7 1.5 %collective-permute-start.9 = (f32[32,2176]{1,0:T(8,128)S(1)}, f32[32,2176]{1,0:T(8,128)S(1)}, u32[]{:S(2)}, u32[]{:S(2)}) collective-permute-start(f32[32,2176]{1,0:T(8,128)S(1)} %collective-permute-done.6.refs_4_), channel_id=1, source_target_pairs={{0,96},{32,64},{64,32},{96,0},{128,224},{160,192},{192,160},{224,1... | collective-permute-start | bytes 835592 | tf_op jit(solution)/shard_map/ppermute | solution.py:369
  31.2 5.2 %collective-permute-done.1.refs_7_ = f32[32,2176]{1,0:T(8,128)S(1)} collective-permute-done((f32[32,2176]{1,0:T(8,128)S(1)}, f32[32,2176]{1,0:T(8,128)S(1)}, u32[]{:S(2)}, u32[]{:S(2)}) %collective-permute-start.1) | collective-permute-done | bytes 278560 | tf_op jit(solution)/shard_map/ppermute | solution.py:369
  36.4 6.0 %collective-permute-done.8.refs_6_ = f32[32,2176]{1,0:T(8,128)S(1)} collective-permute-done((f32[32,2176]{1,0:T(8,128)S(1)}, f32[32,2176]{1,0:T(8,128)S(1)}, u32[]{:S(2)}, u32[]{:S(2)}) %collective-permute-start.8) | collective-permute-done | bytes 278560 | tf_op jit(solution)/shard_map/ppermute | solution.py:369
  44.7 2.3 %collective-permute-start.11 = (f32[16,264,128]{2,1,0:T(8,128)S(1)}, f32[16,264,128]{2,1,0:T(8,128)S(1)}, u32[]{:S(2)}, u32[]{:S(2)}) collective-permute-start(f32[16,264,128]{2,1,0:T(8,128)S(1)} %own_table.1.refs_3_), channel_id=1, source_target_pairs={{0,1},{1,0},{2,3},{3,2},{4,5},{5,4},{6,7},{7,6},{8,9},{9,8},{10,11... | collective-permute-start | bytes 6488072 | tf_op jit(solution)/shard_map/ppermute | solution.py:373
  48.2 7.4 %collective-permute-done.13.refs_6_ = f32[32,2176]{1,0:T(8,128)S(1)} collective-permute-done((f32[32,2176]{1,0:T(8,128)S(1)}, f32[32,2176]{1,0:T(8,128)S(1)}, u32[]{:S(2)}, u32[]{:S(2)}) %collective-permute-start.13) | collective-permute-done | bytes 278560 | tf_op jit(solution)/shard_map/ppermute | solution.py:369
  56.3 2.2 %collective-permute-start.15 = (f32[32,2176]{1,0:T(8,128)S(1)}, f32[32,2176]{1,0:T(8,128)S(1)}, u32[]{:S(2)}, u32[]{:S(2)}) collective-permute-start(f32[32,2176]{1,0:T(8,128)S(1)} %collective-permute-done.13.refs_6_), channel_id=1, source_target_pairs={{0,96},{32,64},{64,32},{96,0},{128,224},{160,192},{192,160},{224,1... | collective-permute-start | bytes 835592 | tf_op jit(solution)/shard_map/ppermute | solution.py:369
  59.1 6.1 %collective-permute-done.14.refs_9_ = f32[32,2176]{1,0:T(8,128)S(1)} collective-permute-done((f32[32,2176]{1,0:T(8,128)S(1)}, f32[32,2176]{1,0:T(8,128)S(1)}, u32[]{:S(2)}, u32[]{:S(2)}) %collective-permute-start.14) | collective-permute-done | bytes 278560 | tf_op jit(solution)/shard_map/ppermute | solution.py:369
  65.2 2.0 %collective-permute-start.16 = (f32[32,2176]{1,0:T(8,128)S(1)}, f32[32,2176]{1,0:T(8,128)S(1)}, u32[]{:S(2)}, u32[]{:S(2)}) collective-permute-start(f32[32,2176]{1,0:T(8,128)S(1)} %collective-permute-done.14.refs_9_), channel_id=1, source_target_pairs={{0,96},{32,64},{64,32},{96,0},{128,224},{160,192},{192,160},{224,1... | collective-permute-start | bytes 835592 | tf_op jit(solution)/shard_map/ppermute | solution.py:369
  67.3 1.7 %collective-permute-start.12 = (f32[32,2048]{1,0:T(8,128)S(1)}, f32[32,2048]{1,0:T(8,128)S(1)}, u32[]{:S(2)}, u32[]{:S(2)}) collective-permute-start(f32[32,2048]{1,0:T(8,128)S(1)} %copy-done.11), channel_id=1, source_target_pairs={{0,128},{32,160},{64,192},{96,224},{128,0},{160,32},{192,64},{224,... | collective-permute-start | bytes 786440 | tf_op jit(solution)/shard_map/ppermute | solution.py:369
  70.4 2.9 %collective-permute-start.19 = (f32[32,2048]{1,0:T(8,128)S(1)}, f32[32,2048]{1,0:T(8,128)S(1)}, u32[]{:S(2)}, u32[]{:S(2)}) collective-permute-start(f32[32,2048]{1,0:T(8,128)S(1)} %copy-done.9), channel_id=1, source_target_pairs={{0,96},{32,64},{64,32},{96,0},{128,224},{160,192},{192,160},{224,1... | collective-permute-start | bytes 786440 | tf_op jit(solution)/shard_map/ppermute | solution.py:369
  74.3 2.1 %collective-permute-start.20 = (f32[32,2048]{1,0:T(8,128)S(1)}, f32[32,2048]{1,0:T(8,128)S(1)}, u32[]{:S(2)}, u32[]{:S(2)}) collective-permute-start(f32[32,2048]{1,0:T(8,128)S(1)} %copy-done.7), channel_id=1, source_target_pairs={{0,160},{32,128},{64,224},{96,192},{128,32},{160,0},{192,96},{224,... | collective-permute-start | bytes 786440 | tf_op jit(solution)/shard_map/ppermute | solution.py:369
  76.4 1.8 %collective-permute-done.17.refs_1_ = f32[32,2048]{1,0:T(8,128)S(1)} collective-permute-done((f32[32,2048]{1,0:T(8,128)S(1)}, f32[32,2048]{1,0:T(8,128)S(1)}, u32[]{:S(2)}, u32[]{:S(2)}) %collective-permute-start.17) | collective-permute-done | bytes 262176 | tf_op jit(solution)/shard_map/ppermute | solution.py:369
  78.2 2.1 %collective-permute-start.21 = (f32[32,2048]{1,0:T(8,128)S(1)}, f32[32,2048]{1,0:T(8,128)S(1)}, u32[]{:S(2)}, u32[]{:S(2)}) collective-permute-start(f32[32,2048]{1,0:T(8,128)S(1)} %copy-done.6), channel_id=1, source_target_pairs={{0,192},{32,224},{64,128},{96,160},{128,64},{160,96},{192,0},{224,... | collective-permute-start | bytes 786440 | tf_op jit(solution)/shard_map/ppermute | solution.py:369
  80.3 1.7 %collective-permute-start.22 = (f32[32,2048]{1,0:T(8,128)S(1)}, f32[32,2048]{1,0:T(8,128)S(1)}, u32[]{:S(2)}, u32[]{:S(2)}) collective-permute-start(f32[32,2048]{1,0:T(8,128)S(1)} %copy-done.5), channel_id=1, source_target_pairs={{0,224},{32,192},{64,160},{96,128},{128,96},{160,64},{192,32},{224... | collective-permute-start | bytes 786440 | tf_op jit(solution)/shard_map/ppermute | solution.py:369
  82.0 23.9 %mixing.1 = (f32[16,256,256]{2,1,0:T(8,128)S(1)}, f32[256,128]{1,0:T(8,128)S(1)}) custom-call(s32[2]{0:T(128)S(1)} %copy-done.2, s32[8,16]{1,0:T(8,128)S(1)} %bitcast.5, s32[8,16]{1,0:T(8,128)S(1)} %bitcast.6, f32[16,264,128]{2,1,0:T(8,128)S(1)} %own_table.1.refs_3_, f32[16,264,128]{2,1,0:T(8,128)S(1)} %collective-permute-done.11.refs_4_, ...), custom_call_target="tpu_custom_call" | custom-call | flops 16106127360 | bytes 12582912 | tf_op jit(solution)/shard_map/mixing/pallas_call | solution.py:330
  105.9 5.4 %apply.1 = f32[256,4,512]{2,1,0:T(4,128)} custom-call(s32[2]{0:T(128)S(1)} %copy-done.2, f32[16,256,256]{2,1,0:T(8,128)S(1)} %get-tuple-element.51.root_ref, f32[256,128]{1,0:T(8,128)S(1)} %get-tuple-element.52.offset_ref, f32[32,2048]{1,0:T(8,128)S(1)} %copy-done.1, f32[32,2048]{1,0:T(8,128)S(1)} %collective-permute-done.17.refs_1_, ...), custom_call_target="tpu_custom_call" | custom-call | tf_op jit(solution)/shard_map/apply/pallas_call | solution.py:356
  (51 shorter events, 12.3 us)
Async XLA Ops:
  0.7 81.3 %copy-start.4 = (s32[16,8]{0,1:T(8,128)S(1)}, s32[16,8]{0,1:T(8,128)}, u32[]{:S(2)}) copy-start(s32[16,8]{0,1:T(8,128)} %param.11) | copy-start | bytes 1540
  6.9 12.5 %collective-permute-start.3 = (f32[32,2176]{1,0:T(8,128)}, f32[32,2176]{1,0:T(8,128)S(1)}, u32[]{:S(2)}, u32[]{:S(2)}) collective-permute-start(f32[32,2176]{1,0:T(8,128)} %get-tuple-element.33.refs_0_), channel_id=1, source_target_pairs={{0,128},{32,160},{64,192},{96,224},{128,0},{160,32},{192,64},{224,... | collective-permute-start | bytes 835592 | tf_op jit(solution)/shard_map/ppermute | solution.py:369
  8.6 12.4 %collective-permute-start = (f32[32,2176]{1,0:T(8,128)}, f32[32,2176]{1,0:T(8,128)S(1)}, u32[]{:S(2)}, u32[]{:S(2)}) collective-permute-start(f32[32,2176]{1,0:T(8,128)} %get-tuple-element.33.refs_0_), channel_id=1, source_target_pairs={{1,2},{3,4},{5,6},{7,8},{9,10},{11,12},{13,14},{15,16},{17,18},{19... | collective-permute-start | bytes 835592 | tf_op jit(solution)/shard_map/ppermute | solution.py:385
  13.0 12.1 %collective-permute-start.5 = (f32[32,2176]{1,0:T(8,128)}, f32[32,2176]{1,0:T(8,128)S(1)}, u32[]{:S(2)}, u32[]{:S(2)}) collective-permute-start(f32[32,2176]{1,0:T(8,128)} %get-tuple-element.33.refs_0_), channel_id=1, source_target_pairs={{0,96},{32,64},{64,32},{96,0},{128,224},{160,192},{192,160},{224,1... | collective-permute-start | bytes 835592 | tf_op jit(solution)/shard_map/ppermute | solution.py:369
  19.5 6.9 %collective-permute-start.6 = (f32[32,2176]{1,0:T(8,128)S(1)}, f32[32,2176]{1,0:T(8,128)S(1)}, u32[]{:S(2)}, u32[]{:S(2)}) collective-permute-start(f32[32,2176]{1,0:T(8,128)S(1)} %collective-permute-done.3.refs_1_), channel_id=1, source_target_pairs={{0,32},{32,0},{64,96},{96,64},{128,160},{160,128},{192,224},{224,1... | collective-permute-start | bytes 835592 | tf_op jit(solution)/shard_map/ppermute | solution.py:369
  21.0 8.7 %collective-permute-start.2 = (f32[32,2176]{1,0:T(8,128)S(1)}, f32[32,2176]{1,0:T(8,128)S(1)}, u32[]{:S(2)}, u32[]{:S(2)}) collective-permute-start(f32[32,2176]{1,0:T(8,128)S(1)} %collective-permute-done.refs_5_), channel_id=1, source_target_pairs={{0,96},{32,64},{64,32},{96,0},{128,224},{160,192},{192,160},{224,1... | collective-permute-start | bytes 835592 | tf_op jit(solution)/shard_map/ppermute | solution.py:369
  23.1 13.3 %collective-permute-start.4 = (f32[32,2176]{1,0:T(8,128)}, f32[32,2176]{1,0:T(8,128)S(1)}, u32[]{:S(2)}, u32[]{:S(2)}) collective-permute-start(f32[32,2176]{1,0:T(8,128)} %get-tuple-element.33.refs_0_), channel_id=1, source_target_pairs={{0,32},{32,0},{64,96},{96,64},{128,160},{160,128},{192,224},{224,1... | collective-permute-start | bytes 835592 | tf_op jit(solution)/shard_map/ppermute | solution.py:369
  23.7 12.8 %collective-permute-start.1 = (f32[32,2176]{1,0:T(8,128)S(1)}, f32[32,2176]{1,0:T(8,128)S(1)}, u32[]{:S(2)}, u32[]{:S(2)}) collective-permute-start(f32[32,2176]{1,0:T(8,128)S(1)} %collective-permute-done.refs_5_), channel_id=1, source_target_pairs={{0,32},{32,0},{64,96},{96,64},{128,160},{160,128},{192,224},{224,1... | collective-permute-start | bytes 835592 | tf_op jit(solution)/shard_map/ppermute | solution.py:369
  25.1 17.3 %collective-permute-start.7 = (f32[32,2176]{1,0:T(8,128)S(1)}, f32[32,2176]{1,0:T(8,128)S(1)}, u32[]{:S(2)}, u32[]{:S(2)}) collective-permute-start(f32[32,2176]{1,0:T(8,128)S(1)} %collective-permute-done.3.refs_1_), channel_id=1, source_target_pairs={{0,96},{32,64},{64,32},{96,0},{128,224},{160,192},{192,160},{224,1... | collective-permute-start | bytes 835592 | tf_op jit(solution)/shard_map/ppermute | solution.py:369
  26.4 16.0 %collective-permute-start.8 = (f32[32,2176]{1,0:T(8,128)S(1)}, f32[32,2176]{1,0:T(8,128)S(1)}, u32[]{:S(2)}, u32[]{:S(2)}) collective-permute-start(f32[32,2176]{1,0:T(8,128)S(1)} %collective-permute-done.5.refs_3_), channel_id=1, source_target_pairs={{0,32},{32,0},{64,96},{96,64},{128,160},{160,128},{192,224},{224,1... | collective-permute-start | bytes 835592 | tf_op jit(solution)/shard_map/ppermute | solution.py:369
  29.7 12.7 %collective-permute-start.9 = (f32[32,2176]{1,0:T(8,128)S(1)}, f32[32,2176]{1,0:T(8,128)S(1)}, u32[]{:S(2)}, u32[]{:S(2)}) collective-permute-start(f32[32,2176]{1,0:T(8,128)S(1)} %collective-permute-done.6.refs_4_), channel_id=1, source_target_pairs={{0,96},{32,64},{64,32},{96,0},{128,224},{160,192},{192,160},{224,1... | collective-permute-start | bytes 835592 | tf_op jit(solution)/shard_map/ppermute | solution.py:369
  44.7 29.0 %collective-permute-start.11 = (f32[16,264,128]{2,1,0:T(8,128)S(1)}, f32[16,264,128]{2,1,0:T(8,128)S(1)}, u32[]{:S(2)}, u32[]{:S(2)}) collective-permute-start(f32[16,264,128]{2,1,0:T(8,128)S(1)} %own_table.1.refs_3_), channel_id=1, source_target_pairs={{0,1},{1,0},{2,3},{3,2},{4,5},{5,4},{6,7},{7,6},{8,9},{9,8},{10,11... | collective-permute-start | bytes 6488072 | tf_op jit(solution)/shard_map/ppermute | solution.py:373
  47.0 8.7 %collective-permute-start.13 = (f32[32,2176]{1,0:T(8,128)S(1)}, f32[32,2176]{1,0:T(8,128)S(1)}, u32[]{:S(2)}, u32[]{:S(2)}) collective-permute-start(f32[32,2176]{1,0:T(8,128)S(1)} %collective-permute-done.refs_5_), channel_id=1, source_target_pairs={{0,128},{32,160},{64,192},{96,224},{128,0},{160,32},{192,64},{224,... | collective-permute-start | bytes 835592 | tf_op jit(solution)/shard_map/ppermute | solution.py:369
  55.6 9.6 %collective-permute-start.14 = (f32[32,2176]{1,0:T(8,128)S(1)}, f32[32,2176]{1,0:T(8,128)S(1)}, u32[]{:S(2)}, u32[]{:S(2)}) collective-permute-start(f32[32,2176]{1,0:T(8,128)S(1)} %collective-permute-done.13.refs_6_), channel_id=1, source_target_pairs={{0,32},{32,0},{64,96},{96,64},{128,160},{160,128},{192,224},{224,1... | collective-permute-start | bytes 835592 | tf_op jit(solution)/shard_map/ppermute | solution.py:369
  56.3 12.7 %collective-permute-start.15 = (f32[32,2176]{1,0:T(8,128)S(1)}, f32[32,2176]{1,0:T(8,128)S(1)}, u32[]{:S(2)}, u32[]{:S(2)}) collective-permute-start(f32[32,2176]{1,0:T(8,128)S(1)} %collective-permute-done.13.refs_6_), channel_id=1, source_target_pairs={{0,96},{32,64},{64,32},{96,0},{128,224},{160,192},{192,160},{224,1... | collective-permute-start | bytes 835592 | tf_op jit(solution)/shard_map/ppermute | solution.py:369
  58.5 11.9 %collective-permute-start.10 = (f32[32,2176]{1,0:T(8,128)S(1)}, f32[32,2176]{1,0:T(8,128)S(1)}, u32[]{:S(2)}, u32[]{:S(2)}) collective-permute-start(f32[32,2176]{1,0:T(8,128)S(1)} %collective-permute-done.2.refs_8_), channel_id=1, source_target_pairs={{0,32},{32,0},{64,96},{96,64},{128,160},{160,128},{192,224},{224,1... | collective-permute-start | bytes 835592 | tf_op jit(solution)/shard_map/ppermute | solution.py:369
  65.2 15.1 %collective-permute-start.16 = (f32[32,2176]{1,0:T(8,128)S(1)}, f32[32,2176]{1,0:T(8,128)S(1)}, u32[]{:S(2)}, u32[]{:S(2)}) collective-permute-start(f32[32,2176]{1,0:T(8,128)S(1)} %collective-permute-done.14.refs_9_), channel_id=1, source_target_pairs={{0,96},{32,64},{64,32},{96,0},{128,224},{160,192},{192,160},{224,1... | collective-permute-start | bytes 835592 | tf_op jit(solution)/shard_map/ppermute | solution.py:369
  67.3 6.4 %collective-permute-start.12 = (f32[32,2048]{1,0:T(8,128)S(1)}, f32[32,2048]{1,0:T(8,128)S(1)}, u32[]{:S(2)}, u32[]{:S(2)}) collective-permute-start(f32[32,2048]{1,0:T(8,128)S(1)} %copy-done.11), channel_id=1, source_target_pairs={{0,128},{32,160},{64,192},{96,224},{128,0},{160,32},{192,64},{224,... | collective-permute-start | bytes 786440 | tf_op jit(solution)/shard_map/ppermute | solution.py:369
  69.0 9.2 %collective-permute-start.17 = (f32[32,2048]{1,0:T(8,128)S(1)}, f32[32,2048]{1,0:T(8,128)S(1)}, u32[]{:S(2)}, u32[]{:S(2)}) collective-permute-start(f32[32,2048]{1,0:T(8,128)S(1)} %copy-done.10), channel_id=1, source_target_pairs={{0,32},{32,0},{64,96},{96,64},{128,160},{160,128},{192,224},{224,1... | collective-permute-start | bytes 786440 | tf_op jit(solution)/shard_map/ppermute | solution.py:369
  70.4 35.5 %collective-permute-start.19 = (f32[32,2048]{1,0:T(8,128)S(1)}, f32[32,2048]{1,0:T(8,128)S(1)}, u32[]{:S(2)}, u32[]{:S(2)}) collective-permute-start(f32[32,2048]{1,0:T(8,128)S(1)} %copy-done.9), channel_id=1, source_target_pairs={{0,96},{32,64},{64,32},{96,0},{128,224},{160,192},{192,160},{224,1... | collective-permute-start | bytes 786440 | tf_op jit(solution)/shard_map/ppermute | solution.py:369
  73.7 32.2 %collective-permute-start.18 = (f32[32,2048]{1,0:T(8,128)S(1)}, f32[32,2048]{1,0:T(8,128)S(1)}, u32[]{:S(2)}, u32[]{:S(2)}) collective-permute-start(f32[32,2048]{1,0:T(8,128)S(1)} %copy-done.8), channel_id=1, source_target_pairs={{0,64},{32,96},{64,0},{96,32},{128,192},{160,224},{192,128},{224,1... | collective-permute-start | bytes 786440 | tf_op jit(solution)/shard_map/ppermute | solution.py:369
  74.3 31.6 %collective-permute-start.20 = (f32[32,2048]{1,0:T(8,128)S(1)}, f32[32,2048]{1,0:T(8,128)S(1)}, u32[]{:S(2)}, u32[]{:S(2)}) collective-permute-start(f32[32,2048]{1,0:T(8,128)S(1)} %copy-done.7), channel_id=1, source_target_pairs={{0,160},{32,128},{64,224},{96,192},{128,32},{160,0},{192,96},{224,... | collective-permute-start | bytes 786440 | tf_op jit(solution)/shard_map/ppermute | solution.py:369
  78.2 27.7 %collective-permute-start.21 = (f32[32,2048]{1,0:T(8,128)S(1)}, f32[32,2048]{1,0:T(8,128)S(1)}, u32[]{:S(2)}, u32[]{:S(2)}) collective-permute-start(f32[32,2048]{1,0:T(8,128)S(1)} %copy-done.6), channel_id=1, source_target_pairs={{0,192},{32,224},{64,128},{96,160},{128,64},{160,96},{192,0},{224,... | collective-permute-start | bytes 786440 | tf_op jit(solution)/shard_map/ppermute | solution.py:369
  80.3 25.6 %collective-permute-start.22 = (f32[32,2048]{1,0:T(8,128)S(1)}, f32[32,2048]{1,0:T(8,128)S(1)}, u32[]{:S(2)}, u32[]{:S(2)}) collective-permute-start(f32[32,2048]{1,0:T(8,128)S(1)} %copy-done.5), channel_id=1, source_target_pairs={{0,224},{32,192},{64,160},{96,128},{128,96},{160,64},{192,32},{224... | collective-permute-start | bytes 786440 | tf_op jit(solution)/shard_map/ppermute | solution.py:369
  (11 other events, 357.4 us)

commit v4 on v3

--- a/solution.py
+++ b/solution.py
@@ -390,8 +390,8 @@
     own5, own7, own2 = send(own4, 1), send(own4, 3), send(own3, 1)
     far4, far1, far3 = send(far0, 4), send(far0, 1), send(far0, 3)
     own6 = send(own5, 3)
+    far1, far3, far4, own4 = hold((far1, far3, far4, own4))
     far5, far7 = send(far4, 1), send(far4, 3)
-    far1, far3, own4 = hold((far1, far3, own4))
     table = own_table(where, (obs, own4, own1, own3, own5, own7, own2, own6))
     table, four, one = hold((table, pieces[4], pieces[1]))
     sibling = swap_cores(table)

time: 112 us -> 103 us (0.920)
  waiting for transfers between devices: 33.9 us -> 29.5 us
  starting transfers between devices: 38.8 us -> 34.7 us
    ppermute x21, waiting for transfers between devices: 33.9 us -> 29.5 us  [send(): return lax.ppermute(x, 'mem', [(i, i ^ flip) for i in range(MEM)])]
    ppermute x21, starting transfers between devices: 32.1 us -> 28.4 us  [send(): return lax.ppermute(x, 'mem', [(i, i ^ flip) for i in range(MEM)])]
  transfers between devices with their start and end apart: 23 -> 23, of which waited for: 9 -> 8; matrix products, arithmetic and copies ran while one was open for 0% -> 0% of each run, Pallas kernels for 21% -> 23%
where the time goes in v4:
time: 103 us
  Pallas kernels  36.8 us (36%)
  starting transfers between devices  34.7 us (34%)
  waiting for transfers between devices  29.5 us (29%)
    ppermute x21, waiting for transfers between devices, send(): return lax.ppermute(x, 'mem', [(i, i ^ flip) for i in range(MEM)])  29.5 us
    ppermute x21, starting transfers between devices, send(): return lax.ppermute(x, 'mem', [(i, i ^ flip) for i in range(MEM)])  28.4 us
    pallas_call x1, Pallas kernels, find_mixing(): pl.pallas_call(mixing_kernel, out_shape=[jax.ShapeDtypeStruct((16, 256, 2...  23.9 us
    pallas_call x1, Pallas kernels, local_obs(): pl.pallas_call(obs_kernel, out_shape=[jax.ShapeDtypeStruct((members, 2048...  6.26 us
    pallas_call x1, Pallas kernels, apply_mixing(): pl.pallas_call(apply_kernel, out_shape=jax.ShapeDtypeStruct((256, 4, 512)...  5.42 us
    ppermute x1, starting transfers between devices, local(): lax.ppermute(obs, 'tile', [(i, i + 1) for i in range(1, 31, 2)] + [(i + 1...  4.4 us
  transfers between devices with their start and end apart: 23, of which 8 were waited for; matrix products, arithmetic and copies ran while one was open for 0% of the time, Pallas kernels for 23%

profile of v4, /device:TPU:192, one launch (start us, length us, event | category | flops | bytes accessed | tf_op | source)
XLA Modules:
  0.0 103.0 jit_solution(16601692695943506323)
XLA Ops:
  0.7 6.3 %local_obs.1 = (f32[32,2048]{1,0:T(8,128)}, f32[32,2048]{1,0:T(8,128)}, f32[32,2048]{1,0:T(8,128)}, f32[32,2048]{1,0:T(8,128)}, f32[32,2048]{1,0:T(8,128)}, /*in...) custom-call(s32[2]{0:T(128)} %pad_add_fusion.where_ref.refs_0_, ...), custom_call_target="tpu_custom_call" | custom-call | tf_op jit(solution)/shard_map/local_obs/pallas_call | solution.py:113
  6.9 1.7 %collective-permute-start.4 = (f32[32,2176]{1,0:T(8,128)}, f32[32,2176]{1,0:T(8,128)S(1)}, u32[]{:S(2)}, u32[]{:S(2)}) collective-permute-start(f32[32,2176]{1,0:T(8,128)} %get-tuple-element.34.refs_0_), channel_id=1, source_target_pairs={{0,128},{32,160},{64,192},{96,224},{128,0},{160,32},{192,64},{224,... | collective-permute-start | bytes 835592 | tf_op jit(solution)/shard_map/ppermute | solution.py:369
  8.6 4.4 %collective-permute-start = (f32[32,2176]{1,0:T(8,128)}, f32[32,2176]{1,0:T(8,128)S(1)}, u32[]{:S(2)}, u32[]{:S(2)}) collective-permute-start(f32[32,2176]{1,0:T(8,128)} %get-tuple-element.34.refs_0_), channel_id=1, source_target_pairs={{1,2},{3,4},{5,6},{7,8},{9,10},{11,12},{13,14},{15,16},{17,18},{19... | collective-permute-start | bytes 835592 | tf_op jit(solution)/shard_map/ppermute | solution.py:385
  13.0 2.8 %collective-permute-start.6 = (f32[32,2176]{1,0:T(8,128)}, f32[32,2176]{1,0:T(8,128)S(1)}, u32[]{:S(2)}, u32[]{:S(2)}) collective-permute-start(f32[32,2176]{1,0:T(8,128)} %get-tuple-element.34.refs_0_), channel_id=1, source_target_pairs={{0,96},{32,64},{64,32},{96,0},{128,224},{160,192},{192,160},{224,1... | collective-permute-start | bytes 835592 | tf_op jit(solution)/shard_map/ppermute | solution.py:369
  15.9 3.6 %collective-permute-done.4.refs_1_ = f32[32,2176]{1,0:T(8,128)S(1)} collective-permute-done((f32[32,2176]{1,0:T(8,128)}, f32[32,2176]{1,0:T(8,128)S(1)}, u32[]{:S(2)}, u32[]{:S(2)}) %collective-permute-start.4) | collective-permute-done | bytes 278560 | tf_op jit(solution)/shard_map/ppermute | solution.py:369
  19.5 1.5 %collective-permute-start.7 = (f32[32,2176]{1,0:T(8,128)S(1)}, f32[32,2176]{1,0:T(8,128)S(1)}, u32[]{:S(2)}, u32[]{:S(2)}) collective-permute-start(f32[32,2176]{1,0:T(8,128)S(1)} %collective-permute-done.4.refs_1_), channel_id=1, source_target_pairs={{0,32},{32,0},{64,96},{96,64},{128,160},{160,128},{192,224},{224,1... | collective-permute-start | bytes 835592 | tf_op jit(solution)/shard_map/ppermute | solution.py:369
  21.0 1.3 %collective-permute-start.3 = (f32[32,2176]{1,0:T(8,128)S(1)}, f32[32,2176]{1,0:T(8,128)S(1)}, u32[]{:S(2)}, u32[]{:S(2)}) collective-permute-start(f32[32,2176]{1,0:T(8,128)S(1)} %collective-permute-done.refs_5_), channel_id=1, source_target_pairs={{0,128},{32,160},{64,192},{96,224},{128,0},{160,32},{192,64},{224,... | collective-permute-start | bytes 835592 | tf_op jit(solution)/shard_map/ppermute | solution.py:369
  22.3 2.1 %collective-permute-start.2 = (f32[32,2176]{1,0:T(8,128)S(1)}, f32[32,2176]{1,0:T(8,128)S(1)}, u32[]{:S(2)}, u32[]{:S(2)}) collective-permute-start(f32[32,2176]{1,0:T(8,128)S(1)} %collective-permute-done.refs_5_), channel_id=1, source_target_pairs={{0,96},{32,64},{64,32},{96,0},{128,224},{160,192},{192,160},{224,1... | collective-permute-start | bytes 835592 | tf_op jit(solution)/shard_map/ppermute | solution.py:369
  24.9 1.4 %collective-permute-start.1 = (f32[32,2176]{1,0:T(8,128)S(1)}, f32[32,2176]{1,0:T(8,128)S(1)}, u32[]{:S(2)}, u32[]{:S(2)}) collective-permute-start(f32[32,2176]{1,0:T(8,128)S(1)} %collective-permute-done.refs_5_), channel_id=1, source_target_pairs={{0,32},{32,0},{64,96},{96,64},{128,160},{160,128},{192,224},{224,1... | collective-permute-start | bytes 835592 | tf_op jit(solution)/shard_map/ppermute | solution.py:369
  26.4 2.4 %collective-permute-start.8 = (f32[32,2176]{1,0:T(8,128)S(1)}, f32[32,2176]{1,0:T(8,128)S(1)}, u32[]{:S(2)}, u32[]{:S(2)}) collective-permute-start(f32[32,2176]{1,0:T(8,128)S(1)} %collective-permute-done.4.refs_1_), channel_id=1, source_target_pairs={{0,96},{32,64},{64,32},{96,0},{128,224},{160,192},{192,160},{224,1... | collective-permute-start | bytes 835592 | tf_op jit(solution)/shard_map/ppermute | solution.py:369
  29.0 2.6 %collective-permute-done.2.refs_8_ = f32[32,2176]{1,0:T(8,128)S(1)} collective-permute-done((f32[32,2176]{1,0:T(8,128)S(1)}, f32[32,2176]{1,0:T(8,128)S(1)}, u32[]{:S(2)}, u32[]{:S(2)}) %collective-permute-start.2) | collective-permute-done | bytes 278560 | tf_op jit(solution)/shard_map/ppermute | solution.py:369
  31.7 1.2 %collective-permute-start.10 = (f32[32,2176]{1,0:T(8,128)S(1)}, f32[32,2176]{1,0:T(8,128)S(1)}, u32[]{:S(2)}, u32[]{:S(2)}) collective-permute-start(f32[32,2176]{1,0:T(8,128)S(1)} %collective-permute-done.7.refs_4_), channel_id=1, source_target_pairs={{0,96},{32,64},{64,32},{96,0},{128,224},{160,192},{192,160},{224,1... | collective-permute-start | bytes 835592 | tf_op jit(solution)/shard_map/ppermute | solution.py:369
  32.9 5.2 %collective-permute-done.1.refs_7_ = f32[32,2176]{1,0:T(8,128)S(1)} collective-permute-done((f32[32,2176]{1,0:T(8,128)S(1)}, f32[32,2176]{1,0:T(8,128)S(1)}, u32[]{:S(2)}, u32[]{:S(2)}) %collective-permute-start.1) | collective-permute-done | bytes 278560 | tf_op jit(solution)/shard_map/ppermute | solution.py:369
  38.1 6.0 %collective-permute-done.9.refs_6_ = f32[32,2176]{1,0:T(8,128)S(1)} collective-permute-done((f32[32,2176]{1,0:T(8,128)S(1)}, f32[32,2176]{1,0:T(8,128)S(1)}, u32[]{:S(2)}, u32[]{:S(2)}) %collective-permute-start.9) | collective-permute-done | bytes 278560 | tf_op jit(solution)/shard_map/ppermute | solution.py:369
  45.1 1.3 %own_table.1.refs_3_ = f32[16,264,128]{2,1,0:T(8,128)S(1)} custom-call(s32[2]{0:T(128)S(1)} %copy-done.2, f32[32,2176]{1,0:T(8,128)S(1)} %copy-done, f32[32,2176]{1,0:T(8,128)S(1)} %collective-permute-done.4.refs_1_, f32[32,2176]{1,0:T(8,128)S(1)} %collective-permute-done.5.refs_2_, f32[32,2176]{1,0:T(8,128)S(1)} %collective-permute-done.6.refs_3_, ...), custom_call_target="tpu_custom_call" | custom-call | flops 2097152 | bytes 6291456 | tf_op jit(solution)/shard_map/own_table/pallas_call | solution.py:182
  46.4 1.8 %collective-permute-start.12 = (f32[16,264,128]{2,1,0:T(8,128)S(1)}, f32[16,264,128]{2,1,0:T(8,128)S(1)}, u32[]{:S(2)}, u32[]{:S(2)}) collective-permute-start(f32[16,264,128]{2,1,0:T(8,128)S(1)} %own_table.1.refs_3_), channel_id=1, source_target_pairs={{0,1},{1,0},{2,3},{3,2},{4,5},{5,4},{6,7},{7,6},{8,9},{9,8},{10,11... | collective-permute-start | bytes 6488072 | tf_op jit(solution)/shard_map/ppermute | solution.py:373
  50.8 6.9 %collective-permute-done.14.refs_9_ = f32[32,2176]{1,0:T(8,128)S(1)} collective-permute-done((f32[32,2176]{1,0:T(8,128)S(1)}, f32[32,2176]{1,0:T(8,128)S(1)}, u32[]{:S(2)}, u32[]{:S(2)}) %collective-permute-start.14) | collective-permute-done | bytes 278560 | tf_op jit(solution)/shard_map/ppermute | solution.py:369
  59.9 3.8 %collective-permute-done.11.refs_11_ = f32[32,2176]{1,0:T(8,128)S(1)} collective-permute-done((f32[32,2176]{1,0:T(8,128)S(1)}, f32[32,2176]{1,0:T(8,128)S(1)}, u32[]{:S(2)}, u32[]{:S(2)}) %collective-permute-start.11) | collective-permute-done | bytes 278560 | tf_op jit(solution)/shard_map/ppermute | solution.py:369
  65.3 1.5 %collective-permute-start.18 = (f32[32,2048]{1,0:T(8,128)S(1)}, f32[32,2048]{1,0:T(8,128)S(1)}, u32[]{:S(2)}, u32[]{:S(2)}) collective-permute-start(f32[32,2048]{1,0:T(8,128)S(1)} %copy-done.8), channel_id=1, source_target_pairs={{0,64},{32,96},{64,0},{96,32},{128,192},{160,224},{192,128},{224,1... | collective-permute-start | bytes 786440 | tf_op jit(solution)/shard_map/ppermute | solution.py:369
  66.8 1.6 %collective-permute-start.20 = (f32[32,2048]{1,0:T(8,128)S(1)}, f32[32,2048]{1,0:T(8,128)S(1)}, u32[]{:S(2)}, u32[]{:S(2)}) collective-permute-start(f32[32,2048]{1,0:T(8,128)S(1)} %copy-done.7), channel_id=1, source_target_pairs={{0,160},{32,128},{64,224},{96,192},{128,32},{160,0},{192,96},{224,... | collective-permute-start | bytes 786440 | tf_op jit(solution)/shard_map/ppermute | solution.py:369
  69.3 1.8 %collective-permute-start.21 = (f32[32,2048]{1,0:T(8,128)S(1)}, f32[32,2048]{1,0:T(8,128)S(1)}, u32[]{:S(2)}, u32[]{:S(2)}) collective-permute-start(f32[32,2048]{1,0:T(8,128)S(1)} %copy-done.6), channel_id=1, source_target_pairs={{0,192},{32,224},{64,128},{96,160},{128,64},{160,96},{192,0},{224,... | collective-permute-start | bytes 786440 | tf_op jit(solution)/shard_map/ppermute | solution.py:369
  71.1 2.4 %collective-permute-start.22 = (f32[32,2048]{1,0:T(8,128)S(1)}, f32[32,2048]{1,0:T(8,128)S(1)}, u32[]{:S(2)}, u32[]{:S(2)}) collective-permute-start(f32[32,2048]{1,0:T(8,128)S(1)} %copy-done.5), channel_id=1, source_target_pairs={{0,224},{32,192},{64,160},{96,128},{128,96},{160,64},{192,32},{224... | collective-permute-start | bytes 786440 | tf_op jit(solution)/shard_map/ppermute | solution.py:369
  73.5 23.9 %mixing.1 = (f32[16,256,256]{2,1,0:T(8,128)S(1)}, f32[256,128]{1,0:T(8,128)S(1)}) custom-call(s32[2]{0:T(128)S(1)} %copy-done.2, s32[8,16]{1,0:T(8,128)S(1)} %bitcast.5, s32[8,16]{1,0:T(8,128)S(1)} %bitcast.6, f32[16,264,128]{2,1,0:T(8,128)S(1)} %own_table.1.refs_3_, f32[16,264,128]{2,1,0:T(8,128)S(1)} %collective-permute-done.12.refs_4_, ...), custom_call_target="tpu_custom_call" | custom-call | flops 16106127360 | bytes 12582912 | tf_op jit(solution)/shard_map/mixing/pallas_call | solution.py:330
  97.4 5.4 %apply.1 = f32[256,4,512]{2,1,0:T(4,128)} custom-call(s32[2]{0:T(128)S(1)} %copy-done.2, f32[16,256,256]{2,1,0:T(8,128)S(1)} %get-tuple-element.53.root_ref, f32[256,128]{1,0:T(8,128)S(1)} %get-tuple-element.54.offset_ref, f32[32,2048]{1,0:T(8,128)S(1)} %copy-done.1, f32[32,2048]{1,0:T(8,128)S(1)} %collective-permute-done.17.refs_1_, ...), custom_call_target="tpu_custom_call" | custom-call | tf_op jit(solution)/shard_map/apply/pallas_call | solution.py:356
  (51 shorter events, 9.7 us)
Async XLA Ops:
  0.7 72.8 %copy-start.4 = (s32[16,8]{0,1:T(8,128)S(1)}, s32[16,8]{0,1:T(8,128)}, u32[]{:S(2)}) copy-start(s32[16,8]{0,1:T(8,128)} %param.11) | copy-start | bytes 1540
  6.9 12.5 %collective-permute-start.4 = (f32[32,2176]{1,0:T(8,128)}, f32[32,2176]{1,0:T(8,128)S(1)}, u32[]{:S(2)}, u32[]{:S(2)}) collective-permute-start(f32[32,2176]{1,0:T(8,128)} %get-tuple-element.34.refs_0_), channel_id=1, source_target_pairs={{0,128},{32,160},{64,192},{96,224},{128,0},{160,32},{192,64},{224,... | collective-permute-start | bytes 835592 | tf_op jit(solution)/shard_map/ppermute | solution.py:369
  8.6 12.4 %collective-permute-start = (f32[32,2176]{1,0:T(8,128)}, f32[32,2176]{1,0:T(8,128)S(1)}, u32[]{:S(2)}, u32[]{:S(2)}) collective-permute-start(f32[32,2176]{1,0:T(8,128)} %get-tuple-element.34.refs_0_), channel_id=1, source_target_pairs={{1,2},{3,4},{5,6},{7,8},{9,10},{11,12},{13,14},{15,16},{17,18},{19... | collective-permute-start | bytes 835592 | tf_op jit(solution)/shard_map/ppermute | solution.py:385
  13.0 11.9 %collective-permute-start.6 = (f32[32,2176]{1,0:T(8,128)}, f32[32,2176]{1,0:T(8,128)S(1)}, u32[]{:S(2)}, u32[]{:S(2)}) collective-permute-start(f32[32,2176]{1,0:T(8,128)} %get-tuple-element.34.refs_0_), channel_id=1, source_target_pairs={{0,96},{32,64},{64,32},{96,0},{128,224},{160,192},{192,160},{224,1... | collective-permute-start | bytes 835592 | tf_op jit(solution)/shard_map/ppermute | solution.py:369
  19.5 6.9 %collective-permute-start.7 = (f32[32,2176]{1,0:T(8,128)S(1)}, f32[32,2176]{1,0:T(8,128)S(1)}, u32[]{:S(2)}, u32[]{:S(2)}) collective-permute-start(f32[32,2176]{1,0:T(8,128)S(1)} %collective-permute-done.4.refs_1_), channel_id=1, source_target_pairs={{0,32},{32,0},{64,96},{96,64},{128,160},{160,128},{192,224},{224,1... | collective-permute-start | bytes 835592 | tf_op jit(solution)/shard_map/ppermute | solution.py:369
  21.0 7.8 %collective-permute-start.3 = (f32[32,2176]{1,0:T(8,128)S(1)}, f32[32,2176]{1,0:T(8,128)S(1)}, u32[]{:S(2)}, u32[]{:S(2)}) collective-permute-start(f32[32,2176]{1,0:T(8,128)S(1)} %collective-permute-done.refs_5_), channel_id=1, source_target_pairs={{0,128},{32,160},{64,192},{96,224},{128,0},{160,32},{192,64},{224,... | collective-permute-start | bytes 835592 | tf_op jit(solution)/shard_map/ppermute | solution.py:369
  22.3 9.4 %collective-permute-start.2 = (f32[32,2176]{1,0:T(8,128)S(1)}, f32[32,2176]{1,0:T(8,128)S(1)}, u32[]{:S(2)}, u32[]{:S(2)}) collective-permute-start(f32[32,2176]{1,0:T(8,128)S(1)} %collective-permute-done.refs_5_), channel_id=1, source_target_pairs={{0,96},{32,64},{64,32},{96,0},{128,224},{160,192},{192,160},{224,1... | collective-permute-start | bytes 835592 | tf_op jit(solution)/shard_map/ppermute | solution.py:369
  24.3 13.8 %collective-permute-start.5 = (f32[32,2176]{1,0:T(8,128)}, f32[32,2176]{1,0:T(8,128)S(1)}, u32[]{:S(2)}, u32[]{:S(2)}) collective-permute-start(f32[32,2176]{1,0:T(8,128)} %get-tuple-element.34.refs_0_), channel_id=1, source_target_pairs={{0,32},{32,0},{64,96},{96,64},{128,160},{160,128},{192,224},{224,1... | collective-permute-start | bytes 835592 | tf_op jit(solution)/shard_map/ppermute | solution.py:369
  24.9 13.2 %collective-permute-start.1 = (f32[32,2176]{1,0:T(8,128)S(1)}, f32[32,2176]{1,0:T(8,128)S(1)}, u32[]{:S(2)}, u32[]{:S(2)}) collective-permute-start(f32[32,2176]{1,0:T(8,128)S(1)} %collective-permute-done.refs_5_), channel_id=1, source_target_pairs={{0,32},{32,0},{64,96},{96,64},{128,160},{160,128},{192,224},{224,1... | collective-permute-start | bytes 835592 | tf_op jit(solution)/shard_map/ppermute | solution.py:369
  26.4 17.7 %collective-permute-start.8 = (f32[32,2176]{1,0:T(8,128)S(1)}, f32[32,2176]{1,0:T(8,128)S(1)}, u32[]{:S(2)}, u32[]{:S(2)}) collective-permute-start(f32[32,2176]{1,0:T(8,128)S(1)} %collective-permute-done.4.refs_1_), channel_id=1, source_target_pairs={{0,96},{32,64},{64,32},{96,0},{128,224},{160,192},{192,160},{224,1... | collective-permute-start | bytes 835592 | tf_op jit(solution)/shard_map/ppermute | solution.py:369
  28.8 15.3 %collective-permute-start.9 = (f32[32,2176]{1,0:T(8,128)S(1)}, f32[32,2176]{1,0:T(8,128)S(1)}, u32[]{:S(2)}, u32[]{:S(2)}) collective-permute-start(f32[32,2176]{1,0:T(8,128)S(1)} %collective-permute-done.6.refs_3_), channel_id=1, source_target_pairs={{0,32},{32,0},{64,96},{96,64},{128,160},{160,128},{192,224},{224,1... | collective-permute-start | bytes 835592 | tf_op jit(solution)/shard_map/ppermute | solution.py:369
  31.7 12.4 %collective-permute-start.10 = (f32[32,2176]{1,0:T(8,128)S(1)}, f32[32,2176]{1,0:T(8,128)S(1)}, u32[]{:S(2)}, u32[]{:S(2)}) collective-permute-start(f32[32,2176]{1,0:T(8,128)S(1)} %collective-permute-done.7.refs_4_), channel_id=1, source_target_pairs={{0,96},{32,64},{64,32},{96,0},{128,224},{160,192},{192,160},{224,1... | collective-permute-start | bytes 835592 | tf_op jit(solution)/shard_map/ppermute | solution.py:369
  46.4 18.9 %collective-permute-start.12 = (f32[16,264,128]{2,1,0:T(8,128)S(1)}, f32[16,264,128]{2,1,0:T(8,128)S(1)}, u32[]{:S(2)}, u32[]{:S(2)}) collective-permute-start(f32[16,264,128]{2,1,0:T(8,128)S(1)} %own_table.1.refs_3_), channel_id=1, source_target_pairs={{0,1},{1,0},{2,3},{3,2},{4,5},{5,4},{6,7},{7,6},{8,9},{9,8},{10,11... | collective-permute-start | bytes 6488072 | tf_op jit(solution)/shard_map/ppermute | solution.py:373
  48.2 9.5 %collective-permute-start.14 = (f32[32,2176]{1,0:T(8,128)S(1)}, f32[32,2176]{1,0:T(8,128)S(1)}, u32[]{:S(2)}, u32[]{:S(2)}) collective-permute-start(f32[32,2176]{1,0:T(8,128)S(1)} %collective-permute-done.3.refs_6_), channel_id=1, source_target_pairs={{0,32},{32,0},{64,96},{96,64},{128,160},{160,128},{192,224},{224,1... | collective-permute-start | bytes 835592 | tf_op jit(solution)/shard_map/ppermute | solution.py:369
  48.8 10.9 %collective-permute-start.15 = (f32[32,2176]{1,0:T(8,128)S(1)}, f32[32,2176]{1,0:T(8,128)S(1)}, u32[]{:S(2)}, u32[]{:S(2)}) collective-permute-start(f32[32,2176]{1,0:T(8,128)S(1)} %collective-permute-done.3.refs_6_), channel_id=1, source_target_pairs={{0,96},{32,64},{64,32},{96,0},{128,224},{160,192},{192,160},{224,1... | collective-permute-start | bytes 835592 | tf_op jit(solution)/shard_map/ppermute | solution.py:369
  49.7 14.0 %collective-permute-start.11 = (f32[32,2176]{1,0:T(8,128)S(1)}, f32[32,2176]{1,0:T(8,128)S(1)}, u32[]{:S(2)}, u32[]{:S(2)}) collective-permute-start(f32[32,2176]{1,0:T(8,128)S(1)} %collective-permute-done.2.refs_8_), channel_id=1, source_target_pairs={{0,32},{32,0},{64,96},{96,64},{128,160},{160,128},{192,224},{224,1... | collective-permute-start | bytes 835592 | tf_op jit(solution)/shard_map/ppermute | solution.py:369
  57.7 13.4 %collective-permute-start.16 = (f32[32,2176]{1,0:T(8,128)S(1)}, f32[32,2176]{1,0:T(8,128)S(1)}, u32[]{:S(2)}, u32[]{:S(2)}) collective-permute-start(f32[32,2176]{1,0:T(8,128)S(1)} %collective-permute-done.14.refs_9_), channel_id=1, source_target_pairs={{0,96},{32,64},{64,32},{96,0},{128,224},{160,192},{192,160},{224,1... | collective-permute-start | bytes 835592 | tf_op jit(solution)/shard_map/ppermute | solution.py:369
  58.9 6.4 %collective-permute-start.13 = (f32[32,2048]{1,0:T(8,128)S(1)}, f32[32,2048]{1,0:T(8,128)S(1)}, u32[]{:S(2)}, u32[]{:S(2)}) collective-permute-start(f32[32,2048]{1,0:T(8,128)S(1)} %copy-done.11), channel_id=1, source_target_pairs={{0,128},{32,160},{64,192},{96,224},{128,0},{160,32},{192,64},{224,... | collective-permute-start | bytes 786440 | tf_op jit(solution)/shard_map/ppermute | solution.py:369
  59.7 9.6 %collective-permute-start.17 = (f32[32,2048]{1,0:T(8,128)S(1)}, f32[32,2048]{1,0:T(8,128)S(1)}, u32[]{:S(2)}, u32[]{:S(2)}) collective-permute-start(f32[32,2048]{1,0:T(8,128)S(1)} %copy-done.10), channel_id=1, source_target_pairs={{0,32},{32,0},{64,96},{96,64},{128,160},{160,128},{192,224},{224,1... | collective-permute-start | bytes 786440 | tf_op jit(solution)/shard_map/ppermute | solution.py:369
  63.7 33.7 %collective-permute-start.19 = (f32[32,2048]{1,0:T(8,128)S(1)}, f32[32,2048]{1,0:T(8,128)S(1)}, u32[]{:S(2)}, u32[]{:S(2)}) collective-permute-start(f32[32,2048]{1,0:T(8,128)S(1)} %copy-done.9), channel_id=1, source_target_pairs={{0,96},{32,64},{64,32},{96,0},{128,224},{160,192},{192,160},{224,1... | collective-permute-start | bytes 786440 | tf_op jit(solution)/shard_map/ppermute | solution.py:369
  65.3 32.1 %collective-permute-start.18 = (f32[32,2048]{1,0:T(8,128)S(1)}, f32[32,2048]{1,0:T(8,128)S(1)}, u32[]{:S(2)}, u32[]{:S(2)}) collective-permute-start(f32[32,2048]{1,0:T(8,128)S(1)} %copy-done.8), channel_id=1, source_target_pairs={{0,64},{32,96},{64,0},{96,32},{128,192},{160,224},{192,128},{224,1... | collective-permute-start | bytes 786440 | tf_op jit(solution)/shard_map/ppermute | solution.py:369
  66.8 30.6 %collective-permute-start.20 = (f32[32,2048]{1,0:T(8,128)S(1)}, f32[32,2048]{1,0:T(8,128)S(1)}, u32[]{:S(2)}, u32[]{:S(2)}) collective-permute-start(f32[32,2048]{1,0:T(8,128)S(1)} %copy-done.7), channel_id=1, source_target_pairs={{0,160},{32,128},{64,224},{96,192},{128,32},{160,0},{192,96},{224,... | collective-permute-start | bytes 786440 | tf_op jit(solution)/shard_map/ppermute | solution.py:369
  69.3 28.1 %collective-permute-start.21 = (f32[32,2048]{1,0:T(8,128)S(1)}, f32[32,2048]{1,0:T(8,128)S(1)}, u32[]{:S(2)}, u32[]{:S(2)}) collective-permute-start(f32[32,2048]{1,0:T(8,128)S(1)} %copy-done.6), channel_id=1, source_target_pairs={{0,192},{32,224},{64,128},{96,160},{128,64},{160,96},{192,0},{224,... | collective-permute-start | bytes 786440 | tf_op jit(solution)/shard_map/ppermute | solution.py:369
  71.1 26.3 %collective-permute-start.22 = (f32[32,2048]{1,0:T(8,128)S(1)}, f32[32,2048]{1,0:T(8,128)S(1)}, u32[]{:S(2)}, u32[]{:S(2)}) collective-permute-start(f32[32,2048]{1,0:T(8,128)S(1)} %copy-done.5), channel_id=1, source_target_pairs={{0,224},{32,192},{64,160},{96,128},{128,96},{160,64},{192,32},{224... | collective-permute-start | bytes 786440 | tf_op jit(solution)/shard_map/ppermute | solution.py:369
  (11 other events, 280.4 us)

commit v5 on v4

--- a/solution.py
+++ b/solution.py
@@ -9,7 +9,7 @@
 BF16 = jnp.bfloat16
 MEM = 8
 LANES = 128
-WIDE = 4
+WIDE = 8
 LIMIT = 62 << 20
 VMEM = pl.BlockSpec(memory_space=pltpu.VMEM)
 SMEM = pl.BlockSpec(memory_space=pltpu.SMEM)
@@ -344,7 +344,7 @@
             pltpu.VMEM((48, 264, LANES), F32),
             pltpu.SemaphoreType.DMA((MEM + 2,)),
         ],
-        compiler_params=pltpu.CompilerParams(vmem_limit_bytes=30 << 20),
+        compiler_params=pltpu.CompilerParams(vmem_limit_bytes=42 << 20),
         cost_estimate=pl.CostEstimate(
             flops=16 * 30 * 2 * 256**3, bytes_accessed=12 << 20, transcendentals=0
         ),
@@ -393,12 +393,12 @@
     far1, far3, far4, own4 = hold((far1, far3, far4, own4))
     far5, far7 = send(far4, 1), send(far4, 3)
     table = own_table(where, (obs, own4, own1, own3, own5, own7, own2, own6))
-    table, four, one = hold((table, pieces[4], pieces[1]))
-    sibling = swap_cores(table)
+    table, four = hold((table, pieces[4]))
     got[4] = send(four, 4)
-    far2, far6 = send(far3, 1), send(far5, 3)
-    far5, far7, *rest = hold((far5, far7, one, pieces[3]))
-    got[1], got[3] = send(rest[0], 1), send(rest[1], 3)
+    far2 = send(far3, 1)
+    far5, far7, table, one, three = hold((far5, far7, table, pieces[1], pieces[3]))
+    far6, sibling = send(far5, 3), swap_cores(table)
+    got[1], got[3] = send(one, 1), send(three, 3)
     far2, sibling, got[4], *rest = hold((far2, sibling, got[4], pieces[2], *pieces[5:]))
     for s, x in zip((2, 5, 6, 7), rest):
         got[s] = send(x, s)

time: 103 us -> 100 us (0.971)
  waiting for transfers between devices: 29.5 us -> 25.2 us
  starting transfers between devices: 34.7 us -> 36.5 us
    ppermute x21, waiting for transfers between devices: 29.5 us -> 25.2 us  [send(): return lax.ppermute(x, 'mem', [(i, i ^ flip) for i in range(MEM)])]
    ppermute x21, starting transfers between devices: 28.4 us -> 30.3 us  [send(): return lax.ppermute(x, 'mem', [(i, i ^ flip) for i in range(MEM)])]
  transfers between devices with their start and end apart: 23 -> 23, of which waited for: 8 -> 8; matrix products, arithmetic and copies ran while one was open for 0% -> 0% of each run, Pallas kernels for 23% -> 24%
where the time goes in v5:
time: 100 us; the launch traced here: 99.8 us
  starting transfers between devices  36.5 us (36%)
  Pallas kernels  36.1 us (36%)
  waiting for transfers between devices  25.2 us (25%)
    ppermute x21, starting transfers between devices, send(): return lax.ppermute(x, 'mem', [(i, i ^ flip) for i in range(MEM)])  30.3 us
    ppermute x21, waiting for transfers between devices, send(): return lax.ppermute(x, 'mem', [(i, i ^ flip) for i in range(MEM)])  25.2 us
    pallas_call x1, Pallas kernels, find_mixing(): pl.pallas_call(mixing_kernel, out_shape=[jax.ShapeDtypeStruct((16, 256, 2...  23.2 us
    pallas_call x1, Pallas kernels, local_obs(): pl.pallas_call(obs_kernel, out_shape=[jax.ShapeDtypeStruct((members, 2048...  6.26 us
    pallas_call x1, Pallas kernels, apply_mixing(): pl.pallas_call(apply_kernel, out_shape=jax.ShapeDtypeStruct((256, 4, 512)...  5.42 us
    ppermute x1, starting transfers between devices, local(): lax.ppermute(obs, 'tile', [(i, i + 1) for i in range(1, 31, 2)] + [(i + 1...  4.4 us
  transfers between devices with their start and end apart: 23, of which 8 were waited for; matrix products, arithmetic and copies ran while one was open for 0% of the time, Pallas kernels for 24%

profile of v5, /device:TPU:192, one launch (start us, length us, event | category | flops | bytes accessed | tf_op | source)
XLA Modules:
  0.0 99.8 jit_solution(18367010419966458640)
XLA Ops:
  0.7 6.3 %local_obs.1 = (f32[32,2048]{1,0:T(8,128)}, f32[32,2048]{1,0:T(8,128)}, f32[32,2048]{1,0:T(8,128)}, f32[32,2048]{1,0:T(8,128)}, f32[32,2048]{1,0:T(8,128)}, /*in...) custom-call(s32[2]{0:T(128)} %pad_add_fusion.where_ref.refs_0_, ...), custom_call_target="tpu_custom_call" | custom-call | tf_op jit(solution)/shard_map/local_obs/pallas_call | solution.py:113
  6.9 1.7 %collective-permute-start.4 = (f32[32,2176]{1,0:T(8,128)}, f32[32,2176]{1,0:T(8,128)S(1)}, u32[]{:S(2)}, u32[]{:S(2)}) collective-permute-start(f32[32,2176]{1,0:T(8,128)} %get-tuple-element.34.refs_0_), channel_id=1, source_target_pairs={{0,128},{32,160},{64,192},{96,224},{128,0},{160,32},{192,64},{224,... | collective-permute-start | bytes 835592 | tf_op jit(solution)/shard_map/ppermute | solution.py:369
  8.6 4.4 %collective-permute-start = (f32[32,2176]{1,0:T(8,128)}, f32[32,2176]{1,0:T(8,128)S(1)}, u32[]{:S(2)}, u32[]{:S(2)}) collective-permute-start(f32[32,2176]{1,0:T(8,128)} %get-tuple-element.34.refs_0_), channel_id=1, source_target_pairs={{1,2},{3,4},{5,6},{7,8},{9,10},{11,12},{13,14},{15,16},{17,18},{19... | collective-permute-start | bytes 835592 | tf_op jit(solution)/shard_map/ppermute | solution.py:385
  13.0 2.8 %collective-permute-start.8 = (f32[32,2176]{1,0:T(8,128)}, f32[32,2176]{1,0:T(8,128)S(1)}, u32[]{:S(2)}, u32[]{:S(2)}) collective-permute-start(f32[32,2176]{1,0:T(8,128)} %get-tuple-element.34.refs_0_), channel_id=1, source_target_pairs={{0,96},{32,64},{64,32},{96,0},{128,224},{160,192},{192,160},{224,1... | collective-permute-start | bytes 835592 | tf_op jit(solution)/shard_map/ppermute | solution.py:369
  15.9 3.6 %collective-permute-done.4.refs_1_ = f32[32,2176]{1,0:T(8,128)S(1)} collective-permute-done((f32[32,2176]{1,0:T(8,128)}, f32[32,2176]{1,0:T(8,128)S(1)}, u32[]{:S(2)}, u32[]{:S(2)}) %collective-permute-start.4) | collective-permute-done | bytes 278560 | tf_op jit(solution)/shard_map/ppermute | solution.py:369
  19.5 1.5 %collective-permute-start.9 = (f32[32,2176]{1,0:T(8,128)S(1)}, f32[32,2176]{1,0:T(8,128)S(1)}, u32[]{:S(2)}, u32[]{:S(2)}) collective-permute-start(f32[32,2176]{1,0:T(8,128)S(1)} %collective-permute-done.4.refs_1_), channel_id=1, source_target_pairs={{0,32},{32,0},{64,96},{96,64},{128,160},{160,128},{192,224},{224,1... | collective-permute-start | bytes 835592 | tf_op jit(solution)/shard_map/ppermute | solution.py:369
  21.0 1.3 %collective-permute-start.3 = (f32[32,2176]{1,0:T(8,128)S(1)}, f32[32,2176]{1,0:T(8,128)S(1)}, u32[]{:S(2)}, u32[]{:S(2)}) collective-permute-start(f32[32,2176]{1,0:T(8,128)S(1)} %collective-permute-done.refs_5_), channel_id=1, source_target_pairs={{0,128},{32,160},{64,192},{96,224},{128,0},{160,32},{192,64},{224,... | collective-permute-start | bytes 835592 | tf_op jit(solution)/shard_map/ppermute | solution.py:369
  22.3 2.1 %collective-permute-start.2 = (f32[32,2176]{1,0:T(8,128)S(1)}, f32[32,2176]{1,0:T(8,128)S(1)}, u32[]{:S(2)}, u32[]{:S(2)}) collective-permute-start(f32[32,2176]{1,0:T(8,128)S(1)} %collective-permute-done.refs_5_), channel_id=1, source_target_pairs={{0,96},{32,64},{64,32},{96,0},{128,224},{160,192},{192,160},{224,1... | collective-permute-start | bytes 835592 | tf_op jit(solution)/shard_map/ppermute | solution.py:369
  24.9 1.4 %collective-permute-start.7 = (f32[32,2176]{1,0:T(8,128)}, f32[32,2176]{1,0:T(8,128)S(1)}, u32[]{:S(2)}, u32[]{:S(2)}) collective-permute-start(f32[32,2176]{1,0:T(8,128)} %get-tuple-element.34.refs_0_), channel_id=1, source_target_pairs={{0,32},{32,0},{64,96},{96,64},{128,160},{160,128},{192,224},{224,1... | collective-permute-start | bytes 835592 | tf_op jit(solution)/shard_map/ppermute | solution.py:369
  26.4 2.4 %collective-permute-start.10 = (f32[32,2176]{1,0:T(8,128)S(1)}, f32[32,2176]{1,0:T(8,128)S(1)}, u32[]{:S(2)}, u32[]{:S(2)}) collective-permute-start(f32[32,2176]{1,0:T(8,128)S(1)} %collective-permute-done.4.refs_1_), channel_id=1, source_target_pairs={{0,96},{32,64},{64,32},{96,0},{128,224},{160,192},{192,160},{224,1... | collective-permute-start | bytes 835592 | tf_op jit(solution)/shard_map/ppermute | solution.py:369
  29.0 2.6 %collective-permute-done.2.refs_8_ = f32[32,2176]{1,0:T(8,128)S(1)} collective-permute-done((f32[32,2176]{1,0:T(8,128)S(1)}, f32[32,2176]{1,0:T(8,128)S(1)}, u32[]{:S(2)}, u32[]{:S(2)}) %collective-permute-start.2) | collective-permute-done | bytes 278560 | tf_op jit(solution)/shard_map/ppermute | solution.py:369
  32.9 2.0 %collective-permute-start.6 = (f32[32,2176]{1,0:T(8,128)S(1)}, f32[32,2176]{1,0:T(8,128)S(1)}, u32[]{:S(2)}, u32[]{:S(2)}) collective-permute-start(f32[32,2176]{1,0:T(8,128)S(1)} %collective-permute-done.3.refs_6_), channel_id=1, source_target_pairs={{0,96},{32,64},{64,32},{96,0},{128,224},{160,192},{192,160},{224,1... | collective-permute-start | bytes 835592 | tf_op jit(solution)/shard_map/ppermute | solution.py:369
  34.9 3.0 %collective-permute-done.7.refs_2_ = f32[32,2176]{1,0:T(8,128)S(1)} collective-permute-done((f32[32,2176]{1,0:T(8,128)}, f32[32,2176]{1,0:T(8,128)S(1)}, u32[]{:S(2)}, u32[]{:S(2)}) %collective-permute-start.7) | collective-permute-done | bytes 278560 | tf_op jit(solution)/shard_map/ppermute | solution.py:369
  38.8 5.0 %collective-permute-done.11.refs_6_ = f32[32,2176]{1,0:T(8,128)S(1)} collective-permute-done((f32[32,2176]{1,0:T(8,128)S(1)}, f32[32,2176]{1,0:T(8,128)S(1)}, u32[]{:S(2)}, u32[]{:S(2)}) %collective-permute-start.11) | collective-permute-done | bytes 278560 | tf_op jit(solution)/shard_map/ppermute | solution.py:369
  44.9 1.3 %own_table.1.refs_3_ = f32[16,264,128]{2,1,0:T(8,128)S(1)} custom-call(s32[2]{0:T(128)S(1)} %copy-done.2, f32[32,2176]{1,0:T(8,128)S(1)} %copy-done, f32[32,2176]{1,0:T(8,128)S(1)} %collective-permute-done.4.refs_1_, f32[32,2176]{1,0:T(8,128)S(1)} %collective-permute-done.7.refs_2_, f32[32,2176]{1,0:T(8,128)S(1)} %collective-permute-done.8.refs_3_, ...), custom_call_target="tpu_custom_call" | custom-call | flops 2097152 | bytes 6291456 | tf_op jit(solution)/shard_map/own_table/pallas_call | solution.py:182
  46.2 3.4 %collective-permute-done.6.refs_10_ = f32[32,2176]{1,0:T(8,128)S(1)} collective-permute-done((f32[32,2176]{1,0:T(8,128)S(1)}, f32[32,2176]{1,0:T(8,128)S(1)}, u32[]{:S(2)}, u32[]{:S(2)}) %collective-permute-start.6) | collective-permute-done | bytes 278560 | tf_op jit(solution)/shard_map/ppermute | solution.py:369
  49.8 1.8 %collective-permute-start.14 = (f32[16,264,128]{2,1,0:T(8,128)S(1)}, f32[16,264,128]{2,1,0:T(8,128)S(1)}, u32[]{:S(2)}, u32[]{:S(2)}) collective-permute-start(f32[16,264,128]{2,1,0:T(8,128)S(1)} %own_table.1.refs_3_), channel_id=1, source_target_pairs={{0,1},{1,0},{2,3},{3,2},{4,5},{5,4},{6,7},{7,6},{8,9},{9,8},{10,11... | collective-permute-start | bytes 6488072 | tf_op jit(solution)/shard_map/ppermute | solution.py:373
  55.2 5.9 %collective-permute-done.13.refs_11_ = f32[32,2176]{1,0:T(8,128)S(1)} collective-permute-done((f32[32,2176]{1,0:T(8,128)S(1)}, f32[32,2176]{1,0:T(8,128)S(1)}, u32[]{:S(2)}, u32[]{:S(2)}) %collective-permute-start.13) | collective-permute-done | bytes 278560 | tf_op jit(solution)/shard_map/ppermute | solution.py:369
  62.4 1.5 %collective-permute-start.18 = (f32[32,2048]{1,0:T(8,128)S(1)}, f32[32,2048]{1,0:T(8,128)S(1)}, u32[]{:S(2)}, u32[]{:S(2)}) collective-permute-start(f32[32,2048]{1,0:T(8,128)S(1)} %copy-done.8), channel_id=1, source_target_pairs={{0,64},{32,96},{64,0},{96,32},{128,192},{160,224},{192,128},{224,1... | collective-permute-start | bytes 786440 | tf_op jit(solution)/shard_map/ppermute | solution.py:369
  63.9 1.6 %collective-permute-start.20 = (f32[32,2048]{1,0:T(8,128)S(1)}, f32[32,2048]{1,0:T(8,128)S(1)}, u32[]{:S(2)}, u32[]{:S(2)}) collective-permute-start(f32[32,2048]{1,0:T(8,128)S(1)} %copy-done.7), channel_id=1, source_target_pairs={{0,160},{32,128},{64,224},{96,192},{128,32},{160,0},{192,96},{224,... | collective-permute-start | bytes 786440 | tf_op jit(solution)/shard_map/ppermute | solution.py:369
  66.8 1.9 %collective-permute-start.21 = (f32[32,2048]{1,0:T(8,128)S(1)}, f32[32,2048]{1,0:T(8,128)S(1)}, u32[]{:S(2)}, u32[]{:S(2)}) collective-permute-start(f32[32,2048]{1,0:T(8,128)S(1)} %copy-done.6), channel_id=1, source_target_pairs={{0,192},{32,224},{64,128},{96,160},{128,64},{160,96},{192,0},{224,... | collective-permute-start | bytes 786440 | tf_op jit(solution)/shard_map/ppermute | solution.py:369
  68.6 2.3 %collective-permute-start.22 = (f32[32,2048]{1,0:T(8,128)S(1)}, f32[32,2048]{1,0:T(8,128)S(1)}, u32[]{:S(2)}, u32[]{:S(2)}) collective-permute-start(f32[32,2048]{1,0:T(8,128)S(1)} %copy-done.5), channel_id=1, source_target_pairs={{0,224},{32,192},{64,160},{96,128},{128,96},{160,64},{192,32},{224... | collective-permute-start | bytes 786440 | tf_op jit(solution)/shard_map/ppermute | solution.py:369
  70.9 23.2 %mixing.1 = (f32[16,256,256]{2,1,0:T(8,128)S(1)}, f32[256,128]{1,0:T(8,128)S(1)}) custom-call(s32[2]{0:T(128)S(1)} %copy-done.2, s32[8,16]{1,0:T(8,128)S(1)} %bitcast.5, s32[8,16]{1,0:T(8,128)S(1)} %bitcast.6, f32[16,264,128]{2,1,0:T(8,128)S(1)} %own_table.1.refs_3_, f32[16,264,128]{2,1,0:T(8,128)S(1)} %collective-permute-done.14.refs_4_, ...), custom_call_target="tpu_custom_call" | custom-call | flops 16106127360 | bytes 12582912 | tf_op jit(solution)/shard_map/mixing/pallas_call | solution.py:330
  94.2 5.4 %apply.1 = f32[256,4,512]{2,1,0:T(4,128)} custom-call(s32[2]{0:T(128)S(1)} %copy-done.2, f32[16,256,256]{2,1,0:T(8,128)S(1)} %get-tuple-element.53.root_ref, f32[256,128]{1,0:T(8,128)S(1)} %get-tuple-element.54.offset_ref, f32[32,2048]{1,0:T(8,128)S(1)} %copy-done.1, f32[32,2048]{1,0:T(8,128)S(1)} %collective-permute-done.17.refs_1_, ...), custom_call_target="tpu_custom_call" | custom-call | tf_op jit(solution)/shard_map/apply/pallas_call | solution.py:356
  (51 shorter events, 10.9 us)
Async XLA Ops:
  0.7 70.3 %copy-start.4 = (s32[16,8]{0,1:T(8,128)S(1)}, s32[16,8]{0,1:T(8,128)}, u32[]{:S(2)}) copy-start(s32[16,8]{0,1:T(8,128)} %param.11) | copy-start | bytes 1540
  6.9 12.5 %collective-permute-start.4 = (f32[32,2176]{1,0:T(8,128)}, f32[32,2176]{1,0:T(8,128)S(1)}, u32[]{:S(2)}, u32[]{:S(2)}) collective-permute-start(f32[32,2176]{1,0:T(8,128)} %get-tuple-element.34.refs_0_), channel_id=1, source_target_pairs={{0,128},{32,160},{64,192},{96,224},{128,0},{160,32},{192,64},{224,... | collective-permute-start | bytes 835592 | tf_op jit(solution)/shard_map/ppermute | solution.py:369
  8.6 12.4 %collective-permute-start = (f32[32,2176]{1,0:T(8,128)}, f32[32,2176]{1,0:T(8,128)S(1)}, u32[]{:S(2)}, u32[]{:S(2)}) collective-permute-start(f32[32,2176]{1,0:T(8,128)} %get-tuple-element.34.refs_0_), channel_id=1, source_target_pairs={{1,2},{3,4},{5,6},{7,8},{9,10},{11,12},{13,14},{15,16},{17,18},{19... | collective-permute-start | bytes 835592 | tf_op jit(solution)/shard_map/ppermute | solution.py:385
  13.0 11.9 %collective-permute-start.8 = (f32[32,2176]{1,0:T(8,128)}, f32[32,2176]{1,0:T(8,128)S(1)}, u32[]{:S(2)}, u32[]{:S(2)}) collective-permute-start(f32[32,2176]{1,0:T(8,128)} %get-tuple-element.34.refs_0_), channel_id=1, source_target_pairs={{0,96},{32,64},{64,32},{96,0},{128,224},{160,192},{192,160},{224,1... | collective-permute-start | bytes 835592 | tf_op jit(solution)/shard_map/ppermute | solution.py:369
  19.5 6.9 %collective-permute-start.9 = (f32[32,2176]{1,0:T(8,128)S(1)}, f32[32,2176]{1,0:T(8,128)S(1)}, u32[]{:S(2)}, u32[]{:S(2)}) collective-permute-start(f32[32,2176]{1,0:T(8,128)S(1)} %collective-permute-done.4.refs_1_), channel_id=1, source_target_pairs={{0,32},{32,0},{64,96},{96,64},{128,160},{160,128},{192,224},{224,1... | collective-permute-start | bytes 835592 | tf_op jit(solution)/shard_map/ppermute | solution.py:369
  21.0 7.8 %collective-permute-start.3 = (f32[32,2176]{1,0:T(8,128)S(1)}, f32[32,2176]{1,0:T(8,128)S(1)}, u32[]{:S(2)}, u32[]{:S(2)}) collective-permute-start(f32[32,2176]{1,0:T(8,128)S(1)} %collective-permute-done.refs_5_), channel_id=1, source_target_pairs={{0,128},{32,160},{64,192},{96,224},{128,0},{160,32},{192,64},{224,... | collective-permute-start | bytes 835592 | tf_op jit(solution)/shard_map/ppermute | solution.py:369
  22.3 9.4 %collective-permute-start.2 = (f32[32,2176]{1,0:T(8,128)S(1)}, f32[32,2176]{1,0:T(8,128)S(1)}, u32[]{:S(2)}, u32[]{:S(2)}) collective-permute-start(f32[32,2176]{1,0:T(8,128)S(1)} %collective-permute-done.refs_5_), channel_id=1, source_target_pairs={{0,96},{32,64},{64,32},{96,0},{128,224},{160,192},{192,160},{224,1... | collective-permute-start | bytes 835592 | tf_op jit(solution)/shard_map/ppermute | solution.py:369
  24.3 8.5 %collective-permute-start.1 = (f32[32,2176]{1,0:T(8,128)S(1)}, f32[32,2176]{1,0:T(8,128)S(1)}, u32[]{:S(2)}, u32[]{:S(2)}) collective-permute-start(f32[32,2176]{1,0:T(8,128)S(1)} %collective-permute-done.refs_5_), channel_id=1, source_target_pairs={{0,32},{32,0},{64,96},{96,64},{128,160},{160,128},{192,224},{224,1... | collective-permute-start | bytes 835592 | tf_op jit(solution)/shard_map/ppermute | solution.py:369
  24.9 13.0 %collective-permute-start.7 = (f32[32,2176]{1,0:T(8,128)}, f32[32,2176]{1,0:T(8,128)S(1)}, u32[]{:S(2)}, u32[]{:S(2)}) collective-permute-start(f32[32,2176]{1,0:T(8,128)} %get-tuple-element.34.refs_0_), channel_id=1, source_target_pairs={{0,32},{32,0},{64,96},{96,64},{128,160},{160,128},{192,224},{224,1... | collective-permute-start | bytes 835592 | tf_op jit(solution)/shard_map/ppermute | solution.py:369
  26.4 17.5 %collective-permute-start.10 = (f32[32,2176]{1,0:T(8,128)S(1)}, f32[32,2176]{1,0:T(8,128)S(1)}, u32[]{:S(2)}, u32[]{:S(2)}) collective-permute-start(f32[32,2176]{1,0:T(8,128)S(1)} %collective-permute-done.4.refs_1_), channel_id=1, source_target_pairs={{0,96},{32,64},{64,32},{96,0},{128,224},{160,192},{192,160},{224,1... | collective-permute-start | bytes 835592 | tf_op jit(solution)/shard_map/ppermute | solution.py:369
  28.8 15.1 %collective-permute-start.11 = (f32[32,2176]{1,0:T(8,128)S(1)}, f32[32,2176]{1,0:T(8,128)S(1)}, u32[]{:S(2)}, u32[]{:S(2)}) collective-permute-start(f32[32,2176]{1,0:T(8,128)S(1)} %collective-permute-done.8.refs_3_), channel_id=1, source_target_pairs={{0,32},{32,0},{64,96},{96,64},{128,160},{160,128},{192,224},{224,1... | collective-permute-start | bytes 835592 | tf_op jit(solution)/shard_map/ppermute | solution.py:369
  31.7 12.2 %collective-permute-start.12 = (f32[32,2176]{1,0:T(8,128)S(1)}, f32[32,2176]{1,0:T(8,128)S(1)}, u32[]{:S(2)}, u32[]{:S(2)}) collective-permute-start(f32[32,2176]{1,0:T(8,128)S(1)} %collective-permute-done.9.refs_4_), channel_id=1, source_target_pairs={{0,96},{32,64},{64,32},{96,0},{128,224},{160,192},{192,160},{224,1... | collective-permute-start | bytes 835592 | tf_op jit(solution)/shard_map/ppermute | solution.py:369
  32.9 16.7 %collective-permute-start.6 = (f32[32,2176]{1,0:T(8,128)S(1)}, f32[32,2176]{1,0:T(8,128)S(1)}, u32[]{:S(2)}, u32[]{:S(2)}) collective-permute-start(f32[32,2176]{1,0:T(8,128)S(1)} %collective-permute-done.3.refs_6_), channel_id=1, source_target_pairs={{0,96},{32,64},{64,32},{96,0},{128,224},{160,192},{192,160},{224,1... | collective-permute-start | bytes 835592 | tf_op jit(solution)/shard_map/ppermute | solution.py:369
  37.9 11.9 %collective-permute-start.5 = (f32[32,2176]{1,0:T(8,128)S(1)}, f32[32,2176]{1,0:T(8,128)S(1)}, u32[]{:S(2)}, u32[]{:S(2)}) collective-permute-start(f32[32,2176]{1,0:T(8,128)S(1)} %collective-permute-done.3.refs_6_), channel_id=1, source_target_pairs={{0,32},{32,0},{64,96},{96,64},{128,160},{160,128},{192,224},{224,1... | collective-permute-start | bytes 835592 | tf_op jit(solution)/shard_map/ppermute | solution.py:369
  49.8 12.5 %collective-permute-start.14 = (f32[16,264,128]{2,1,0:T(8,128)S(1)}, f32[16,264,128]{2,1,0:T(8,128)S(1)}, u32[]{:S(2)}, u32[]{:S(2)}) collective-permute-start(f32[16,264,128]{2,1,0:T(8,128)S(1)} %own_table.1.refs_3_), channel_id=1, source_target_pairs={{0,1},{1,0},{2,3},{3,2},{4,5},{5,4},{6,7},{7,6},{8,9},{9,8},{10,11... | collective-permute-start | bytes 6488072 | tf_op jit(solution)/shard_map/ppermute | solution.py:373
  51.6 9.5 %collective-permute-start.13 = (f32[32,2176]{1,0:T(8,128)S(1)}, f32[32,2176]{1,0:T(8,128)S(1)}, u32[]{:S(2)}, u32[]{:S(2)}) collective-permute-start(f32[32,2176]{1,0:T(8,128)S(1)} %collective-permute-done.2.refs_8_), channel_id=1, source_target_pairs={{0,32},{32,0},{64,96},{96,64},{128,160},{160,128},{192,224},{224,1... | collective-permute-start | bytes 835592 | tf_op jit(solution)/shard_map/ppermute | solution.py:369
  52.2 16.4 %collective-permute-start.16 = (f32[32,2176]{1,0:T(8,128)S(1)}, f32[32,2176]{1,0:T(8,128)S(1)}, u32[]{:S(2)}, u32[]{:S(2)}) collective-permute-start(f32[32,2176]{1,0:T(8,128)S(1)} %collective-permute-done.5.refs_9_), channel_id=1, source_target_pairs={{0,96},{32,64},{64,32},{96,0},{128,224},{160,192},{192,160},{224,1... | collective-permute-start | bytes 835592 | tf_op jit(solution)/shard_map/ppermute | solution.py:369
  53.3 9.0 %collective-permute-start.15 = (f32[32,2048]{1,0:T(8,128)S(1)}, f32[32,2048]{1,0:T(8,128)S(1)}, u32[]{:S(2)}, u32[]{:S(2)}) collective-permute-start(f32[32,2048]{1,0:T(8,128)S(1)} %copy-done.11), channel_id=1, source_target_pairs={{0,128},{32,160},{64,192},{96,224},{128,0},{160,32},{192,64},{224,... | collective-permute-start | bytes 786440 | tf_op jit(solution)/shard_map/ppermute | solution.py:369
  54.6 12.2 %collective-permute-start.17 = (f32[32,2048]{1,0:T(8,128)S(1)}, f32[32,2048]{1,0:T(8,128)S(1)}, u32[]{:S(2)}, u32[]{:S(2)}) collective-permute-start(f32[32,2048]{1,0:T(8,128)S(1)} %copy-done.10), channel_id=1, source_target_pairs={{0,32},{32,0},{64,96},{96,64},{128,160},{160,128},{192,224},{224,1... | collective-permute-start | bytes 786440 | tf_op jit(solution)/shard_map/ppermute | solution.py:369
  61.1 33.0 %collective-permute-start.19 = (f32[32,2048]{1,0:T(8,128)S(1)}, f32[32,2048]{1,0:T(8,128)S(1)}, u32[]{:S(2)}, u32[]{:S(2)}) collective-permute-start(f32[32,2048]{1,0:T(8,128)S(1)} %copy-done.9), channel_id=1, source_target_pairs={{0,96},{32,64},{64,32},{96,0},{128,224},{160,192},{192,160},{224,1... | collective-permute-start | bytes 786440 | tf_op jit(solution)/shard_map/ppermute | solution.py:369
  62.4 31.8 %collective-permute-start.18 = (f32[32,2048]{1,0:T(8,128)S(1)}, f32[32,2048]{1,0:T(8,128)S(1)}, u32[]{:S(2)}, u32[]{:S(2)}) collective-permute-start(f32[32,2048]{1,0:T(8,128)S(1)} %copy-done.8), channel_id=1, source_target_pairs={{0,64},{32,96},{64,0},{96,32},{128,192},{160,224},{192,128},{224,1... | collective-permute-start | bytes 786440 | tf_op jit(solution)/shard_map/ppermute | solution.py:369
  63.9 30.2 %collective-permute-start.20 = (f32[32,2048]{1,0:T(8,128)S(1)}, f32[32,2048]{1,0:T(8,128)S(1)}, u32[]{:S(2)}, u32[]{:S(2)}) collective-permute-start(f32[32,2048]{1,0:T(8,128)S(1)} %copy-done.7), channel_id=1, source_target_pairs={{0,160},{32,128},{64,224},{96,192},{128,32},{160,0},{192,96},{224,... | collective-permute-start | bytes 786440 | tf_op jit(solution)/shard_map/ppermute | solution.py:369
  66.8 27.4 %collective-permute-start.21 = (f32[32,2048]{1,0:T(8,128)S(1)}, f32[32,2048]{1,0:T(8,128)S(1)}, u32[]{:S(2)}, u32[]{:S(2)}) collective-permute-start(f32[32,2048]{1,0:T(8,128)S(1)} %copy-done.6), channel_id=1, source_target_pairs={{0,192},{32,224},{64,128},{96,160},{128,64},{160,96},{192,0},{224,... | collective-permute-start | bytes 786440 | tf_op jit(solution)/shard_map/ppermute | solution.py:369
  68.6 25.5 %collective-permute-start.22 = (f32[32,2048]{1,0:T(8,128)S(1)}, f32[32,2048]{1,0:T(8,128)S(1)}, u32[]{:S(2)}, u32[]{:S(2)}) collective-permute-start(f32[32,2048]{1,0:T(8,128)S(1)} %copy-done.5), channel_id=1, source_target_pairs={{0,224},{32,192},{64,160},{96,128},{128,96},{160,64},{192,32},{224... | collective-permute-start | bytes 786440 | tf_op jit(solution)/shard_map/ppermute | solution.py:369
  (11 other events, 254.3 us)

commit v6 on v5

--- a/solution.py
+++ b/solution.py
@@ -310,7 +310,7 @@
 
     odd, high = lane_bits(256)
     lane = lax.broadcasted_iota(jnp.int32, (256, LANES), 1)
-    groups = [pl.program_id(0) * 4 + g for g in range(4)]
+    groups = [pl.program_id(0) * 8 + g for g in range(8)]
     value = [field[:, pl.ds(pl.multiple_of(g * LANES, LANES), LANES)] for g in groups]
     centre = each(lambda x: jnp.sum(x, axis=0, keepdims=True) * (1.0 / 256.0), value)
     anomaly = each(lambda x, a: x - a, value, centre)
@@ -320,10 +320,12 @@
     base = each(
         lambda a, x, o: a + jnp.sum(x * o, axis=0, keepdims=True), centre, anomaly, offset
     )
-    spread = each(mul3, [split(root_ref[u]) for u in range(4)], each(split, anomaly))
-    layers = exchange_lanes(each(lambda b, x: b + x, base, spread), odd, high)
-    for l in range(4):
-        out_ref[:, l, :] = layers[l]
+    spread = each(mul3, [split(root_ref[u]) for u in range(8)], each(split, anomaly))
+    mixed = each(lambda b, x: b + x, base, spread)
+    for c in range(2):
+        layers = exchange_lanes(mixed[4 * c : 4 * c + 4], odd, high)
+        for l in range(4):
+            out_ref[:, l, c * LANES : (c + 1) * LANES] = layers[l]
 
 
 def find_mixing(where, nearby, damping, own, sib, far):
@@ -356,9 +358,9 @@
     return pl.pallas_call(
         apply_kernel,
         out_shape=jax.ShapeDtypeStruct((256, 4, 512), F32),
-        grid=(4,),
-        in_specs=[SMEM, pl.BlockSpec((4, 256, 256), lambda i: (i, 0, 0)), VMEM] + [ANYWHERE] * MEM,
-        out_specs=pl.BlockSpec((256, 4, LANES), lambda i: (0, 0, i)),
+        grid=(2,),
+        in_specs=[SMEM, pl.BlockSpec((8, 256, 256), lambda i: (i, 0, 0)), VMEM] + [ANYWHERE] * MEM,
+        out_specs=pl.BlockSpec((256, 4, 2 * LANES), lambda i: (0, 0, i)),
         scratch_shapes=[pltpu.VMEM((256, 2048), F32), pltpu.SemaphoreType.DMA((MEM,))],
         compiler_params=pltpu.CompilerParams(vmem_limit_bytes=30 << 20),
         name="apply",

time: 100 us -> 99.8 us (level)
  transfers between devices with their start and end apart: 23 -> 23, of which waited for: 8 -> 8; matrix products, arithmetic and copies ran while one was open for 0% -> 0% of each run, Pallas kernels for 24% -> 25%
where the time goes in v6:
time: 99.8 us; the launch traced here: 99.7 us
  starting transfers between devices  36.5 us (37%)
  Pallas kernels  36 us (36%)
  waiting for transfers between devices  25.2 us (25%)
    ppermute x21, starting transfers between devices, send(): return lax.ppermute(x, 'mem', [(i, i ^ flip) for i in range(MEM)])  30.3 us
    ppermute x21, waiting for transfers between devices, send(): return lax.ppermute(x, 'mem', [(i, i ^ flip) for i in range(MEM)])  25.2 us
    pallas_call x1, Pallas kernels, find_mixing(): pl.pallas_call(mixing_kernel, out_shape=[jax.ShapeDtypeStruct((16, 256, 2...  23.2 us
    pallas_call x1, Pallas kernels, local_obs(): pl.pallas_call(obs_kernel, out_shape=[jax.ShapeDtypeStruct((members, 2048...  6.26 us
    pallas_call x1, Pallas kernels, apply_mixing(): pl.pallas_call(apply_kernel, out_shape=jax.ShapeDtypeStruct((256, 4, 512)...  5.31 us
    ppermute x1, starting transfers between devices, local(): lax.ppermute(obs, 'tile', [(i, i + 1) for i in range(1, 31, 2)] + [(i + 1...  4.4 us
  transfers between devices with their start and end apart: 23, of which 8 were waited for; matrix products, arithmetic and copies ran while one was open for 0% of the time, Pallas kernels for 25%

profile of v6, /device:TPU:192, one launch (start us, length us, event | category | flops | bytes accessed | tf_op | source)
XLA Modules:
  0.0 99.7 jit_solution(3870348113396820330)
XLA Ops:
  0.7 6.3 %local_obs.1 = (f32[32,2048]{1,0:T(8,128)}, f32[32,2048]{1,0:T(8,128)}, f32[32,2048]{1,0:T(8,128)}, f32[32,2048]{1,0:T(8,128)}, f32[32,2048]{1,0:T(8,128)}, /*in...) custom-call(s32[2]{0:T(128)} %pad_add_fusion.where_ref.refs_0_, ...), custom_call_target="tpu_custom_call" | custom-call | tf_op jit(solution)/shard_map/local_obs/pallas_call | solution.py:113
  6.9 1.7 %collective-permute-start.4 = (f32[32,2176]{1,0:T(8,128)}, f32[32,2176]{1,0:T(8,128)S(1)}, u32[]{:S(2)}, u32[]{:S(2)}) collective-permute-start(f32[32,2176]{1,0:T(8,128)} %get-tuple-element.34.refs_0_), channel_id=1, source_target_pairs={{0,128},{32,160},{64,192},{96,224},{128,0},{160,32},{192,64},{224,... | collective-permute-start | bytes 835592 | tf_op jit(solution)/shard_map/ppermute | solution.py:371
  8.6 4.4 %collective-permute-start = (f32[32,2176]{1,0:T(8,128)}, f32[32,2176]{1,0:T(8,128)S(1)}, u32[]{:S(2)}, u32[]{:S(2)}) collective-permute-start(f32[32,2176]{1,0:T(8,128)} %get-tuple-element.34.refs_0_), channel_id=1, source_target_pairs={{1,2},{3,4},{5,6},{7,8},{9,10},{11,12},{13,14},{15,16},{17,18},{19... | collective-permute-start | bytes 835592 | tf_op jit(solution)/shard_map/ppermute | solution.py:387
  13.0 2.8 %collective-permute-start.8 = (f32[32,2176]{1,0:T(8,128)}, f32[32,2176]{1,0:T(8,128)S(1)}, u32[]{:S(2)}, u32[]{:S(2)}) collective-permute-start(f32[32,2176]{1,0:T(8,128)} %get-tuple-element.34.refs_0_), channel_id=1, source_target_pairs={{0,96},{32,64},{64,32},{96,0},{128,224},{160,192},{192,160},{224,1... | collective-permute-start | bytes 835592 | tf_op jit(solution)/shard_map/ppermute | solution.py:371
  15.9 3.6 %collective-permute-done.4.refs_1_ = f32[32,2176]{1,0:T(8,128)S(1)} collective-permute-done((f32[32,2176]{1,0:T(8,128)}, f32[32,2176]{1,0:T(8,128)S(1)}, u32[]{:S(2)}, u32[]{:S(2)}) %collective-permute-start.4) | collective-permute-done | bytes 278560 | tf_op jit(solution)/shard_map/ppermute | solution.py:371
  19.5 1.5 %collective-permute-start.9 = (f32[32,2176]{1,0:T(8,128)S(1)}, f32[32,2176]{1,0:T(8,128)S(1)}, u32[]{:S(2)}, u32[]{:S(2)}) collective-permute-start(f32[32,2176]{1,0:T(8,128)S(1)} %collective-permute-done.4.refs_1_), channel_id=1, source_target_pairs={{0,32},{32,0},{64,96},{96,64},{128,160},{160,128},{192,224},{224,1... | collective-permute-start | bytes 835592 | tf_op jit(solution)/shard_map/ppermute | solution.py:371
  21.0 1.3 %collective-permute-start.3 = (f32[32,2176]{1,0:T(8,128)S(1)}, f32[32,2176]{1,0:T(8,128)S(1)}, u32[]{:S(2)}, u32[]{:S(2)}) collective-permute-start(f32[32,2176]{1,0:T(8,128)S(1)} %collective-permute-done.refs_5_), channel_id=1, source_target_pairs={{0,128},{32,160},{64,192},{96,224},{128,0},{160,32},{192,64},{224,... | collective-permute-start | bytes 835592 | tf_op jit(solution)/shard_map/ppermute | solution.py:371
  22.3 2.1 %collective-permute-start.2 = (f32[32,2176]{1,0:T(8,128)S(1)}, f32[32,2176]{1,0:T(8,128)S(1)}, u32[]{:S(2)}, u32[]{:S(2)}) collective-permute-start(f32[32,2176]{1,0:T(8,128)S(1)} %collective-permute-done.refs_5_), channel_id=1, source_target_pairs={{0,96},{32,64},{64,32},{96,0},{128,224},{160,192},{192,160},{224,1... | collective-permute-start | bytes 835592 | tf_op jit(solution)/shard_map/ppermute | solution.py:371
  24.9 1.4 %collective-permute-start.7 = (f32[32,2176]{1,0:T(8,128)}, f32[32,2176]{1,0:T(8,128)S(1)}, u32[]{:S(2)}, u32[]{:S(2)}) collective-permute-start(f32[32,2176]{1,0:T(8,128)} %get-tuple-element.34.refs_0_), channel_id=1, source_target_pairs={{0,32},{32,0},{64,96},{96,64},{128,160},{160,128},{192,224},{224,1... | collective-permute-start | bytes 835592 | tf_op jit(solution)/shard_map/ppermute | solution.py:371
  26.4 2.4 %collective-permute-start.10 = (f32[32,2176]{1,0:T(8,128)S(1)}, f32[32,2176]{1,0:T(8,128)S(1)}, u32[]{:S(2)}, u32[]{:S(2)}) collective-permute-start(f32[32,2176]{1,0:T(8,128)S(1)} %collective-permute-done.4.refs_1_), channel_id=1, source_target_pairs={{0,96},{32,64},{64,32},{96,0},{128,224},{160,192},{192,160},{224,1... | collective-permute-start | bytes 835592 | tf_op jit(solution)/shard_map/ppermute | solution.py:371
  29.0 2.6 %collective-permute-done.2.refs_8_ = f32[32,2176]{1,0:T(8,128)S(1)} collective-permute-done((f32[32,2176]{1,0:T(8,128)S(1)}, f32[32,2176]{1,0:T(8,128)S(1)}, u32[]{:S(2)}, u32[]{:S(2)}) %collective-permute-start.2) | collective-permute-done | bytes 278560 | tf_op jit(solution)/shard_map/ppermute | solution.py:371
  32.9 2.0 %collective-permute-start.6 = (f32[32,2176]{1,0:T(8,128)S(1)}, f32[32,2176]{1,0:T(8,128)S(1)}, u32[]{:S(2)}, u32[]{:S(2)}) collective-permute-start(f32[32,2176]{1,0:T(8,128)S(1)} %collective-permute-done.3.refs_6_), channel_id=1, source_target_pairs={{0,96},{32,64},{64,32},{96,0},{128,224},{160,192},{192,160},{224,1... | collective-permute-start | bytes 835592 | tf_op jit(solution)/shard_map/ppermute | solution.py:371
  34.9 3.0 %collective-permute-done.7.refs_2_ = f32[32,2176]{1,0:T(8,128)S(1)} collective-permute-done((f32[32,2176]{1,0:T(8,128)}, f32[32,2176]{1,0:T(8,128)S(1)}, u32[]{:S(2)}, u32[]{:S(2)}) %collective-permute-start.7) | collective-permute-done | bytes 278560 | tf_op jit(solution)/shard_map/ppermute | solution.py:371
  38.8 5.0 %collective-permute-done.11.refs_6_ = f32[32,2176]{1,0:T(8,128)S(1)} collective-permute-done((f32[32,2176]{1,0:T(8,128)S(1)}, f32[32,2176]{1,0:T(8,128)S(1)}, u32[]{:S(2)}, u32[]{:S(2)}) %collective-permute-start.11) | collective-permute-done | bytes 278560 | tf_op jit(solution)/shard_map/ppermute | solution.py:371
  44.9 1.3 %own_table.1.refs_3_ = f32[16,264,128]{2,1,0:T(8,128)S(1)} custom-call(s32[2]{0:T(128)S(1)} %copy-done.2, f32[32,2176]{1,0:T(8,128)S(1)} %copy-done, f32[32,2176]{1,0:T(8,128)S(1)} %collective-permute-done.4.refs_1_, f32[32,2176]{1,0:T(8,128)S(1)} %collective-permute-done.7.refs_2_, f32[32,2176]{1,0:T(8,128)S(1)} %collective-permute-done.8.refs_3_, ...), custom_call_target="tpu_custom_call" | custom-call | flops 2097152 | bytes 6291456 | tf_op jit(solution)/shard_map/own_table/pallas_call | solution.py:182
  46.2 3.4 %collective-permute-done.6.refs_10_ = f32[32,2176]{1,0:T(8,128)S(1)} collective-permute-done((f32[32,2176]{1,0:T(8,128)S(1)}, f32[32,2176]{1,0:T(8,128)S(1)}, u32[]{:S(2)}, u32[]{:S(2)}) %collective-permute-start.6) | collective-permute-done | bytes 278560 | tf_op jit(solution)/shard_map/ppermute | solution.py:371
  49.8 1.8 %collective-permute-start.14 = (f32[16,264,128]{2,1,0:T(8,128)S(1)}, f32[16,264,128]{2,1,0:T(8,128)S(1)}, u32[]{:S(2)}, u32[]{:S(2)}) collective-permute-start(f32[16,264,128]{2,1,0:T(8,128)S(1)} %own_table.1.refs_3_), channel_id=1, source_target_pairs={{0,1},{1,0},{2,3},{3,2},{4,5},{5,4},{6,7},{7,6},{8,9},{9,8},{10,11... | collective-permute-start | bytes 6488072 | tf_op jit(solution)/shard_map/ppermute | solution.py:375
  55.2 5.9 %collective-permute-done.13.refs_11_ = f32[32,2176]{1,0:T(8,128)S(1)} collective-permute-done((f32[32,2176]{1,0:T(8,128)S(1)}, f32[32,2176]{1,0:T(8,128)S(1)}, u32[]{:S(2)}, u32[]{:S(2)}) %collective-permute-start.13) | collective-permute-done | bytes 278560 | tf_op jit(solution)/shard_map/ppermute | solution.py:371
  62.4 1.5 %collective-permute-start.18 = (f32[32,2048]{1,0:T(8,128)S(1)}, f32[32,2048]{1,0:T(8,128)S(1)}, u32[]{:S(2)}, u32[]{:S(2)}) collective-permute-start(f32[32,2048]{1,0:T(8,128)S(1)} %copy-done.8), channel_id=1, source_target_pairs={{0,64},{32,96},{64,0},{96,32},{128,192},{160,224},{192,128},{224,1... | collective-permute-start | bytes 786440 | tf_op jit(solution)/shard_map/ppermute | solution.py:371
  63.9 1.6 %collective-permute-start.20 = (f32[32,2048]{1,0:T(8,128)S(1)}, f32[32,2048]{1,0:T(8,128)S(1)}, u32[]{:S(2)}, u32[]{:S(2)}) collective-permute-start(f32[32,2048]{1,0:T(8,128)S(1)} %copy-done.7), channel_id=1, source_target_pairs={{0,160},{32,128},{64,224},{96,192},{128,32},{160,0},{192,96},{224,... | collective-permute-start | bytes 786440 | tf_op jit(solution)/shard_map/ppermute | solution.py:371
  66.8 1.9 %collective-permute-start.21 = (f32[32,2048]{1,0:T(8,128)S(1)}, f32[32,2048]{1,0:T(8,128)S(1)}, u32[]{:S(2)}, u32[]{:S(2)}) collective-permute-start(f32[32,2048]{1,0:T(8,128)S(1)} %copy-done.6), channel_id=1, source_target_pairs={{0,192},{32,224},{64,128},{96,160},{128,64},{160,96},{192,0},{224,... | collective-permute-start | bytes 786440 | tf_op jit(solution)/shard_map/ppermute | solution.py:371
  68.6 2.3 %collective-permute-start.22 = (f32[32,2048]{1,0:T(8,128)S(1)}, f32[32,2048]{1,0:T(8,128)S(1)}, u32[]{:S(2)}, u32[]{:S(2)}) collective-permute-start(f32[32,2048]{1,0:T(8,128)S(1)} %copy-done.5), channel_id=1, source_target_pairs={{0,224},{32,192},{64,160},{96,128},{128,96},{160,64},{192,32},{224... | collective-permute-start | bytes 786440 | tf_op jit(solution)/shard_map/ppermute | solution.py:371
  70.9 23.2 %mixing.1 = (f32[16,256,256]{2,1,0:T(8,128)S(1)}, f32[256,128]{1,0:T(8,128)S(1)}) custom-call(s32[2]{0:T(128)S(1)} %copy-done.2, s32[8,16]{1,0:T(8,128)S(1)} %bitcast.5, s32[8,16]{1,0:T(8,128)S(1)} %bitcast.6, f32[16,264,128]{2,1,0:T(8,128)S(1)} %own_table.1.refs_3_, f32[16,264,128]{2,1,0:T(8,128)S(1)} %collective-permute-done.14.refs_4_, ...), custom_call_target="tpu_custom_call" | custom-call | flops 16106127360 | bytes 12582912 | tf_op jit(solution)/shard_map/mixing/pallas_call | solution.py:332
  94.2 5.3 %apply.1 = f32[256,4,512]{2,1,0:T(4,128)} custom-call(s32[2]{0:T(128)S(1)} %copy-done.2, f32[16,256,256]{2,1,0:T(8,128)S(1)} %get-tuple-element.53.root_ref, f32[256,128]{1,0:T(8,128)S(1)} %get-tuple-element.54.offset_ref, f32[32,2048]{1,0:T(8,128)S(1)} %copy-done.1, f32[32,2048]{1,0:T(8,128)S(1)} %collective-permute-done.17.refs_1_, ...), custom_call_target="tpu_custom_call" | custom-call | tf_op jit(solution)/shard_map/apply/pallas_call | solution.py:358
  (51 shorter events, 10.9 us)
Async XLA Ops:
  0.7 70.3 %copy-start.4 = (s32[16,8]{0,1:T(8,128)S(1)}, s32[16,8]{0,1:T(8,128)}, u32[]{:S(2)}) copy-start(s32[16,8]{0,1:T(8,128)} %param.11) | copy-start | bytes 1540
  6.9 12.5 %collective-permute-start.4 = (f32[32,2176]{1,0:T(8,128)}, f32[32,2176]{1,0:T(8,128)S(1)}, u32[]{:S(2)}, u32[]{:S(2)}) collective-permute-start(f32[32,2176]{1,0:T(8,128)} %get-tuple-element.34.refs_0_), channel_id=1, source_target_pairs={{0,128},{32,160},{64,192},{96,224},{128,0},{160,32},{192,64},{224,... | collective-permute-start | bytes 835592 | tf_op jit(solution)/shard_map/ppermute | solution.py:371
  8.6 12.4 %collective-permute-start = (f32[32,2176]{1,0:T(8,128)}, f32[32,2176]{1,0:T(8,128)S(1)}, u32[]{:S(2)}, u32[]{:S(2)}) collective-permute-start(f32[32,2176]{1,0:T(8,128)} %get-tuple-element.34.refs_0_), channel_id=1, source_target_pairs={{1,2},{3,4},{5,6},{7,8},{9,10},{11,12},{13,14},{15,16},{17,18},{19... | collective-permute-start | bytes 835592 | tf_op jit(solution)/shard_map/ppermute | solution.py:387
  13.0 11.9 %collective-permute-start.8 = (f32[32,2176]{1,0:T(8,128)}, f32[32,2176]{1,0:T(8,128)S(1)}, u32[]{:S(2)}, u32[]{:S(2)}) collective-permute-start(f32[32,2176]{1,0:T(8,128)} %get-tuple-element.34.refs_0_), channel_id=1, source_target_pairs={{0,96},{32,64},{64,32},{96,0},{128,224},{160,192},{192,160},{224,1... | collective-permute-start | bytes 835592 | tf_op jit(solution)/shard_map/ppermute | solution.py:371
  19.5 6.9 %collective-permute-start.9 = (f32[32,2176]{1,0:T(8,128)S(1)}, f32[32,2176]{1,0:T(8,128)S(1)}, u32[]{:S(2)}, u32[]{:S(2)}) collective-permute-start(f32[32,2176]{1,0:T(8,128)S(1)} %collective-permute-done.4.refs_1_), channel_id=1, source_target_pairs={{0,32},{32,0},{64,96},{96,64},{128,160},{160,128},{192,224},{224,1... | collective-permute-start | bytes 835592 | tf_op jit(solution)/shard_map/ppermute | solution.py:371
  21.0 7.8 %collective-permute-start.3 = (f32[32,2176]{1,0:T(8,128)S(1)}, f32[32,2176]{1,0:T(8,128)S(1)}, u32[]{:S(2)}, u32[]{:S(2)}) collective-permute-start(f32[32,2176]{1,0:T(8,128)S(1)} %collective-permute-done.refs_5_), channel_id=1, source_target_pairs={{0,128},{32,160},{64,192},{96,224},{128,0},{160,32},{192,64},{224,... | collective-permute-start | bytes 835592 | tf_op jit(solution)/shard_map/ppermute | solution.py:371
  22.3 9.4 %collective-permute-start.2 = (f32[32,2176]{1,0:T(8,128)S(1)}, f32[32,2176]{1,0:T(8,128)S(1)}, u32[]{:S(2)}, u32[]{:S(2)}) collective-permute-start(f32[32,2176]{1,0:T(8,128)S(1)} %collective-permute-done.refs_5_), channel_id=1, source_target_pairs={{0,96},{32,64},{64,32},{96,0},{128,224},{160,192},{192,160},{224,1... | collective-permute-start | bytes 835592 | tf_op jit(solution)/shard_map/ppermute | solution.py:371
  24.3 8.5 %collective-permute-start.1 = (f32[32,2176]{1,0:T(8,128)S(1)}, f32[32,2176]{1,0:T(8,128)S(1)}, u32[]{:S(2)}, u32[]{:S(2)}) collective-permute-start(f32[32,2176]{1,0:T(8,128)S(1)} %collective-permute-done.refs_5_), channel_id=1, source_target_pairs={{0,32},{32,0},{64,96},{96,64},{128,160},{160,128},{192,224},{224,1... | collective-permute-start | bytes 835592 | tf_op jit(solution)/shard_map/ppermute | solution.py:371
  24.9 13.0 %collective-permute-start.7 = (f32[32,2176]{1,0:T(8,128)}, f32[32,2176]{1,0:T(8,128)S(1)}, u32[]{:S(2)}, u32[]{:S(2)}) collective-permute-start(f32[32,2176]{1,0:T(8,128)} %get-tuple-element.34.refs_0_), channel_id=1, source_target_pairs={{0,32},{32,0},{64,96},{96,64},{128,160},{160,128},{192,224},{224,1... | collective-permute-start | bytes 835592 | tf_op jit(solution)/shard_map/ppermute | solution.py:371
  26.4 17.5 %collective-permute-start.10 = (f32[32,2176]{1,0:T(8,128)S(1)}, f32[32,2176]{1,0:T(8,128)S(1)}, u32[]{:S(2)}, u32[]{:S(2)}) collective-permute-start(f32[32,2176]{1,0:T(8,128)S(1)} %collective-permute-done.4.refs_1_), channel_id=1, source_target_pairs={{0,96},{32,64},{64,32},{96,0},{128,224},{160,192},{192,160},{224,1... | collective-permute-start | bytes 835592 | tf_op jit(solution)/shard_map/ppermute | solution.py:371
  28.8 15.1 %collective-permute-start.11 = (f32[32,2176]{1,0:T(8,128)S(1)}, f32[32,2176]{1,0:T(8,128)S(1)}, u32[]{:S(2)}, u32[]{:S(2)}) collective-permute-start(f32[32,2176]{1,0:T(8,128)S(1)} %collective-permute-done.8.refs_3_), channel_id=1, source_target_pairs={{0,32},{32,0},{64,96},{96,64},{128,160},{160,128},{192,224},{224,1... | collective-permute-start | bytes 835592 | tf_op jit(solution)/shard_map/ppermute | solution.py:371
  31.7 12.2 %collective-permute-start.12 = (f32[32,2176]{1,0:T(8,128)S(1)}, f32[32,2176]{1,0:T(8,128)S(1)}, u32[]{:S(2)}, u32[]{:S(2)}) collective-permute-start(f32[32,2176]{1,0:T(8,128)S(1)} %collective-permute-done.9.refs_4_), channel_id=1, source_target_pairs={{0,96},{32,64},{64,32},{96,0},{128,224},{160,192},{192,160},{224,1... | collective-permute-start | bytes 835592 | tf_op jit(solution)/shard_map/ppermute | solution.py:371
  32.9 16.7 %collective-permute-start.6 = (f32[32,2176]{1,0:T(8,128)S(1)}, f32[32,2176]{1,0:T(8,128)S(1)}, u32[]{:S(2)}, u32[]{:S(2)}) collective-permute-start(f32[32,2176]{1,0:T(8,128)S(1)} %collective-permute-done.3.refs_6_), channel_id=1, source_target_pairs={{0,96},{32,64},{64,32},{96,0},{128,224},{160,192},{192,160},{224,1... | collective-permute-start | bytes 835592 | tf_op jit(solution)/shard_map/ppermute | solution.py:371
  37.9 11.9 %collective-permute-start.5 = (f32[32,2176]{1,0:T(8,128)S(1)}, f32[32,2176]{1,0:T(8,128)S(1)}, u32[]{:S(2)}, u32[]{:S(2)}) collective-permute-start(f32[32,2176]{1,0:T(8,128)S(1)} %collective-permute-done.3.refs_6_), channel_id=1, source_target_pairs={{0,32},{32,0},{64,96},{96,64},{128,160},{160,128},{192,224},{224,1... | collective-permute-start | bytes 835592 | tf_op jit(solution)/shard_map/ppermute | solution.py:371
  49.8 12.5 %collective-permute-start.14 = (f32[16,264,128]{2,1,0:T(8,128)S(1)}, f32[16,264,128]{2,1,0:T(8,128)S(1)}, u32[]{:S(2)}, u32[]{:S(2)}) collective-permute-start(f32[16,264,128]{2,1,0:T(8,128)S(1)} %own_table.1.refs_3_), channel_id=1, source_target_pairs={{0,1},{1,0},{2,3},{3,2},{4,5},{5,4},{6,7},{7,6},{8,9},{9,8},{10,11... | collective-permute-start | bytes 6488072 | tf_op jit(solution)/shard_map/ppermute | solution.py:375
  51.6 9.5 %collective-permute-start.13 = (f32[32,2176]{1,0:T(8,128)S(1)}, f32[32,2176]{1,0:T(8,128)S(1)}, u32[]{:S(2)}, u32[]{:S(2)}) collective-permute-start(f32[32,2176]{1,0:T(8,128)S(1)} %collective-permute-done.2.refs_8_), channel_id=1, source_target_pairs={{0,32},{32,0},{64,96},{96,64},{128,160},{160,128},{192,224},{224,1... | collective-permute-start | bytes 835592 | tf_op jit(solution)/shard_map/ppermute | solution.py:371
  52.2 16.4 %collective-permute-start.16 = (f32[32,2176]{1,0:T(8,128)S(1)}, f32[32,2176]{1,0:T(8,128)S(1)}, u32[]{:S(2)}, u32[]{:S(2)}) collective-permute-start(f32[32,2176]{1,0:T(8,128)S(1)} %collective-permute-done.5.refs_9_), channel_id=1, source_target_pairs={{0,96},{32,64},{64,32},{96,0},{128,224},{160,192},{192,160},{224,1... | collective-permute-start | bytes 835592 | tf_op jit(solution)/shard_map/ppermute | solution.py:371
  53.3 9.0 %collective-permute-start.15 = (f32[32,2048]{1,0:T(8,128)S(1)}, f32[32,2048]{1,0:T(8,128)S(1)}, u32[]{:S(2)}, u32[]{:S(2)}) collective-permute-start(f32[32,2048]{1,0:T(8,128)S(1)} %copy-done.11), channel_id=1, source_target_pairs={{0,128},{32,160},{64,192},{96,224},{128,0},{160,32},{192,64},{224,... | collective-permute-start | bytes 786440 | tf_op jit(solution)/shard_map/ppermute | solution.py:371
  54.6 12.2 %collective-permute-start.17 = (f32[32,2048]{1,0:T(8,128)S(1)}, f32[32,2048]{1,0:T(8,128)S(1)}, u32[]{:S(2)}, u32[]{:S(2)}) collective-permute-start(f32[32,2048]{1,0:T(8,128)S(1)} %copy-done.10), channel_id=1, source_target_pairs={{0,32},{32,0},{64,96},{96,64},{128,160},{160,128},{192,224},{224,1... | collective-permute-start | bytes 786440 | tf_op jit(solution)/shard_map/ppermute | solution.py:371
  61.1 33.0 %collective-permute-start.19 = (f32[32,2048]{1,0:T(8,128)S(1)}, f32[32,2048]{1,0:T(8,128)S(1)}, u32[]{:S(2)}, u32[]{:S(2)}) collective-permute-start(f32[32,2048]{1,0:T(8,128)S(1)} %copy-done.9), channel_id=1, source_target_pairs={{0,96},{32,64},{64,32},{96,0},{128,224},{160,192},{192,160},{224,1... | collective-permute-start | bytes 786440 | tf_op jit(solution)/shard_map/ppermute | solution.py:371
  62.4 31.8 %collective-permute-start.18 = (f32[32,2048]{1,0:T(8,128)S(1)}, f32[32,2048]{1,0:T(8,128)S(1)}, u32[]{:S(2)}, u32[]{:S(2)}) collective-permute-start(f32[32,2048]{1,0:T(8,128)S(1)} %copy-done.8), channel_id=1, source_target_pairs={{0,64},{32,96},{64,0},{96,32},{128,192},{160,224},{192,128},{224,1... | collective-permute-start | bytes 786440 | tf_op jit(solution)/shard_map/ppermute | solution.py:371
  63.9 30.3 %collective-permute-start.20 = (f32[32,2048]{1,0:T(8,128)S(1)}, f32[32,2048]{1,0:T(8,128)S(1)}, u32[]{:S(2)}, u32[]{:S(2)}) collective-permute-start(f32[32,2048]{1,0:T(8,128)S(1)} %copy-done.7), channel_id=1, source_target_pairs={{0,160},{32,128},{64,224},{96,192},{128,32},{160,0},{192,96},{224,... | collective-permute-start | bytes 786440 | tf_op jit(solution)/shard_map/ppermute | solution.py:371
  66.8 27.4 %collective-permute-start.21 = (f32[32,2048]{1,0:T(8,128)S(1)}, f32[32,2048]{1,0:T(8,128)S(1)}, u32[]{:S(2)}, u32[]{:S(2)}) collective-permute-start(f32[32,2048]{1,0:T(8,128)S(1)} %copy-done.6), channel_id=1, source_target_pairs={{0,192},{32,224},{64,128},{96,160},{128,64},{160,96},{192,0},{224,... | collective-permute-start | bytes 786440 | tf_op jit(solution)/shard_map/ppermute | solution.py:371
  68.6 25.6 %collective-permute-start.22 = (f32[32,2048]{1,0:T(8,128)S(1)}, f32[32,2048]{1,0:T(8,128)S(1)}, u32[]{:S(2)}, u32[]{:S(2)}) collective-permute-start(f32[32,2048]{1,0:T(8,128)S(1)} %copy-done.5), channel_id=1, source_target_pairs={{0,224},{32,192},{64,160},{96,128},{128,96},{160,64},{192,32},{224... | collective-permute-start | bytes 786440 | tf_op jit(solution)/shard_map/ppermute | solution.py:371
  (11 other events, 254.4 us)
